TPU v7x, 32 devices: a whole 2x2x4 slice. The times are simulated.
32 devices in a mesh: blk: 4 (over y, core), dom: 8 (over z, x).
Axes of the slice: x: 2, y: 2, z: 4, core: 2. Of those that a mesh axis runs over, the one named last changes fastest.
Arguments:
- features: bfloat16 [8, 2048, 256], P('dom', 'blk'), may hold values from -6 to 6
- weight: bfloat16 [256, 256], replicated, may hold values from -0.375 to 0.375
- tiles: bfloat16 [8, 4, 4, 6, 128, 128], P('dom', 'blk'), may hold values from -0.3046875 to 0.3046875
- tile_pos: int32 [8, 4, 4, 6], P('dom', 'blk'), may hold values from 0 to 15, as said below
- tile_count: int32 [8, 4, 4], P('dom', 'blk'), may hold values from 1 to 6
- send_list: int32 [8, 4, 8, 32], P('dom', 'blk'), may hold values from 0 to 511
- send_count: int32 [8, 4, 8], P('dom', 'blk'), may hold values from 0 to 32, as said below
- owner_map: int32 [8, 4, 8, 32], P('dom', 'blk'), may hold values from 0 to 511
- halo_weight: float32 [8, 4, 8, 32], P('dom', 'blk'), may hold values from 0.25 to 1
- cotangent: bfloat16 [8, 2048, 256], P('dom', 'blk'), may hold values from -6 to 6
Outputs:
- layer_out: bfloat16 [8, 2048, 256], P('dom', 'blk')
- feature_grad: bfloat16 [8, 2048, 256], P('dom', 'blk')
- weight_grad: float32 [256, 256], replicated
Inputs may be any that keep to these rules, and one draw needn't show every extreme that they name: `tile_pos`: the 6 positions of one row group in one column group are distinct. `send_count`: zero where the peer is the sender's own partition.
All inputs are finite; a program needn't handle non-finite values.
Results may differ from a plain program's by a relative error of at most 0.019.
Values may be sent and summed in bfloat16 or wider, within the bound.
No kernel may reach another device: no remote copies, remote signals or barrier semaphores. Data moves between devices by JAX's collectives and lax.ppermute only.
A program may use at most 128 MiB of HBM per device.

v0:
```python
import jax
import jax.numpy as jnp
from jax import lax
from jax.sharding import PartitionSpec as P


def spread_rows(tile_set, positions, counts, panel, per):
    groups, slots = positions.shape
    tile = tile_set.shape[-1]
    width = panel.shape[-1]
    grid = panel.reshape(groups, per, tile, width)
    column = positions % per
    row_tile = positions // per
    picked = grid[jnp.arange(groups)[:, None], column]
    product = jnp.einsum("gtij,gtjf->gtif", tile_set, picked, preferred_element_type=jnp.float32)
    live = jnp.arange(slots)[None, :] < counts[:, None]
    select = ((row_tile[..., None] == jnp.arange(per)[None, None, :]) & live[..., None]).astype(
        jnp.float32
    )
    return jnp.einsum("gtif,gtr->rif", product, select).reshape(per * tile, width)


def spread_cols(tile_set, positions, counts, grad_rows, per):
    groups, slots = positions.shape
    tile = tile_set.shape[-1]
    width = grad_rows.shape[-1]
    grid = grad_rows.reshape(per, tile, width)
    column = positions % per
    row_tile = positions // per
    picked = grid[row_tile]
    product = jnp.einsum("gtij,gtif->gtjf", tile_set, picked, preferred_element_type=jnp.float32)
    live = jnp.arange(slots)[None, :] < counts[:, None]
    select = ((column[..., None] == jnp.arange(per)[None, None, :]) & live[..., None]).astype(
        jnp.float32
    )
    return jnp.einsum("gtjf,gtc->gcjf", product, select).reshape(groups * per * tile, width)


def on_device(
    features,
    weight,
    tiles,
    tile_pos,
    tile_count,
    send_list,
    send_count,
    owner_map,
    halo_weight,
    cotangent,
):
    feats = features[0]
    rows, width = feats.shape
    tile_set = tiles[0, 0]
    positions = tile_pos[0, 0]
    counts = tile_count[0, 0]
    tile = tile_set.shape[-1]
    per = rows // tile
    send_rows = send_list[0, 0]
    send_live = send_count[0, 0]
    owners = owner_map[0, 0]
    edge_weight = halo_weight[0, 0]
    grad_in = cotangent[0]
    slots = send_rows.shape[1]
    live = (jnp.arange(slots)[None, :] < send_live[:, None])[..., None]
    empty = jnp.zeros((rows, width), jnp.float32)
    projected = jnp.dot(feats, weight, preferred_element_type=jnp.float32).astype(jnp.bfloat16)
    part_tiles = tile_set
    part_pos = positions
    part_count = counts
    local = spread_rows(
        part_tiles, part_pos, part_count, lax.all_gather(projected, "blk", axis=0, tiled=True), per
    )
    outgoing = jnp.where(live, projected[send_rows], jnp.zeros((), jnp.bfloat16))
    incoming = lax.all_to_all(outgoing, "dom", split_axis=0, concat_axis=0, tiled=True)
    weighted = edge_weight.reshape(-1, 1) * incoming.reshape(-1, width).astype(jnp.float32)
    halo_sum = empty.at[owners.reshape(-1)].add(weighted)
    layer_out = (local + halo_sum).astype(jnp.bfloat16)
    back = (edge_weight[..., None] * grad_in[owners].astype(jnp.float32)).astype(jnp.bfloat16)
    returned = lax.all_to_all(back, "dom", split_axis=0, concat_axis=0, tiled=True)
    returned = jnp.where(live, returned, jnp.zeros((), jnp.bfloat16))
    halo_back = empty.at[send_rows.reshape(-1)].add(returned.reshape(-1, width).astype(jnp.float32))
    part_tiles = tile_set
    part_pos = positions
    part_count = counts
    local_grad = lax.psum_scatter(
        spread_cols(part_tiles, part_pos, part_count, grad_in, per).astype(jnp.bfloat16),
        "blk",
        scatter_dimension=0,
        tiled=True,
    ).astype(jnp.float32)
    proj_grad = (local_grad + halo_back).astype(jnp.bfloat16)
    feature_grad = lax.dot_general(
        proj_grad, weight, (((1,), (1,)), ((), ())), preferred_element_type=jnp.float32
    )
    feature_grad = feature_grad.astype(jnp.bfloat16)
    weight_term = lax.dot_general(
        feats, proj_grad, (((0,), (0,)), ((), ())), preferred_element_type=jnp.float32
    )
    total = lax.psum(weight_term, ("blk", "dom"))
    scale = float(lax.axis_size("blk") * lax.axis_size("dom") * rows) ** (-0.5)
    return (layer_out[None], feature_grad[None], total * scale)


def solution(mesh):
    return jax.shard_map(
        on_device,
        mesh=mesh,
        in_specs=(
            P("dom", "blk", None),
            P(),
            P("dom", "blk", None, None, None, None),
            P("dom", "blk", None, None),
            P("dom", "blk", None),
            P("dom", "blk", None, None),
            P("dom", "blk", None),
            P("dom", "blk", None, None),
            P("dom", "blk", None, None),
            P("dom", "blk", None),
        ),
        out_specs=(P("dom", "blk", None), P("dom", "blk", None), P()),
        check_vma=False,
    )
```

profile of v0, /device:TPU:0, one launch (start us, length us, event | category | flops | bytes accessed | tf_op | source)
XLA Modules:
  0.0 197.4 jit_solution(8924370056776361853)
XLA Ops:
  7.2 0.0 copy-start
  7.2 0.0 copy-start.1
  7.2 0.0 all-gather.2.cloned.1.call-start
  7.2 2.0 %convolution_convert_fusion.1 = bf16[512,256]{1,0:T(8,128)(2,1)} fusion(bf16[256,256]{1,0:T(8,128)(2,1)} %param.11, bf16[1,512,256]{2,1,0:T(8,128)(2,1)} %param.10), kind=kOutput, calls=%fused_computation.13 | convolution fusion | flops 67239936 | bytes 655360 | tf_op jit(solution)/shard_map/dot_general | solution.py:66
  9.2 0.0 all-gather.2.cloned.1.call-update
  9.3 0.0 reduce-scatter.2.cloned.1.call-start
  9.3 0.7 compare_select_fusion.4
  10.0 0.1 reshape.340
  10.1 0.0 copy-done.1
  10.1 0.6 gather_fusion.2
  10.8 0.0 copy-done
  10.8 1.8 fusion.11
  12.6 0.0 copy-start.9
  12.6 0.0 copy-start.8
  12.6 3.3 %copy.19 = bf16[4,6,256,128]{2,1,3,0:T(8,128)(2,1)S(1)} copy(bf16[4,6,256,128]{3,2,1,0:T(8,128)(2,1)} %fusion.11) | data formatting | bytes 3145728 | tf_op jit(solution)/shard_map/gtij,gtif->gtjf/dot_general | solution.py:31
  15.8 0.0 copy-done.9
  15.8 0.1 iota_compare_fusion.3
  15.9 0.0 copy-done.8
  15.9 0.7 fusion.4
  16.6 0.0 copy-start.6
  16.6 1.1 copy.15
  17.8 0.0 copy-start.5
  17.8 0.0 reduce-scatter.2.cloned.1.call-update
  17.8 0.0 copy-done.6
  17.8 0.1 reshape.348
  17.9 1.2 gather_fusion.3
  19.1 0.0 copy-done.5
  19.1 0.8 fusion.17
  19.8 7.2 %all-to-all-start.1 = ((bf16[8,32,256]{2,1,0:T(8,128)(2,1)}), bf16[8,32,256]{2,1,0:T(8,128)(2,1)S(1)}, u32[]{:S(2)}, u32[]{:S(2)}) async-start(bf16[8,32,256]{2,1,0:T(8,128)(2,1)} %fusion.17), calls=%async_computation.2 | async-start | bytes 262144 | tf_op jit(solution)/shard_map/all_to_all | solution.py:79
  27.1 0.1 reshape_squeeze.10
  27.2 0.0 copy-done.7
  27.2 0.1 reshape.332
  27.3 0.0 copy-done.10
  27.3 0.1 iota_compare_fusion.2
  27.3 0.1 mul.26
  27.4 0.1 reshape_squeeze.12
  27.5 0.1 reshape.324
  27.6 0.0 copy-done.2
  27.6 1.2 gather_fusion.1
  28.8 5.7 %all-to-all-done.1 = bf16[8,32,256]{2,1,0:T(8,128)(2,1)S(1)} async-done(((bf16[8,32,256]{2,1,0:T(8,128)(2,1)}), bf16[8,32,256]{2,1,0:T(8,128)(2,1)S(1)}, u32[]{:S(2)}, u32[]{:S(2)}) %all-to-all-start.1) | async-done | bytes 131104 | tf_op jit(solution)/shard_map/all_to_all | solution.py:79
  34.4 0.8 broadcast_select_fusion
  35.2 3.4 %all-to-all-start = ((bf16[8,32,256]{2,1,0:T(8,128)(2,1)}), bf16[8,32,256]{2,1,0:T(8,128)(2,1)S(1)}, u32[]{:S(2)}, u32[]{:S(2)}) async-start(bf16[8,32,256]{2,1,0:T(8,128)(2,1)} %get-tuple-element.14), calls=%async_computation | async-start | bytes 262144 | tf_op jit(solution)/shard_map/all_to_all | solution.py:74
  38.6 0.0 all-reduce.2.cloned.1.call-start
  38.6 0.0 all-gather.2.cloned.1.call-done
  38.7 2.0 %gather_fusion = bf16[24,128,256]{2,1,0:T(8,128)(2,1)S(1)} fusion(bf16[4,4,128,256]{3,2,1,0:T(8,128)(2,1)} %bitcast.127, s32[24]{0:T(128)S(1)} %reshape.324), kind=kCustom, calls=%fused_computation | custom fusion | bytes 3145920 | tf_op jit(solution)/shard_map/gather | solution.py:14
  40.6 1.8 fusion.13
  42.4 3.3 %copy.17 = bf16[4,6,256,128]{2,1,0,3:T(8,128)(2,1)S(1)} copy(bf16[4,6,256,128]{3,2,1,0:T(8,128)(2,1)} %fusion.13) | data formatting | bytes 3145728 | tf_op jit(solution)/shard_map/gtij,gtjf->gtif/dot_general | solution.py:15
  45.8 0.9 fusion.7
  46.6 0.1 copy.14
  46.7 0.0 copy-start.3
  46.8 0.0 all-to-all-done
  46.8 2.3 %scatter_custom_fusion = f32[512,256]{1,0:T(8,128)S(1)} fusion(f32[512,256]{1,0:T(8,128)S(1)} %bitcast.128, s32[256]{0:T(256)S(1)} %bitcast.135, bf16[256,256]{1,0:T(8,128)(2,1)S(1)} %bitcast.129, f32[256]{0:T(256)S(1)} %mul.26), kind=kCustom, calls=%fused_computation.25 | custom fusion | flops 196608 | bytes 656384 | tf_op jit(solution)/shard_map/scatter-add | solution.py:76
  49.0 0.7 convert_bitcast_fusion
  49.8 7.3 %reduce-scatter.2.cloned.1.call-done = bf16[512,256]{1,0:T(8,128)(2,1)} async-done(((bf16[2048,256]{1,0:T(8,128)(2,1)}), bf16[512,256]{1,0:T(8,128)(2,1)}) %reduce-scatter.2.cloned.1.call-update) | async-done | bytes 262160 | tf_op jit(solution)/shard_map/reduce_scatter | solution.py:85
  57.1 1.0 convert_element_type.47
  58.1 2.2 %scatter_custom_fusion.1 = f32[512,256]{1,0:T(8,128)S(1)} fusion(f32[512,256]{1,0:T(8,128)S(1)} %convert_element_type.47, s32[256]{0:T(256)S(1)} %bitcast.134, bf16[256,256]{1,0:T(8,128)(2,1)S(1)} %bitcast.131), kind=kCustom, calls=%fused_computation.20 | custom fusion | flops 131072 | bytes 655360 | tf_op jit(solution)/shard_map/scatter-add | solution.py:81
  60.3 0.0 copy-done.3
  60.3 1.0 convolution_bitcast_fusion
  61.2 0.0 all-reduce.2.cloned.1.call-update
  61.3 0.0 copy-done.4
  61.3 1.0 fusion.10
  62.2 126.9 %all-reduce.2.cloned.1.call-done = f32[256,256]{0,1:T(8,128)} async-done(((f32[256,256]{0,1:T(8,128)}), f32[256,256]{0,1:T(8,128)}) %all-reduce.2.cloned.1.call-update) | async-done | bytes 262160 | tf_op jit(solution)/shard_map/psum | solution.py:99
  189.1 1.0 broadcast_multiply_fusion
  190.1 0.8 copy.16
  (12 shorter events, 0.1 us)
Async XLA Ops:
  7.2 3.6 %copy-start = (bf16[1,1,4,6,128,128]{5,4,3,2,1,0:T(8,128)(2,1)S(1)}, bf16[1,1,4,6,128,128]{5,4,3,2,1,0:T(8,128)(2,1)}, u32[]{:S(2)}) copy-start(bf16[1,1,4,6,128,128]{5,4,3,2,1,0:T(8,128)(2,1)} %param.12) | copy-start | bytes 2359300
  7.2 2.9 %copy-start.1 = (bf16[1,512,256]{2,1,0:T(8,128)(2,1)S(1)}, bf16[1,512,256]{2,1,0:T(8,128)(2,1)}, u32[]{:S(2)}) copy-start(bf16[1,512,256]{2,1,0:T(8,128)(2,1)} %param.19) | copy-start | bytes 786436
  7.2 31.5 %all-gather.2.cloned.1.call-start = ((), (), s32[]{:S(2)}) async-start(), calls=%async_computation.3 | async-start | bytes 1310720 | tf_op jit(solution)/shard_map/all_gather | solution.py:71
  9.3 47.8 %reduce-scatter.2.cloned.1.call-start = ((), (), s32[]{:S(2)}) async-start(), calls=%async_computation.4 | async-start | bytes 1310720 | tf_op jit(solution)/shard_map/reduce_scatter | solution.py:85
  12.6 3.3 %copy-start.9 = (s32[1,1,4]{2,1,0:T(1,128)S(1)}, s32[1,1,4]{2,1,0:T(1,128)}, u32[]{:S(2)}) copy-start(s32[1,1,4]{2,1,0:T(1,128)} %param.14) | copy-start | bytes 52
  12.6 3.3 %copy-start.8 = (s32[1,1,4,6]{3,2,1,0:T(4,128)S(1)}, s32[1,1,4,6]{3,2,1,0:T(4,128)}, u32[]{:S(2)}) copy-start(s32[1,1,4,6]{3,2,1,0:T(4,128)} %param.13) | copy-start | bytes 292
  16.6 1.2 copy-start.6
  17.8 1.3 copy-start.5
  17.8 9.4 %copy-start.7 = (s32[1,1,8,32]{3,2,1,0:T(8,128)S(1)}, s32[1,1,8,32]{3,2,1,0:T(8,128)}, u32[]{:S(2)}) copy-start(s32[1,1,8,32]{3,2,1,0:T(8,128)} %param.15) | copy-start | bytes 3076
  17.8 9.5 %copy-start.10 = (s32[1,1,8]{2,1,0:T(1,128)S(1)}, s32[1,1,8]{2,1,0:T(1,128)}, u32[]{:S(2)}) copy-start(s32[1,1,8]{2,1,0:T(1,128)} %param.16) | copy-start | bytes 100
  17.8 9.8 %copy-start.2 = (bf16[512,256]{1,0:T(8,128)(2,1)S(1)}, bf16[512,256]{1,0:T(8,128)(2,1)}, u32[]{:S(2)}) copy-start(bf16[512,256]{1,0:T(8,128)(2,1)} %convolution_convert_fusion.1) | copy-start | bytes 786436
  19.8 14.6 %all-to-all-start.1 = ((bf16[8,32,256]{2,1,0:T(8,128)(2,1)}), bf16[8,32,256]{2,1,0:T(8,128)(2,1)S(1)}, u32[]{:S(2)}, u32[]{:S(2)}) async-start(bf16[8,32,256]{2,1,0:T(8,128)(2,1)} %fusion.17), calls=%async_computation.2 | async-start | bytes 262144 | tf_op jit(solution)/shard_map/all_to_all | solution.py:79
  35.2 11.6 %all-to-all-start = ((bf16[8,32,256]{2,1,0:T(8,128)(2,1)}), bf16[8,32,256]{2,1,0:T(8,128)(2,1)S(1)}, u32[]{:S(2)}, u32[]{:S(2)}) async-start(bf16[8,32,256]{2,1,0:T(8,128)(2,1)} %get-tuple-element.14), calls=%async_computation | async-start | bytes 262144 | tf_op jit(solution)/shard_map/all_to_all | solution.py:74
  38.6 150.5 %all-reduce.2.cloned.1.call-start = ((), (), s32[]{:S(2)}) async-start(), calls=%async_computation.5 | async-start | bytes 524288 | tf_op jit(solution)/shard_map/psum | solution.py:99
  46.7 13.5 %copy-start.3 = (bf16[1,512,256]{2,1,0:T(8,128)(2,1)S(1)}, bf16[1,512,256]{2,1,0:T(8,128)(2,1)}, u32[]{:S(2)}) copy-start(bf16[1,512,256]{2,1,0:T(8,128)(2,1)} %param.10) | copy-start | bytes 786436
  49.8 11.5 %copy-start.4 = (bf16[256,256]{1,0:T(8,128)(2,1)S(1)}, bf16[256,256]{1,0:T(8,128)(2,1)}, u32[]{:S(2)}) copy-start(bf16[256,256]{1,0:T(8,128)(2,1)} %param.11) | copy-start | bytes 393220
Sparse Core Ops, SparseCore 0:
  10.2 19.4 all-gather.1
  32.1 24.8 reduce-scatter.1
  64.1 124.9 all-reduce.1
where the time goes:
time: 198 us; the launch traced here: 197 us
  waiting for transfers between devices  140 us (71%)
  local copies, waits for them, and re-layouts  14.2 us (7%)
  between operations  14 us (7%)
  starting transfers between devices  10.7 us (5%)
  other arithmetic  9.56 us (5%)
  matrix products  9.09 us (5%)
    psum x1, waiting for transfers between devices, on_device(): total = lax.psum(weight_term, ('blk', 'dom'))  127 us
    reduce_scatter x1, waiting for transfers between devices, on_device(): lax.psum_scatter(spread_cols(part_tiles, part_pos, part_count, grad_in, p...  7.3 us
    all_to_all x1, starting transfers between devices, on_device(): lax.all_to_all(back, 'dom', split_axis=0, concat_axis=0, tiled=True)  7.25 us
    all_to_all x1, waiting for transfers between devices, on_device(): lax.all_to_all(back, 'dom', split_axis=0, concat_axis=0, tiled=True)  5.68 us
  transfers between devices with their start and end apart: 5, of which 3 were waited for; matrix products, arithmetic and copies ran while one was open for 13% of the time, Pallas kernels for 0%

commit v1 on v0

v1 whole, which is shorter than its diff:
```python
import functools
import jax
import jax.numpy as jnp
from jax import lax
from jax.experimental import pallas as pl
from jax.experimental.pallas import tpu as pltpu
from jax.sharding import PartitionSpec as P

BF16 = jnp.bfloat16
F32 = jnp.float32
VMEM = pl.BlockSpec(memory_space=pltpu.VMEM)
SMEM = pl.BlockSpec(memory_space=pltpu.SMEM)
MIB = 1 << 20


def swap(value, axis, bit):
    return lax.ppermute(value, axis, [(i, i ^ bit) for i in range(lax.axis_size(axis))])


def bits_of(size):
    return [1 << k for k in range(size.bit_length() - 1)]


def matmul(left, right, left_dim, right_dim):
    return lax.dot_general(
        left, right, (((left_dim,), (right_dim,)), ((), ())), preferred_element_type=F32
    )


def one_hot(rows, index):
    return lax.broadcasted_iota(jnp.int32, (rows, index.shape[1]), 0) == index


def halo_kernel(feats, grad, send_index, owner, edge, out):
    rows, width = feats.shape
    peers, both, unused = out.shape
    slots = both // 2
    sent = matmul(one_hot(rows, send_index[...]).astype(BF16), feats[...], 0, 0)
    out[:, :slots, :] = sent.astype(BF16).reshape(peers, slots, width)
    weights = jnp.where(one_hot(rows, owner[...]), edge[...], 0.0).astype(BF16)
    back = matmul(weights, grad[...], 0, 0)
    out[:, slots:, :] = back.astype(BF16).reshape(peers, slots, width)


def adjacency_kernel(blk, pos, count, tiles, grad, dense, keep, send):
    groups, slots, tile, unused = tiles.shape
    rows, width = grad.shape
    per = rows // tile
    dense[...] = jnp.zeros_like(dense)
    for j in range(groups):
        c = blk[0] ^ j
        for t in range(slots):
            spot = pos[c * slots + t]
            row = pl.multiple_of((spot // per) * tile, tile)
            column = pl.multiple_of(j * rows + (spot % per) * tile, tile)
            live = t < count[c]
            dense[pl.ds(row, tile), pl.ds(column, tile)] = jnp.where(
                live, tiles[c, t], jnp.zeros((), BF16)
            )
    turned = grad[...].T
    for j in range(groups):
        part = matmul(turned, dense[:, j * rows : (j + 1) * rows], 1, 0).astype(BF16)
        (send if j % 2 else keep)[j // 2] = part


def forward_kernel(groups, blk, dense, halo, owner, edge, grad, *refs):
    panels, (agg, keep, send, term) = refs[:groups], refs[groups:]
    rows, width = grad.shape
    slots = halo.shape[1] // 2
    total = matmul(dense[:, :rows], panels[0][...], 1, 0)
    for j in range(1, groups):
        total += matmul(dense[:, j * rows : (j + 1) * rows], panels[j][...], 1, 0)
    weights = jnp.where(one_hot(rows, owner[...]), edge[...], 0.0).astype(BF16)
    total += matmul(weights, halo[:, :slots, :].reshape(-1, width), 1, 0)
    rounded = total.astype(BF16)
    agg[...] = rounded
    term[...] = matmul(rounded, grad[...], 0, 0)
    half = width // 2
    core = blk[0] % 2
    keep[...] = term[pl.ds(pl.multiple_of(core * half, half), half), :].astype(BF16)
    send[...] = term[pl.ds(pl.multiple_of((1 - core) * half, half), half), :].astype(BF16)


def output_kernel(agg, weight, out):
    out[...] = matmul(agg[...], weight[...], 1, 0).astype(BF16)


def backward_kernel(first, second, third, halo, send_index, weight, out):
    rows, width = out.shape
    slots = halo.shape[1] // 2
    local = first[...].astype(F32) + second[...].astype(F32) + third[...].astype(F32)
    total = local.T + matmul(
        one_hot(rows, send_index[...]).astype(BF16), halo[:, slots:, :].reshape(-1, width), 1, 0
    )
    out[...] = matmul(total.astype(BF16), weight[...], 1, 1).astype(BF16)


def call(kernel, outs, specs, limit, scratch=()):
    return pl.pallas_call(
        kernel,
        out_shape=[jax.ShapeDtypeStruct(shape, dtype) for shape, dtype in outs],
        in_specs=specs,
        out_specs=[VMEM] * len(outs),
        scratch_shapes=list(scratch),
        compiler_params=pltpu.CompilerParams(vmem_limit_bytes=limit),
    )


def add(left, right):
    return (left.astype(F32) + right.astype(F32)).astype(BF16)


def on_device(
    features,
    weight,
    tiles,
    tile_pos,
    tile_count,
    send_list,
    send_count,
    owner_map,
    halo_weight,
    cotangent,
):
    groups, peers = lax.axis_size("blk"), lax.axis_size("dom")
    feats, grad = features[0], cotangent[0]
    rows, width = feats.shape
    slots = send_list.shape[-1]
    links = peers * slots
    me = lax.axis_index("blk").astype(jnp.int32)
    blk = me.reshape(1)
    live = jnp.arange(slots)[None, :] < send_count[0, 0][:, None]
    send_index = jnp.where(live, send_list[0, 0], -1).reshape(1, links)
    owner = owner_map[0, 0].reshape(1, links)
    edge = halo_weight[0, 0].reshape(1, links)

    (outgoing,) = call(
        halo_kernel, [((peers, 2 * slots, width), BF16)], [VMEM] * 5, 16 * MIB
    )(feats, grad, send_index, owner, edge)
    halo = lax.all_to_all(outgoing, "dom", split_axis=0, concat_axis=0, tiled=True)

    panels = {0: feats}
    for bit in reversed(bits_of(groups)):
        for j in list(panels):
            panels[j ^ bit] = swap(panels[j], "blk", bit)

    half = groups // 2
    dense, keep, send = call(
        adjacency_kernel,
        [
            ((rows, groups * rows), BF16),
            ((half, width, rows), BF16),
            ((half, width, rows), BF16),
        ],
        [SMEM] * 3 + [VMEM] * 2,
        (8 + 4 * groups) * MIB,
    )(blk, tile_pos.reshape(-1), tile_count.reshape(-1), tiles[0, 0], grad)
    got = swap(send, "blk", 1)
    for bit in bits_of(groups)[1:]:
        later = [add(keep[j], got[j]) for j in range(1, keep.shape[0], 2)]
        first = [(keep[j], got[j]) for j in range(0, keep.shape[0], 2)]
        if len(first) == 1:
            third = swap(later[0], "blk", bit)
            first, second = first[0]
        else:
            keep = jnp.stack([add(*pair) for pair in first])
            got = swap(jnp.stack(later), "blk", bit)

    agg, kept, sent = call(
        functools.partial(forward_kernel, groups),
        [((rows, width), BF16), ((width // 2, width), BF16), ((width // 2, width), BF16)],
        [SMEM] + [VMEM] * (5 + groups),
        (8 + 4 * groups) * MIB,
        [pltpu.VMEM((width, width), F32)],
    )(blk, dense, halo, owner, edge, grad, *[panels[j] for j in range(groups)])
    term = add(kept, swap(sent, "blk", 1))
    for bit in bits_of(peers):
        term = add(term, swap(term, "dom", bit))
    for bit in bits_of(groups)[1:]:
        term = add(term, swap(term, "blk", bit))
    other = swap(term, "blk", 1)
    scale = float(groups * peers * rows) ** (-0.5)
    low = jnp.where(me % 2 == 0, term, other)
    high = jnp.where(me % 2 == 0, other, term)
    weight_grad = jnp.concatenate([low, high]).astype(F32) * scale

    (layer_out,) = call(output_kernel, [((rows, width), BF16)], [VMEM] * 2, 16 * MIB)(agg, weight)
    (feature_grad,) = call(backward_kernel, [((rows, width), BF16)], [VMEM] * 6, 16 * MIB)(
        first, second, third, halo, send_index, weight
    )
    return layer_out[None], feature_grad[None], weight_grad


def solution(mesh):
    return jax.shard_map(
        on_device,
        mesh=mesh,
        in_specs=(
            P("dom", "blk", None),
            P(),
            P("dom", "blk", None, None, None, None),
            P("dom", "blk", None, None),
            P("dom", "blk", None),
            P("dom", "blk", None, None),
            P("dom", "blk", None),
            P("dom", "blk", None, None),
            P("dom", "blk", None, None),
            P("dom", "blk", None),
        ),
        out_specs=(P("dom", "blk", None), P("dom", "blk", None), P()),
        check_vma=False,
    )
```

time: 198 us -> 52 us (0.26)
  waiting for transfers between devices: 140 us -> 18 us
  between operations: 14 us -> 0.78 us
  matrix products: 9.09 us -> 0 us
  other arithmetic: 9.56 us -> 1.63 us
  Pallas kernels: 0 us -> 7.79 us
  local copies, waits for them, and re-layouts: 14.2 us -> 7.84 us
  starting transfers between devices: 10.7 us -> 15.4 us
    psum x1 -> x0, waiting for transfers between devices: 127 us -> none  [on_device(): total = lax.psum(weight_term, ('blk', 'dom'))]
    ppermute x0 -> x11, waiting for transfers between devices: none -> 15.8 us  [swap(): lax.ppermute(value, axis, [(i, i ^ bit) for i in range(lax.axis_size(axis...]
    ppermute x0 -> x11, starting transfers between devices: none -> 9.63 us  [swap(): lax.ppermute(value, axis, [(i, i ^ bit) for i in range(lax.axis_size(axis...]
    dot_general x7 -> x0, matrix products: 9.09 us -> none  [the longest x1 2 us: on_device(): jnp.dot(feats, weight, preferred_element_type=jnp.float32)]
    pallas_call x0 -> x5, Pallas kernels: none -> 7.79 us  [the longest x1 2.47 us: on_device(): call(adjacency_kernel, [((rows, groups * rows), BF16), ((half, width, row...]
    reduce_scatter x1 -> x0, waiting for transfers between devices: 7.3 us -> none  [on_device(): lax.psum_scatter(spread_cols(part_tiles, part_pos, part_count, grad_in, p...]
    all_to_all x1 -> x0, starting transfers between devices: 7.25 us -> none  [on_device(): lax.all_to_all(back, 'dom', split_axis=0, concat_axis=0, tiled=True)]
    dot_general x3 -> x0, local copies, waits for them, and re-layouts: 6.67 us -> none  [the longest x1 3.32 us: spread_rows(): jnp.einsum('gtij,gtjf->gtif', tile_set, picked, preferred_element_type=jn...]
  transfers between devices with their start and end apart: 5 -> 12, of which waited for: 3 -> 7; matrix products, arithmetic and copies ran while one was open for 13% -> 8% of each run, Pallas kernels for 0% -> 11%
where the time goes in v1:
time: 52 us; the launch traced here: 51.5 us
  waiting for transfers between devices  18 us (35%)
  starting transfers between devices  15.4 us (30%)
  local copies, waits for them, and re-layouts  7.84 us (15%)
  Pallas kernels  7.79 us (15%)
  other arithmetic  1.63 us (3%)
  between operations  0.78 us (2%)
    ppermute x11, waiting for transfers between devices, swap(): lax.ppermute(value, axis, [(i, i ^ bit) for i in range(lax.axis_size(axis...  15.8 us
    ppermute x11, starting transfers between devices, swap(): lax.ppermute(value, axis, [(i, i ^ bit) for i in range(lax.axis_size(axis...  9.63 us
    all_to_all x1, starting transfers between devices, on_device(): lax.all_to_all(outgoing, 'dom', split_axis=0, concat_axis=0, tiled=True)  5.8 us
    unnamed x20, local copies, waits for them, and re-layouts  4.66 us
    pallas_call x1, Pallas kernels, on_device(): call(adjacency_kernel, [((rows, groups * rows), BF16), ((half, width, row...  2.47 us
    pallas_call x1, Pallas kernels, on_device(): call(functools.partial(forward_kernel, groups), [((rows, width), BF16), (...  2.22 us
    all_to_all x1, waiting for transfers between devices, on_device(): lax.all_to_all(outgoing, 'dom', split_axis=0, concat_axis=0, tiled=True)  2.14 us
    pallas_call x1, Pallas kernels, on_device(): call(backward_kernel, [((rows, width), BF16)], [VMEM] * 6, 16 * MIB)  1.11 us
  transfers between devices with their start and end apart: 12, of which 7 were waited for; matrix products, arithmetic and copies ran while one was open for 8% of the time, Pallas kernels for 11%

profile of v1, /device:TPU:0, one launch (start us, length us, event | category | flops | bytes accessed | tf_op | source)
XLA Modules:
  0.0 51.5 jit_solution(1520802180565045386)
XLA Ops:
  0.6 3.0 %collective-permute-start.1 = (bf16[512,256]{1,0:T(8,128)(2,1)}, bf16[512,256]{1,0:T(8,128)(2,1)}, u32[]{:S(2)}, u32[]{:S(2)}) collective-permute-start(bf16[512,256]{1,0:T(8,128)(2,1)} %bitcast.23), channel_id=1, source_target_pairs={{0,16},{8,24},{16,0},{24,8},{1,17},{9,25},{17,1},{25,9},{2,18},{10... | collective-permute-start | bytes 786440 | tf_op jit(solution)/shard_map/ppermute | solution.py:17
  3.7 0.7 %iota_compare_fusion = pred[8,32]{1,0:T(8,128)(4,1)S(1)} fusion(s32[8]{0:T(128)} %bitcast.31), kind=kLoop, calls=%fused_computation.12 | loop fusion | flops 256 | bytes 288 | tf_op jit(solution)/shard_map/lt | solution.py:132
  4.4 0.1 lt.37
  4.5 0.8 %squeeze.23 = s32[1,256]{1,0:T(1,128)S(1)} reshape(s32[1,1,8,32]{3,2,1,0:T(8,128)} %param.15) | data formatting | bytes 2048 | tf_op jit(solution)/shard_map/squeeze | solution.py:133
  5.2 0.8 %reshape_squeeze.6.owner = s32[1,256]{1,0:T(1,128)S(1)} reshape(s32[1,1,8,32]{3,2,1,0:T(8,128)} %param.17) | data formatting | bytes 2048 | tf_op jit(solution)/shard_map/reshape;squeeze | solution.py:134
  6.0 0.8 %reshape_squeeze.7.edge = f32[1,256]{1,0:T(1,128)S(1)} reshape(f32[1,1,8,32]{3,2,1,0:T(8,128)} %param.18) | data formatting | bytes 2048 | tf_op jit(solution)/shard_map/reshape;squeeze | solution.py:135
  6.8 0.0 copy-start
  6.8 0.9 %copy-done = bf16[1,512,256]{2,1,0:T(8,128)(2,1)S(1)} copy-done((bf16[1,512,256]{2,1,0:T(8,128)(2,1)S(1)}, bf16[1,512,256]{2,1,0:T(8,128)(2,1)}, u32[]{:S(2)}) %copy-start) | copy-done | bytes 262168
  7.7 0.0 copy-start.3
  7.7 0.9 %copy-done.3 = bf16[1,512,256]{2,1,0:T(8,128)(2,1)S(1)} copy-done((bf16[1,512,256]{2,1,0:T(8,128)(2,1)S(1)}, bf16[1,512,256]{2,1,0:T(8,128)(2,1)}, u32[]{:S(2)}) %copy-start.3) | copy-done | bytes 262168
  8.7 0.0 copy-start.2
  8.7 0.0 copy-start.4
  8.7 1.1 %shard_map.122 = bf16[8,64,256]{2,1,0:T(8,128)(2,1)} custom-call(bf16[512,256]{1,0:T(8,128)(2,1)S(1)} %bitcast.25, bf16[512,256]{1,0:T(8,128)(2,1)S(1)} %bitcast.20, s32[1,256]{1,0:T(1,128)S(1)} %broadcast_select_fusion.2.send_index, s32[1,256]{1,0:T(1,128)S(1)} %reshape_squeeze.6.owner, f32[1,256]{1,0:T(1,128)S(1)} %reshape_squeeze.7.edge), custom_call_target="tpu_custom_call" | custom-call | tf_op jit(solution)/shard_map/pallas_call | solution.py:137
  9.7 5.8 %all-to-all-start = ((bf16[8,64,256]{2,1,0:T(8,128)(2,1)}), bf16[8,64,256]{2,1,0:T(8,128)(2,1)S(1)}, u32[]{:S(2)}, u32[]{:S(2)}) async-start(bf16[8,64,256]{2,1,0:T(8,128)(2,1)} %shard_map.122), calls=%async_computation | async-start | bytes 524288 | tf_op jit(solution)/shard_map/all_to_all | solution.py:140
  15.6 0.0 collective-permute-start
  15.6 0.0 collective-permute-done.1.refs_2_
  15.6 0.5 collective-permute-start.2
  16.1 0.8 %reshape.54.pos = s32[24]{0:T(128)S(1)} reshape(s32[1,1,4,6]{3,2,1,0:T(4,128)} %param.13) | data formatting | bytes 192 | tf_op jit(solution)/shard_map/reshape | solution.py:157
  16.8 0.0 copy-start.1
  16.8 0.9 %copy-done.1 = bf16[1,512,256]{2,1,0:T(8,128)(2,1)S(1)} copy-done((bf16[1,512,256]{2,1,0:T(8,128)(2,1)S(1)}, bf16[1,512,256]{2,1,0:T(8,128)(2,1)}, u32[]{:S(2)}) %copy-start.1) | copy-done | bytes 262168
  17.8 0.0 copy-start.5
  17.8 1.1 %copy-done.5 = bf16[1,1,4,6,128,128]{5,4,3,2,1,0:T(8,128)(2,1)S(1)} copy-done((bf16[1,1,4,6,128,128]{5,4,3,2,1,0:T(8,128)(2,1)S(1)}, bf16[1,1,4,6,128,128]{5,4,3,2,1,0:T(8,128)(2,1)}, u32[]{:S(2)}) %copy-start.5) | copy-done | bytes 786456
  18.9 0.0 copy-start.9
  18.9 0.7 %copy-done.9 = s32[1,1,4]{2,1,0:T(1,128)S(1)} copy-done((s32[1,1,4]{2,1,0:T(1,128)S(1)}, s32[1,1,4]{2,1,0:T(1,128)}, u32[]{:S(2)}) %copy-start.9) | copy-done | bytes 40
  19.6 2.5 %shard_map.121 = (bf16[512,2048]{1,0:T(8,128)(2,1)S(1)}, bf16[2,256,512]{2,1,0:T(8,128)(2,1)S(1)}, bf16[2,256,512]{2,1,0:T(8,128)(2,1)}) custom-call(s32[1]{0:T(128)} %bitcast.blk, s32[24]{0:T(128)S(1)} %reshape.54.pos, s32[4]{0:T(128)S(1)} %bitcast.28, bf16[4,6,128,128]{3,2,1,0:T(8,128)(2,1)S(1)} %bitcast.27, bf16[512,256]{1,0:T(8,128)(2,1)S(1)} %bitcast.21), custom_call_target="tpu_custom_call" | custom-call | tf_op jit(solution)/shard_map/pallas_call | solution.py:148
  22.0 0.0 collective-permute-done.refs_1_
  22.0 2.1 %all-to-all-done.halo = bf16[8,64,256]{2,1,0:T(8,128)(2,1)S(1)} async-done(((bf16[8,64,256]{2,1,0:T(8,128)(2,1)}), bf16[8,64,256]{2,1,0:T(8,128)(2,1)S(1)}, u32[]{:S(2)}, u32[]{:S(2)}) %all-to-all-start) | async-done | bytes 262176 | tf_op jit(solution)/shard_map/all_to_all | solution.py:140
  24.2 0.0 collective-permute-done.2.refs_3_
  24.2 0.0 copy-done.2
  24.2 0.0 copy-done.4
  24.2 2.2 %shard_map.123 = (bf16[512,256]{1,0:T(8,128)(2,1)S(1)}, bf16[128,256]{1,0:T(8,128)(2,1)S(1)}, bf16[128,256]{1,0:T(8,128)(2,1)S(1)}) custom-call(s32[1]{0:T(128)} %bitcast.blk, bf16[512,2048]{1,0:T(8,128)(2,1)S(1)} %get-tuple-element.9.dense, bf16[8,64,256]{2,1,0:T(8,128)(2,1)S(1)} %all-to-all-done.halo, s32[1,256]{1,0:T(1,128)S(1)} %reshape_squeeze.6.owner, ...), custom_call_target="tpu_custom_call" | custom-call | tf_op jit(solution)/shard_map/pallas_call | solution.py:169
  26.4 0.0 copy-start.7
  26.4 0.0 copy-start.6
  26.5 0.1 collective-permute-start.5
  26.5 1.2 %collective-permute-done.5 = bf16[128,256]{1,0:T(8,128)(2,1)S(1)} collective-permute-done((bf16[128,256]{1,0:T(8,128)(2,1)S(1)}, bf16[128,256]{1,0:T(8,128)(2,1)S(1)}, u32[]{:S(2)}, u32[]{:S(2)}) %collective-permute-start.5) | collective-permute-done | bytes 65568 | tf_op jit(solution)/shard_map/ppermute | solution.py:17
  27.8 1.5 %collective-permute-start.6 = (bf16[128,256]{1,0:T(8,128)(2,1)S(1)}, bf16[128,256]{1,0:T(8,128)(2,1)S(1)}, u32[]{:S(2)}, u32[]{:S(2)}) collective-permute-start(bf16[128,256]{1,0:T(8,128)(2,1)S(1)} %add_convert_fusion.5), channel_id=1, source_target_pairs={{0,1},{1,0},{2,3},{3,2},{4,5},{5,4},{6,7},{7,6},{8,9},{9,8},{10,11... | collective-permute-start | bytes 196616 | tf_op jit(solution)/shard_map/ppermute | solution.py:17
  29.3 2.8 %collective-permute-done.6 = bf16[128,256]{1,0:T(8,128)(2,1)S(1)} collective-permute-done((bf16[128,256]{1,0:T(8,128)(2,1)S(1)}, bf16[128,256]{1,0:T(8,128)(2,1)S(1)}, u32[]{:S(2)}, u32[]{:S(2)}) %collective-permute-start.6) | collective-permute-done | bytes 65568 | tf_op jit(solution)/shard_map/ppermute | solution.py:17
  32.1 1.2 %collective-permute-start.7 = (bf16[128,256]{1,0:T(8,128)(2,1)S(1)}, bf16[128,256]{1,0:T(8,128)(2,1)S(1)}, u32[]{:S(2)}, u32[]{:S(2)}) collective-permute-start(bf16[128,256]{1,0:T(8,128)(2,1)S(1)} %add_convert_fusion.4), channel_id=1, source_target_pairs={{0,2},{1,3},{2,0},{3,1},{4,6},{5,7},{6,4},{7,5},{8,10},{9,11},{10,... | collective-permute-start | bytes 196616 | tf_op jit(solution)/shard_map/ppermute | solution.py:17
  33.3 0.0 collective-permute-start.3
  33.3 3.2 %collective-permute-done.7 = bf16[128,256]{1,0:T(8,128)(2,1)S(1)} collective-permute-done((bf16[128,256]{1,0:T(8,128)(2,1)S(1)}, bf16[128,256]{1,0:T(8,128)(2,1)S(1)}, u32[]{:S(2)}, u32[]{:S(2)}) %collective-permute-start.7) | collective-permute-done | bytes 65568 | tf_op jit(solution)/shard_map/ppermute | solution.py:17
  36.5 1.1 %collective-permute-start.8 = (bf16[128,256]{1,0:T(8,128)(2,1)S(1)}, bf16[128,256]{1,0:T(8,128)(2,1)S(1)}, u32[]{:S(2)}, u32[]{:S(2)}) collective-permute-start(bf16[128,256]{1,0:T(8,128)(2,1)S(1)} %add_convert_fusion.3), channel_id=1, source_target_pairs={{0,4},{1,5},{2,6},{3,7},{4,0},{5,1},{6,2},{7,3},{8,12},{9,13},{10,... | collective-permute-start | bytes 196616 | tf_op jit(solution)/shard_map/ppermute | solution.py:17
  37.6 0.0 copy-done.7
  37.6 0.0 copy-start.8
  37.7 4.8 %collective-permute-done.8 = bf16[128,256]{1,0:T(8,128)(2,1)S(1)} collective-permute-done((bf16[128,256]{1,0:T(8,128)(2,1)S(1)}, bf16[128,256]{1,0:T(8,128)(2,1)S(1)}, u32[]{:S(2)}, u32[]{:S(2)}) %collective-permute-start.8) | collective-permute-done | bytes 65568 | tf_op jit(solution)/shard_map/ppermute | solution.py:17
  42.5 0.6 %collective-permute-start.9 = (bf16[128,256]{1,0:T(8,128)(2,1)S(1)}, bf16[128,256]{1,0:T(8,128)(2,1)S(1)}, u32[]{:S(2)}, u32[]{:S(2)}) collective-permute-start(bf16[128,256]{1,0:T(8,128)(2,1)S(1)} %add_convert_fusion.2), channel_id=1, source_target_pairs={{0,16},{8,24},{16,0},{24,8},{1,17},{9,25},{17,1},{25,9},{2,18},{10... | collective-permute-start | bytes 196616 | tf_op jit(solution)/shard_map/ppermute | solution.py:17
  43.0 0.0 collective-permute-done.3
  43.0 0.1 fusion
  43.1 1.6 %collective-permute-start.4 = (bf16[256,512]{1,0:T(8,128)(2,1)S(1)}, bf16[256,512]{1,0:T(8,128)(2,1)S(1)}, u32[]{:S(2)}, u32[]{:S(2)}) collective-permute-start(bf16[256,512]{1,0:T(8,128)(2,1)S(1)} %fusion), channel_id=1, source_target_pairs={{0,16},{8,24},{16,0},{24,8},{1,17},{9,25},{17,1},{25,9},{2,18},{10... | collective-permute-start | bytes 786440 | tf_op jit(solution)/shard_map/ppermute | solution.py:17
  44.7 2.1 %collective-permute-done.9 = bf16[128,256]{1,0:T(8,128)(2,1)S(1)} collective-permute-done((bf16[128,256]{1,0:T(8,128)(2,1)S(1)}, bf16[128,256]{1,0:T(8,128)(2,1)S(1)}, u32[]{:S(2)}, u32[]{:S(2)}) %collective-permute-start.9) | collective-permute-done | bytes 65568 | tf_op jit(solution)/shard_map/ppermute | solution.py:17
  46.8 0.1 collective-permute-start.10
  46.9 0.0 copy-done.6
  46.9 0.0 copy-done.8
  46.9 0.9 %shard_map.124 = bf16[512,256]{1,0:T(8,128)(2,1)} custom-call(bf16[512,256]{1,0:T(8,128)(2,1)S(1)} %copy-done.8, bf16[256,256]{1,0:T(8,128)(2,1)S(1)} %copy-done.6), custom_call_target="tpu_custom_call" | custom-call | tf_op jit(solution)/shard_map/pallas_call | solution.py:187
  47.9 1.7 %collective-permute-done.4.third = bf16[256,512]{1,0:T(8,128)(2,1)S(1)} collective-permute-done((bf16[256,512]{1,0:T(8,128)(2,1)S(1)}, bf16[256,512]{1,0:T(8,128)(2,1)S(1)}, u32[]{:S(2)}, u32[]{:S(2)}) %collective-permute-start.4) | collective-permute-done | bytes 262176 | tf_op jit(solution)/shard_map/ppermute | solution.py:17
  49.6 1.1 %shard_map.125 = bf16[512,256]{1,0:T(8,128)(2,1)} custom-call(bf16[256,512]{1,0:T(8,128)(2,1)S(1)} %slice_bitcast_fusion.1.first, bf16[256,512]{1,0:T(8,128)(2,1)S(1)} %slice_bitcast_fusion.second, bf16[256,512]{1,0:T(8,128)(2,1)S(1)} %collective-permute-done.4.third, bf16[8,64,256]{2,1,0:T(8,128)(2,1)S(1)} %all-to-all-done.halo, ...), custom_call_target="tpu_custom_call" | custom-call | tf_op jit(solution)/shard_map/pallas_call | solution.py:188
  50.7 0.0 collective-permute-done.10
  50.7 0.7 %convert_multiply_fusion = f32[256,256]{1,0:T(8,128)} fusion(bf16[128,256]{1,0:T(8,128)(2,1)S(1)} %get-tuple-element.16, bf16[128,256]{1,0:T(8,128)(2,1)S(1)} %get-tuple-element.15), kind=kLoop, calls=%fused_computation.3 | loop fusion | flops 327680 | bytes 393216 | tf_op jit(solution)/shard_map/mul | solution.py:185
  (9 shorter events, 0.1 us)
Async XLA Ops:
  0.6 14.9 %collective-permute-start.1 = (bf16[512,256]{1,0:T(8,128)(2,1)}, bf16[512,256]{1,0:T(8,128)(2,1)}, u32[]{:S(2)}, u32[]{:S(2)}) collective-permute-start(bf16[512,256]{1,0:T(8,128)(2,1)} %bitcast.23), channel_id=1, source_target_pairs={{0,16},{8,24},{16,0},{24,8},{1,17},{9,25},{17,1},{25,9},{2,18},{10... | collective-permute-start | bytes 786440 | tf_op jit(solution)/shard_map/ppermute | solution.py:17
  6.8 1.0 %copy-start = (bf16[1,512,256]{2,1,0:T(8,128)(2,1)S(1)}, bf16[1,512,256]{2,1,0:T(8,128)(2,1)}, u32[]{:S(2)}) copy-start(bf16[1,512,256]{2,1,0:T(8,128)(2,1)} %param.19) | copy-start | bytes 786436
  7.7 0.9 %copy-start.3 = (bf16[1,512,256]{2,1,0:T(8,128)(2,1)S(1)}, bf16[1,512,256]{2,1,0:T(8,128)(2,1)}, u32[]{:S(2)}) copy-start(bf16[1,512,256]{2,1,0:T(8,128)(2,1)} %param.10) | copy-start | bytes 786436
  8.7 15.5 %copy-start.2 = (bf16[1,512,256]{2,1,0:T(8,128)(2,1)S(1)}, bf16[1,512,256]{2,1,0:T(8,128)(2,1)}, u32[]{:S(2)}) copy-start(bf16[1,512,256]{2,1,0:T(8,128)(2,1)} %param.19) | copy-start | bytes 786436
  8.7 15.5 %copy-start.4 = (bf16[1,512,256]{2,1,0:T(8,128)(2,1)S(1)}, bf16[1,512,256]{2,1,0:T(8,128)(2,1)}, u32[]{:S(2)}) copy-start(bf16[1,512,256]{2,1,0:T(8,128)(2,1)} %param.10) | copy-start | bytes 786436
  9.7 14.4 %all-to-all-start = ((bf16[8,64,256]{2,1,0:T(8,128)(2,1)}), bf16[8,64,256]{2,1,0:T(8,128)(2,1)S(1)}, u32[]{:S(2)}, u32[]{:S(2)}) async-start(bf16[8,64,256]{2,1,0:T(8,128)(2,1)} %shard_map.122), calls=%async_computation | async-start | bytes 524288 | tf_op jit(solution)/shard_map/all_to_all | solution.py:140
  15.6 6.5 %collective-permute-start = (bf16[512,256]{1,0:T(8,128)(2,1)}, bf16[512,256]{1,0:T(8,128)(2,1)}, u32[]{:S(2)}, u32[]{:S(2)}) collective-permute-start(bf16[512,256]{1,0:T(8,128)(2,1)} %bitcast.24), channel_id=1, source_target_pairs={{0,8},{8,0},{16,24},{24,16},{1,9},{9,1},{17,25},{25,17},{2,10},{10... | collective-permute-start | bytes 786440 | tf_op jit(solution)/shard_map/ppermute | solution.py:17
  15.6 8.6 %collective-permute-start.2 = (bf16[512,256]{1,0:T(8,128)(2,1)}, bf16[512,256]{1,0:T(8,128)(2,1)}, u32[]{:S(2)}, u32[]{:S(2)}) collective-permute-start(bf16[512,256]{1,0:T(8,128)(2,1)} %collective-permute-done.1.refs_2_), channel_id=1, source_target_pairs={{0,8},{8,0},{16,24},{24,16},{1,9},{9,1},{17,25},{25,17},{2,10},{10... | collective-permute-start | bytes 786440 | tf_op jit(solution)/shard_map/ppermute | solution.py:17
  16.8 1.0 %copy-start.1 = (bf16[1,512,256]{2,1,0:T(8,128)(2,1)S(1)}, bf16[1,512,256]{2,1,0:T(8,128)(2,1)}, u32[]{:S(2)}) copy-start(bf16[1,512,256]{2,1,0:T(8,128)(2,1)} %param.19) | copy-start | bytes 786436
  17.8 1.1 %copy-start.5 = (bf16[1,1,4,6,128,128]{5,4,3,2,1,0:T(8,128)(2,1)S(1)}, bf16[1,1,4,6,128,128]{5,4,3,2,1,0:T(8,128)(2,1)}, u32[]{:S(2)}) copy-start(bf16[1,1,4,6,128,128]{5,4,3,2,1,0:T(8,128)(2,1)} %param.12) | copy-start | bytes 2359300
  18.9 0.7 %copy-start.9 = (s32[1,1,4]{2,1,0:T(1,128)S(1)}, s32[1,1,4]{2,1,0:T(1,128)}, u32[]{:S(2)}) copy-start(s32[1,1,4]{2,1,0:T(1,128)} %param.14) | copy-start | bytes 52
  26.4 11.2 %copy-start.7 = (bf16[512,256]{1,0:T(8,128)(2,1)}, bf16[512,256]{1,0:T(8,128)(2,1)S(1)}, u32[]{:S(2)}) copy-start(bf16[512,256]{1,0:T(8,128)(2,1)S(1)} %get-tuple-element.10.agg) | copy-start | bytes 786436
  26.4 20.5 %copy-start.6 = (bf16[256,256]{1,0:T(8,128)(2,1)S(1)}, bf16[256,256]{1,0:T(8,128)(2,1)}, u32[]{:S(2)}) copy-start(bf16[256,256]{1,0:T(8,128)(2,1)} %weight.3) | copy-start | bytes 393220
  26.5 1.3 %collective-permute-start.5 = (bf16[128,256]{1,0:T(8,128)(2,1)S(1)}, bf16[128,256]{1,0:T(8,128)(2,1)S(1)}, u32[]{:S(2)}, u32[]{:S(2)}) collective-permute-start(bf16[128,256]{1,0:T(8,128)(2,1)S(1)} %get-tuple-element.14), channel_id=1, source_target_pairs={{0,8},{8,0},{16,24},{24,16},{1,9},{9,1},{17,25},{25,17},{2,10},{10... | collective-permute-start | bytes 196616 | tf_op jit(solution)/shard_map/ppermute | solution.py:17
  27.8 4.3 %collective-permute-start.6 = (bf16[128,256]{1,0:T(8,128)(2,1)S(1)}, bf16[128,256]{1,0:T(8,128)(2,1)S(1)}, u32[]{:S(2)}, u32[]{:S(2)}) collective-permute-start(bf16[128,256]{1,0:T(8,128)(2,1)S(1)} %add_convert_fusion.5), channel_id=1, source_target_pairs={{0,1},{1,0},{2,3},{3,2},{4,5},{5,4},{6,7},{7,6},{8,9},{9,8},{10,11... | collective-permute-start | bytes 196616 | tf_op jit(solution)/shard_map/ppermute | solution.py:17
  32.1 4.3 %collective-permute-start.7 = (bf16[128,256]{1,0:T(8,128)(2,1)S(1)}, bf16[128,256]{1,0:T(8,128)(2,1)S(1)}, u32[]{:S(2)}, u32[]{:S(2)}) collective-permute-start(bf16[128,256]{1,0:T(8,128)(2,1)S(1)} %add_convert_fusion.4), channel_id=1, source_target_pairs={{0,2},{1,3},{2,0},{3,1},{4,6},{5,7},{6,4},{7,5},{8,10},{9,11},{10,... | collective-permute-start | bytes 196616 | tf_op jit(solution)/shard_map/ppermute | solution.py:17
  33.3 9.7 %collective-permute-start.3 = (bf16[2,256,512]{2,1,0:T(8,128)(2,1)}, bf16[2,256,512]{2,1,0:T(8,128)(2,1)S(1)}, u32[]{:S(2)}, u32[]{:S(2)}) collective-permute-start(bf16[2,256,512]{2,1,0:T(8,128)(2,1)} %get-tuple-element.12), channel_id=1, source_target_pairs={{0,8},{8,0},{16,24},{24,16},{1,9},{9,1},{17,25},{25,17},{2,10},{10... | collective-permute-start | bytes 1572872 | tf_op jit(solution)/shard_map/ppermute | solution.py:17
  36.5 5.9 %collective-permute-start.8 = (bf16[128,256]{1,0:T(8,128)(2,1)S(1)}, bf16[128,256]{1,0:T(8,128)(2,1)S(1)}, u32[]{:S(2)}, u32[]{:S(2)}) collective-permute-start(bf16[128,256]{1,0:T(8,128)(2,1)S(1)} %add_convert_fusion.3), channel_id=1, source_target_pairs={{0,4},{1,5},{2,6},{3,7},{4,0},{5,1},{6,2},{7,3},{8,12},{9,13},{10,... | collective-permute-start | bytes 196616 | tf_op jit(solution)/shard_map/ppermute | solution.py:17
  37.6 9.3 %copy-start.8 = (bf16[512,256]{1,0:T(8,128)(2,1)S(1)}, bf16[512,256]{1,0:T(8,128)(2,1)}, u32[]{:S(2)}) copy-start(bf16[512,256]{1,0:T(8,128)(2,1)} %copy-done.7) | copy-start | bytes 786436
  42.5 4.3 %collective-permute-start.9 = (bf16[128,256]{1,0:T(8,128)(2,1)S(1)}, bf16[128,256]{1,0:T(8,128)(2,1)S(1)}, u32[]{:S(2)}, u32[]{:S(2)}) collective-permute-start(bf16[128,256]{1,0:T(8,128)(2,1)S(1)} %add_convert_fusion.2), channel_id=1, source_target_pairs={{0,16},{8,24},{16,0},{24,8},{1,17},{9,25},{17,1},{25,9},{2,18},{10... | collective-permute-start | bytes 196616 | tf_op jit(solution)/shard_map/ppermute | solution.py:17
  43.1 6.5 %collective-permute-start.4 = (bf16[256,512]{1,0:T(8,128)(2,1)S(1)}, bf16[256,512]{1,0:T(8,128)(2,1)S(1)}, u32[]{:S(2)}, u32[]{:S(2)}) collective-permute-start(bf16[256,512]{1,0:T(8,128)(2,1)S(1)} %fusion), channel_id=1, source_target_pairs={{0,16},{8,24},{16,0},{24,8},{1,17},{9,25},{17,1},{25,9},{2,18},{10... | collective-permute-start | bytes 786440 | tf_op jit(solution)/shard_map/ppermute | solution.py:17
  46.8 3.9 %collective-permute-start.10 = (bf16[128,256]{1,0:T(8,128)(2,1)S(1)}, bf16[128,256]{1,0:T(8,128)(2,1)S(1)}, u32[]{:S(2)}, u32[]{:S(2)}) collective-permute-start(bf16[128,256]{1,0:T(8,128)(2,1)S(1)} %add_convert_fusion.1), channel_id=1, source_target_pairs={{0,8},{8,0},{16,24},{24,16},{1,9},{9,1},{17,25},{25,17},{2,10},{10... | collective-permute-start | bytes 196616 | tf_op jit(solution)/shard_map/ppermute | solution.py:17

commit v2 on v1

v2 whole, which is shorter than its diff:
```python
import functools
import jax
import jax.numpy as jnp
from jax import lax
from jax.experimental import pallas as pl
from jax.experimental.pallas import tpu as pltpu
from jax.sharding import PartitionSpec as P

BF16 = jnp.bfloat16
F32 = jnp.float32
VMEM = pl.BlockSpec(memory_space=pltpu.VMEM)
SMEM = pl.BlockSpec(memory_space=pltpu.SMEM)
HBM = pl.BlockSpec(memory_space=pltpu.HBM)
MIB = 1 << 20


def swap(value, axis, bit):
    return lax.ppermute(value, axis, [(i, i ^ bit) for i in range(lax.axis_size(axis))])


def swap_bits(value, bits):
    groups, peers = lax.axis_size("blk"), lax.axis_size("dom")
    b_bits = sum(bit for axis, bit in bits if axis == "blk")
    d_bits = sum(bit for axis, bit in bits if axis == "dom")
    pairs = [
        (b * peers + d, (b ^ b_bits) * peers + (d ^ d_bits))
        for b in range(groups)
        for d in range(peers)
    ]
    return lax.ppermute(value, ("blk", "dom"), pairs)


def bits_of(size):
    return [1 << k for k in range(size.bit_length() - 1)]


def matmul(left, right, left_dim, right_dim):
    return lax.dot_general(
        left, right, (((left_dim,), (right_dim,)), ((), ())), preferred_element_type=F32
    )


def one_hot(rows, index):
    return lax.broadcasted_iota(jnp.int32, (rows, index.shape[1]), 0) == index


def flat(rows):
    return jnp.concatenate([rows[q : q + 1, :] for q in range(rows.shape[0])], axis=1)


def send_index_of(send_list, send_count):
    peers, slots = send_list.shape
    peer = lax.broadcasted_iota(jnp.int32, (peers, slots), 0)
    slot = lax.broadcasted_iota(jnp.int32, (peers, slots), 1)
    count = jnp.zeros((peers, slots), jnp.int32)
    for q in range(peers):
        count = jnp.where(peer == q, send_count[q], count)
    return flat(jnp.where(slot < count, send_list[...], -1))


def fetch(pairs, sems):
    copies = [pltpu.make_async_copy(src, dst, sems.at[i]) for i, (src, dst) in enumerate(pairs)]
    for copy in copies:
        copy.start()
    return copies


def halo_kernel(feats_in, grad_in, send_in, count_in, owner_in, edge_in, out, *scratch):
    feats, grad, send, count, owner, edge, sems = scratch
    sources = (feats_in, grad_in, send_in, count_in, owner_in, edge_in)
    for copy in fetch(list(zip(sources, scratch)), sems):
        copy.wait()
    rows, width = feats.shape
    peers, both, unused = out.shape
    slots = both // 2
    pick = one_hot(rows, send_index_of(send, count)).astype(BF16)
    sent = matmul(pick, feats[...], 0, 0)
    out[:, :slots, :] = sent.astype(BF16).reshape(peers, slots, width)
    weights = jnp.where(one_hot(rows, flat(owner)), flat(edge), 0.0).astype(BF16)
    back = matmul(weights, grad[...], 0, 0)
    out[:, slots:, :] = back.astype(BF16).reshape(peers, slots, width)


def build(blk, dense, pos, count, tiles, rows):
    groups, slots, tile, unused = tiles.shape
    per = rows // tile
    for j in range(groups):
        c = blk[0] ^ j
        for t in range(slots):
            spot = pos[c, t]
            row = pl.multiple_of((spot // per) * tile, tile)
            column = pl.multiple_of(j * rows + (spot % per) * tile, tile)
            live = t < count[c]
            dense[pl.ds(row, tile), pl.ds(column, tile)] = jnp.where(
                live, tiles[c, t], jnp.zeros((), BF16)
            )


def backward_terms_kernel(groups, blk, pos_in, count_in, tiles_in, grad_in, *refs):
    (send, *keep), (dense, sems, *homes) = refs[: 1 + groups // 2], refs[1 + groups // 2 :]
    pos, count, tiles, grad = homes
    copies = fetch(list(zip((pos_in, count_in, tiles_in, grad_in), homes)), sems)
    rows, width = grad.shape
    dense[...] = jnp.zeros_like(dense)
    for copy in copies:
        copy.wait()
    build(blk, dense, pos, count, tiles, rows)
    turned = grad[...].T
    for j in range(groups):
        part = matmul(turned, dense[:, j * rows : (j + 1) * rows], 1, 0).astype(BF16)
        if j % 2:
            send[j // 2] = part
        else:
            keep[j // 2][...] = part


def local_kernel(groups, blk, pos_in, count_in, tiles_in, *refs):
    panels_in, (local, dense, sems, *homes) = refs[:groups], refs[groups:]
    pos, count, tiles, *panels = homes
    copies = fetch(list(zip((pos_in, count_in, tiles_in, *panels_in), homes)), sems)
    rows, width = local.shape
    dense[...] = jnp.zeros_like(dense)
    for copy in copies:
        copy.wait()
    build(blk, dense, pos, count, tiles, rows)
    value = matmul(dense[:, :rows], panels[0][...], 1, 0)
    for j in range(1, groups):
        value += matmul(dense[:, j * rows : (j + 1) * rows], panels[j][...], 1, 0)
    local[...] = value


def forward_kernel(blk, local, halo, owner, edge, grad, agg, keep, send, term):
    rows, width = grad.shape
    slots = halo.shape[1] // 2
    weights = jnp.where(one_hot(rows, flat(owner)), flat(edge), 0.0).astype(BF16)
    total = local[...] + matmul(weights, halo[:, :slots, :].reshape(-1, width), 1, 0)
    rounded = total.astype(BF16)
    agg[...] = rounded
    term[...] = matmul(rounded, grad[...], 0, 0)
    half = width // 2
    core = blk[0] % 2
    keep[...] = term[pl.ds(pl.multiple_of(core * half, half), half), :].astype(BF16)
    send[...] = term[pl.ds(pl.multiple_of((1 - core) * half, half), half), :].astype(BF16)


def output_kernel(agg, weight, out):
    out[...] = matmul(agg[...], weight[...], 1, 0).astype(BF16)


def backward_kernel(send_count, first, others, third, halo, send_list, weight, out):
    rows, width = out.shape
    slots = halo.shape[1] // 2
    local = first[...].astype(F32) + others[0].astype(F32) + third[...].astype(F32)
    total = local.T + matmul(
        one_hot(rows, send_index_of(send_list, send_count)).astype(BF16),
        halo[:, slots:, :].reshape(-1, width),
        1,
        0,
    )
    out[...] = matmul(total.astype(BF16), weight[...], 1, 1).astype(BF16)


def call(kernel, outs, specs, limit, scratch=()):
    return pl.pallas_call(
        kernel,
        out_shape=[jax.ShapeDtypeStruct(shape, dtype) for shape, dtype in outs],
        in_specs=specs,
        out_specs=[VMEM] * len(outs),
        scratch_shapes=list(scratch),
        compiler_params=pltpu.CompilerParams(vmem_limit_bytes=limit),
    )


def add(left, right):
    return (left.astype(F32) + right.astype(F32)).astype(BF16)


def on_device(
    features,
    weight,
    tiles,
    tile_pos,
    tile_count,
    send_list,
    send_count,
    owner_map,
    halo_weight,
    cotangent,
):
    groups, peers = lax.axis_size("blk"), lax.axis_size("dom")
    feats, grad = features[0], cotangent[0]
    rows, width = feats.shape
    slots = send_list.shape[-1]
    links = peers * slots
    me = lax.axis_index("blk").astype(jnp.int32)
    blk = me.reshape(1)
    sends, send_live = send_list[0, 0], send_count[0, 0]
    owner, edge = owner_map[0, 0], halo_weight[0, 0]

    feats_far = swap(feats, "blk", groups // 2)
    (outgoing,) = call(
        halo_kernel,
        [((peers, 2 * slots, width), BF16)],
        [HBM] * 6,
        64 * MIB,
        [
            pltpu.VMEM((rows, width), BF16),
            pltpu.VMEM((rows, width), BF16),
            pltpu.VMEM((peers, slots), jnp.int32),
            pltpu.SMEM((peers,), jnp.int32),
            pltpu.VMEM((peers, slots), jnp.int32),
            pltpu.VMEM((peers, slots), F32),
            pltpu.SemaphoreType.DMA((6,)),
        ],
    )(feats, grad, sends, send_live, owner, edge)
    outgoing, near, tile_set = lax.optimization_barrier((outgoing, feats, tiles[0, 0]))
    halo = lax.all_to_all(outgoing, "dom", split_axis=0, concat_axis=0, tiled=True)

    panels = {0: near, groups // 2: feats_far}
    for bit in reversed(bits_of(groups // 2)):
        for j in list(panels):
            panels[j ^ bit] = swap(panels[j], "blk", bit)

    half = groups // 2
    tile_scratch = [
        pltpu.SMEM(tile_pos.shape[2:], jnp.int32),
        pltpu.SMEM(tile_count.shape[2:], jnp.int32),
        pltpu.VMEM(tiles.shape[2:], BF16),
    ]
    dense = pltpu.VMEM((rows, groups * rows), BF16)
    panel = pltpu.VMEM((rows, width), BF16)
    send, *keep = call(
        functools.partial(backward_terms_kernel, groups),
        [((half, width, rows), BF16)] + [((width, rows), BF16)] * half,
        [SMEM] + [HBM] * 4,
        64 * MIB,
        [dense, pltpu.SemaphoreType.DMA((4,)), *tile_scratch, panel],
    )(blk, tile_pos[0, 0], tile_count[0, 0], tile_set, grad)
    send, tile_set = lax.optimization_barrier((send, tile_set))
    got = swap(send, "blk", 1)
    (local,) = call(
        functools.partial(local_kernel, groups),
        [((rows, width), F32)],
        [SMEM] + [HBM] * (3 + groups),
        61 * MIB,
        [dense, pltpu.SemaphoreType.DMA((3 + groups,)), *tile_scratch] + [panel] * groups,
    )(
        blk,
        tile_pos[0, 0],
        tile_count[0, 0],
        tile_set,
        *[panels[j] for j in range(groups)],
    )

    agg, kept, sent = call(
        forward_kernel,
        [((rows, width), BF16), ((width // 2, width), BF16), ((width // 2, width), BF16)],
        [SMEM] + [VMEM] * 5,
        16 * MIB,
        [pltpu.VMEM((width, width), F32)],
    )(blk, local, halo, owner, edge, grad)
    other = swap(sent, "blk", 1)
    inner = bits_of(groups)[1:]
    for bit in inner:
        later = [add(keep[j], got[j]) for j in range(1, len(keep), 2)]
        if len(keep) == 2:
            third = swap(later[0], "blk", bit)
        else:
            keep = [add(keep[j], got[j]) for j in range(0, len(keep), 2)]
            got = swap(jnp.stack(later), "blk", bit)
    term = add(kept, other)
    bits = [("dom", bit) for bit in reversed(bits_of(peers))] + [("blk", bit) for bit in inner]
    fours = [bits[i : i + 2] for i in range(0, len(bits), 2)]
    for i, four in enumerate(fours):
        first, last = i == 0, i == len(fours) - 1
        if first:
            term, agg = lax.optimization_barrier((term, agg))
            (layer_out,) = call(output_kernel, [((rows, width), BF16)], [VMEM] * 2, 16 * MIB)(
                agg, weight
            )
        if last:
            (feature_grad,) = call(
                backward_kernel, [((rows, width), BF16)], [SMEM] + [VMEM] * 6, 16 * MIB
            )(send_live, keep[0], got, third, halo, sends, weight)
        others = [swap_bits(term, four[:1])]
        if len(four) == 2:
            others += [swap_bits(term, four[1:]), swap_bits(term, four)]
        if first:
            others, layer_out = lax.optimization_barrier((others, layer_out))
        if last:
            others, feature_grad = lax.optimization_barrier((others, feature_grad))
        wide = [value.astype(F32) for value in (term, *others)]
        total = wide[0] + wide[1]
        if len(four) == 2:
            total += wide[2] + wide[3]
        term = total.astype(BF16)
    other = swap(term, "blk", 1)
    scale = float(groups * peers * rows) ** (-0.5)
    low = jnp.where(me % 2 == 0, term, other)
    high = jnp.where(me % 2 == 0, other, term)
    weight_grad = jnp.concatenate([low, high]).astype(F32) * scale
    return layer_out[None], feature_grad[None], weight_grad


def solution(mesh):
    return jax.shard_map(
        on_device,
        mesh=mesh,
        in_specs=(
            P("dom", "blk", None),
            P(),
            P("dom", "blk", None, None, None, None),
            P("dom", "blk", None, None),
            P("dom", "blk", None),
            P("dom", "blk", None, None),
            P("dom", "blk", None),
            P("dom", "blk", None, None),
            P("dom", "blk", None, None),
            P("dom", "blk", None),
        ),
        out_specs=(P("dom", "blk", None), P("dom", "blk", None), P()),
        check_vma=False,
    )
```

time: 52 us -> 43.2 us (0.83)
  waiting for transfers between devices: 18 us -> 8.38 us
  local copies, waits for them, and re-layouts: 7.84 us -> 1.34 us
  Pallas kernels: 7.79 us -> 13.2 us
  starting transfers between devices: 15.4 us -> 18.2 us
  other arithmetic: 1.63 us -> 0.89 us
    ppermute x11 -> x7, waiting for transfers between devices: 15.8 us -> 2.51 us  [swap(): lax.ppermute(value, axis, [(i, i ^ bit) for i in range(lax.axis_size(axis...]
    ppermute x0 -> x6, starting transfers between devices: none -> 8.01 us  [swap_bits(): return lax.ppermute(value, ('blk', 'dom'), pairs)]
    pallas_call x4 -> x5, Pallas kernels: 6.86 us -> 12.2 us  [the longest x1 3.27 us: on_device(): call(functools.partial(local_kernel, groups), [((rows, width), F32)], [SM...]
    ppermute x11 -> x7, starting transfers between devices: 9.63 us -> 4.39 us  [swap(): lax.ppermute(value, axis, [(i, i ^ bit) for i in range(lax.axis_size(axis...]
    ppermute x0 -> x6, waiting for transfers between devices: none -> 4.16 us  [swap_bits(): return lax.ppermute(value, ('blk', 'dom'), pairs)]
    unnamed x20 -> x18, local copies, waits for them, and re-layouts: 4.66 us -> 1.34 us
    another operation x2 -> x0, local copies, waits for them, and re-layouts: 1.53 us -> none  [the longest x1 0.76 us: on_device(): owner = owner_map[0, 0].reshape(1, links)]
    squeeze x3 -> x0, local copies, waits for them, and re-layouts: 0.8 us -> none  [the longest x1 0.76 us: on_device(): send_index = jnp.where(live, send_list[0, 0], -1).reshape(1, links)]
  transfers between devices with their start and end apart: 12 -> 14, of which waited for: 7 -> 7; matrix products, arithmetic and copies ran while one was open for 8% -> 0% of each run, Pallas kernels for 11% -> 31%
where the time goes in v2:
time: 43.2 us; the launch traced here: 42.8 us
  starting transfers between devices  18.2 us (42%)
  Pallas kernels  13.2 us (31%)
  waiting for transfers between devices  8.38 us (19%)
  local copies, waits for them, and re-layouts  1.34 us (3%)
  other arithmetic  0.89 us (2%)
  between operations  0.79 us (2%)
    ppermute x6, starting transfers between devices, swap_bits(): return lax.ppermute(value, ('blk', 'dom'), pairs)  8.01 us
    all_to_all x1, starting transfers between devices, on_device(): lax.all_to_all(outgoing, 'dom', split_axis=0, concat_axis=0, tiled=True)  5.82 us
    ppermute x7, starting transfers between devices, swap(): lax.ppermute(value, axis, [(i, i ^ bit) for i in range(lax.axis_size(axis...  4.39 us
    ppermute x6, waiting for transfers between devices, swap_bits(): return lax.ppermute(value, ('blk', 'dom'), pairs)  4.16 us
    pallas_call x1, Pallas kernels, on_device(): call(functools.partial(local_kernel, groups), [((rows, width), F32)], [SM...  3.27 us
    pallas_call x1, Pallas kernels, on_device(): call(functools.partial(backward_terms_kernel, groups), [((half, width, ro...  3.04 us
    ppermute x7, waiting for transfers between devices, swap(): lax.ppermute(value, axis, [(i, i ^ bit) for i in range(lax.axis_size(axis...  2.51 us
    pallas_call x1, Pallas kernels, on_device(): call(halo_kernel, [((peers, 2 * slots, width), BF16)], [HBM] * 6, 64 * MI...  2.23 us
  transfers between devices with their start and end apart: 14, of which 7 were waited for; matrix products, arithmetic and copies ran while one was open for 0% of the time, Pallas kernels for 31%

profile of v2, /device:TPU:0, one launch (start us, length us, event | category | flops | bytes accessed | tf_op | source)
XLA Modules:
  0.0 42.8 jit_solution(17947569400795250647)
XLA Ops:
  0.6 3.0 %collective-permute-start.1 = (bf16[512,256]{1,0:T(8,128)(2,1)}, bf16[512,256]{1,0:T(8,128)(2,1)}, u32[]{:S(2)}, u32[]{:S(2)}) collective-permute-start(bf16[512,256]{1,0:T(8,128)(2,1)} %bitcast.3.feats_in.refs_0_), channel_id=1, source_target_pairs={{0,16},{8,24},{16,0},{24,8},{1,17},{9,25},{17,1},{25,9},{2,18},{10... | collective-permute-start | bytes 786440 | tf_op jit(solution)/shard_map/ppermute | solution.py:18
  3.7 2.2 %shard_map.121 = bf16[8,64,256]{2,1,0:T(8,128)(2,1)} custom-call(bf16[512,256]{1,0:T(8,128)(2,1)} %bitcast.3.feats_in.refs_0_, bf16[512,256]{1,0:T(8,128)(2,1)} %bitcast.17, s32[8,32]{1,0:T(8,128)} %bitcast.24, s32[8]{0:T(128)} %bitcast.26, s32[8,32]{1,0:T(8,128)} %bitcast.20, f32[8,32]{1,0:T(8,128)} %bitcast.22), custom_call_target="tpu_custom_call" | custom-call | tf_op jit(solution)/shard_map/pallas_call | solution.py:201
  5.9 5.8 %all-to-all-start = ((bf16[8,64,256]{2,1,0:T(8,128)(2,1)}), bf16[8,64,256]{2,1,0:T(8,128)(2,1)}, u32[]{:S(2)}, u32[]{:S(2)}) async-start(bf16[8,64,256]{2,1,0:T(8,128)(2,1)} %shard_map.121), calls=%async_computation | async-start | bytes 524288 | tf_op jit(solution)/shard_map/all_to_all | solution.py:217
  11.7 0.0 collective-permute-start
  11.7 0.0 collective-permute-done.1.refs_2_
  11.7 0.5 %collective-permute-start.2 = (bf16[512,256]{1,0:T(8,128)(2,1)}, bf16[512,256]{1,0:T(8,128)(2,1)}, u32[]{:S(2)}, u32[]{:S(2)}) collective-permute-start(bf16[512,256]{1,0:T(8,128)(2,1)} %collective-permute-done.1.refs_2_), channel_id=1, source_target_pairs={{0,8},{8,0},{16,24},{24,16},{1,9},{9,1},{17,25},{25,17},{2,10},{10... | collective-permute-start | bytes 786440 | tf_op jit(solution)/shard_map/ppermute | solution.py:18
  12.2 3.0 %shard_map.122 = (bf16[2,256,512]{2,1,0:T(8,128)(2,1)}, bf16[256,512]{1,0:T(8,128)(2,1)}, bf16[256,512]{1,0:T(8,128)(2,1)}) custom-call(s32[1]{0:T(128)} %bitcast.blk, s32[4,6]{1,0:T(4,128)} %bitcast.32, s32[4]{0:T(128)} %bitcast.34, bf16[4,6,128,128]{3,2,1,0:T(8,128)(2,1)} %bitcast.28, bf16[512,256]{1,0:T(8,128)(2,1)} %bitcast.18), custom_call_target="tpu_custom_call" | custom-call | tf_op jit(solution)/shard_map/pallas_call | solution.py:232
  15.3 0.0 copy-start
  15.3 0.0 copy-start.4
  15.3 0.0 copy-start.5
  15.3 0.1 collective-permute-start.10
  15.5 0.0 collective-permute-done.refs_1_
  15.5 0.0 collective-permute-done.2.refs_3_
  15.5 3.3 %shard_map.123.local = f32[512,256]{1,0:T(8,128)} custom-call(s32[1]{0:T(128)} %bitcast.blk, s32[4,6]{1,0:T(4,128)} %bitcast.33, s32[4]{0:T(128)} %bitcast.35, bf16[4,6,128,128]{3,2,1,0:T(8,128)(2,1)} %bitcast.29, bf16[512,256]{1,0:T(8,128)(2,1)} %bitcast.3.feats_in.refs_0_, bf16[512,256]{1,0:T(8,128)(2,1)} %collective-permute-done.refs_1_, ...), custom_call_target="tpu_custom_call" | custom-call | tf_op jit(solution)/shard_map/pallas_call | solution.py:241
  18.7 1.7 %all-to-all-done.halo = bf16[8,64,256]{2,1,0:T(8,128)(2,1)} async-done(((bf16[8,64,256]{2,1,0:T(8,128)(2,1)}), bf16[8,64,256]{2,1,0:T(8,128)(2,1)}, u32[]{:S(2)}, u32[]{:S(2)}) %all-to-all-start) | async-done | bytes 262176 | tf_op jit(solution)/shard_map/all_to_all | solution.py:217
  20.5 0.0 copy-done
  20.5 0.0 copy-done.4
  20.5 0.0 copy-done.5
  20.5 0.0 copy-start.1
  20.5 1.0 %copy-done.1 = f32[512,256]{1,0:T(8,128)S(1)} copy-done((f32[512,256]{1,0:T(8,128)S(1)}, f32[512,256]{1,0:T(8,128)}, u32[]{:S(2)}) %copy-start.1) | copy-done | bytes 524312
  21.5 0.0 copy-start.8
  21.5 1.6 %shard_map.124 = (bf16[512,256]{1,0:T(8,128)(2,1)S(1)}, bf16[128,256]{1,0:T(8,128)(2,1)S(1)}, bf16[128,256]{1,0:T(8,128)(2,1)S(1)}) custom-call(s32[1]{0:T(128)} %bitcast.blk, f32[512,256]{1,0:T(8,128)S(1)} %copy-done.1, bf16[8,64,256]{2,1,0:T(8,128)(2,1)} %all-to-all-done.halo, s32[8,32]{1,0:T(8,128)S(1)} %bitcast.21, f32[8,32]{1,0:T(8,128)S(1)} %bitcast.23, ...), custom_call_target="tpu_custom_call" | custom-call | tf_op jit(solution)/shard_map/pallas_call | solution.py:255
  23.1 0.1 collective-permute-start.3
  23.2 1.2 %collective-permute-done.3 = bf16[128,256]{1,0:T(8,128)(2,1)S(1)} collective-permute-done((bf16[128,256]{1,0:T(8,128)(2,1)S(1)}, bf16[128,256]{1,0:T(8,128)(2,1)S(1)}, u32[]{:S(2)}, u32[]{:S(2)}) %collective-permute-start.3) | collective-permute-done | bytes 65568 | tf_op jit(solution)/shard_map/ppermute | solution.py:18
  24.4 1.4 %collective-permute-start.4 = (bf16[128,256]{1,0:T(8,128)(2,1)S(1)}, bf16[128,256]{1,0:T(8,128)(2,1)S(1)}, u32[]{:S(2)}, u32[]{:S(2)}) collective-permute-start(bf16[128,256]{1,0:T(8,128)(2,1)S(1)} %add_convert_fusion.2), channel_id=1, source_target_pairs={{0,4},{1,5},{2,6},{3,7},{4,0},{5,1},{6,2},{7,3},{8,12},{9,13},{10,... | collective-permute-start | bytes 196616 | tf_op jit(solution)/shard_map/ppermute | solution.py:30
  25.8 1.5 %collective-permute-start.5 = (bf16[128,256]{1,0:T(8,128)(2,1)S(1)}, bf16[128,256]{1,0:T(8,128)(2,1)S(1)}, u32[]{:S(2)}, u32[]{:S(2)}) collective-permute-start(bf16[128,256]{1,0:T(8,128)(2,1)S(1)} %add_convert_fusion.2), channel_id=1, source_target_pairs={{0,2},{1,3},{2,0},{3,1},{4,6},{5,7},{6,4},{7,5},{8,10},{9,11},{10,... | collective-permute-start | bytes 196616 | tf_op jit(solution)/shard_map/ppermute | solution.py:30
  27.3 1.6 %collective-permute-start.6 = (bf16[128,256]{1,0:T(8,128)(2,1)S(1)}, bf16[128,256]{1,0:T(8,128)(2,1)S(1)}, u32[]{:S(2)}, u32[]{:S(2)}) collective-permute-start(bf16[128,256]{1,0:T(8,128)(2,1)S(1)} %add_convert_fusion.2), channel_id=1, source_target_pairs={{0,6},{1,7},{2,4},{3,5},{4,2},{5,3},{6,0},{7,1},{8,14},{9,15},{10,... | collective-permute-start | bytes 196616 | tf_op jit(solution)/shard_map/ppermute | solution.py:30
  28.9 0.0 collective-permute-done.10.others
  28.9 0.0 copy-done.8
  28.9 0.0 copy-start.2
  28.9 0.1 fusion
  29.0 0.6 %collective-permute-start.11 = (bf16[256,512]{1,0:T(8,128)(2,1)S(1)}, bf16[256,512]{1,0:T(8,128)(2,1)S(1)}, u32[]{:S(2)}, u32[]{:S(2)}) collective-permute-start(bf16[256,512]{1,0:T(8,128)(2,1)S(1)} %fusion), channel_id=1, source_target_pairs={{0,16},{8,24},{16,0},{24,8},{1,17},{9,25},{17,1},{25,9},{2,18},{10... | collective-permute-start | bytes 786440 | tf_op jit(solution)/shard_map/ppermute | solution.py:18
  29.5 0.3 copy-done.2
  29.8 0.9 %shard_map.125 = bf16[512,256]{1,0:T(8,128)(2,1)} custom-call(bf16[512,256]{1,0:T(8,128)(2,1)S(1)} %get-tuple-element.33.agg, bf16[256,256]{1,0:T(8,128)(2,1)S(1)} %copy-done.2), custom_call_target="tpu_custom_call" | custom-call | tf_op jit(solution)/shard_map/pallas_call | solution.py:278
  30.7 0.0 copy-start.3
  30.7 0.8 %collective-permute-done.4 = bf16[128,256]{1,0:T(8,128)(2,1)S(1)} collective-permute-done((bf16[128,256]{1,0:T(8,128)(2,1)S(1)}, bf16[128,256]{1,0:T(8,128)(2,1)S(1)}, u32[]{:S(2)}, u32[]{:S(2)}) %collective-permute-start.4) | collective-permute-done | bytes 65568 | tf_op jit(solution)/shard_map/ppermute | solution.py:30
  31.6 0.0 collective-permute-done.5
  31.6 1.8 %collective-permute-done.6 = bf16[128,256]{1,0:T(8,128)(2,1)S(1)} collective-permute-done((bf16[128,256]{1,0:T(8,128)(2,1)S(1)}, bf16[128,256]{1,0:T(8,128)(2,1)S(1)}, u32[]{:S(2)}, u32[]{:S(2)}) %collective-permute-start.6) | collective-permute-done | bytes 65568 | tf_op jit(solution)/shard_map/ppermute | solution.py:30
  33.4 0.0 copy-start.6
  33.5 0.0 copy-start.7
  33.5 1.5 %collective-permute-start.7 = (bf16[128,256]{1,0:T(8,128)(2,1)S(1)}, bf16[128,256]{1,0:T(8,128)(2,1)S(1)}, u32[]{:S(2)}, u32[]{:S(2)}) collective-permute-start(bf16[128,256]{1,0:T(8,128)(2,1)S(1)} %add_convert_fusion.1), channel_id=1, source_target_pairs={{0,1},{1,0},{2,3},{3,2},{4,5},{5,4},{6,7},{7,6},{8,9},{9,8},{10,11... | collective-permute-start | bytes 196616 | tf_op jit(solution)/shard_map/ppermute | solution.py:30
  35.0 0.5 %collective-permute-start.8 = (bf16[128,256]{1,0:T(8,128)(2,1)S(1)}, bf16[128,256]{1,0:T(8,128)(2,1)S(1)}, u32[]{:S(2)}, u32[]{:S(2)}) collective-permute-start(bf16[128,256]{1,0:T(8,128)(2,1)S(1)} %add_convert_fusion.1), channel_id=1, source_target_pairs={{0,16},{1,17},{2,18},{3,19},{4,20},{5,21},{6,22},{7,23},{8,24},{9,... | collective-permute-start | bytes 196616 | tf_op jit(solution)/shard_map/ppermute | solution.py:30
  35.5 1.5 %collective-permute-start.9 = (bf16[128,256]{1,0:T(8,128)(2,1)S(1)}, bf16[128,256]{1,0:T(8,128)(2,1)S(1)}, u32[]{:S(2)}, u32[]{:S(2)}) collective-permute-start(bf16[128,256]{1,0:T(8,128)(2,1)S(1)} %add_convert_fusion.1), channel_id=1, source_target_pairs={{0,17},{1,16},{2,19},{3,18},{4,21},{5,20},{6,23},{7,22},{8,25},{9,... | collective-permute-start | bytes 196616 | tf_op jit(solution)/shard_map/ppermute | solution.py:30
  37.0 0.0 collective-permute-done.11.third
  37.1 0.0 copy-done.3
  37.1 0.0 copy-done.6
  37.1 0.0 copy-done.7
  37.1 2.1 %shard_map.126 = bf16[512,256]{1,0:T(8,128)(2,1)} custom-call(s32[8]{0:T(128)S(1)} %bitcast.27, bf16[256,512]{1,0:T(8,128)(2,1)S(1)} %copy-done.3, bf16[2,256,512]{2,1,0:T(8,128)(2,1)S(1)} %collective-permute-done.10.others, bf16[256,512]{1,0:T(8,128)(2,1)S(1)} %collective-permute-done.11.third, bf16[8,64,256]{2,1,0:T(8,128)(2,1)} %all-to-all-done.halo, ...), custom_call_target="tpu_custom_call" | custom-call | tf_op jit(solution)/shard_map/pallas_call | solution.py:282
  39.2 0.0 collective-permute-done.7
  39.2 0.1 collective-permute-done.8
  39.3 1.4 %collective-permute-done.9 = bf16[128,256]{1,0:T(8,128)(2,1)S(1)} collective-permute-done((bf16[128,256]{1,0:T(8,128)(2,1)S(1)}, bf16[128,256]{1,0:T(8,128)(2,1)S(1)}, u32[]{:S(2)}, u32[]{:S(2)}) %collective-permute-start.9) | collective-permute-done | bytes 65568 | tf_op jit(solution)/shard_map/ppermute | solution.py:30
  40.7 0.1 collective-permute-start.12
  40.8 1.2 %collective-permute-done.12 = bf16[128,256]{1,0:T(8,128)(2,1)S(1)} collective-permute-done((bf16[128,256]{1,0:T(8,128)(2,1)S(1)}, bf16[128,256]{1,0:T(8,128)(2,1)S(1)}, u32[]{:S(2)}, u32[]{:S(2)}) %collective-permute-start.12) | collective-permute-done | bytes 65568 | tf_op jit(solution)/shard_map/ppermute | solution.py:18
  42.1 0.7 %convert_multiply_fusion = f32[256,256]{1,0:T(8,128)} fusion(bf16[128,256]{1,0:T(8,128)(2,1)S(1)} %get-tuple-element.46, bf16[128,256]{1,0:T(8,128)(2,1)S(1)} %get-tuple-element.45), kind=kLoop, calls=%fused_computation.3 | loop fusion | flops 327680 | bytes 393216 | tf_op jit(solution)/shard_map/mul | solution.py:301
  (4 shorter events, 0.1 us)
Async XLA Ops:
  0.6 11.1 %collective-permute-start.1 = (bf16[512,256]{1,0:T(8,128)(2,1)}, bf16[512,256]{1,0:T(8,128)(2,1)}, u32[]{:S(2)}, u32[]{:S(2)}) collective-permute-start(bf16[512,256]{1,0:T(8,128)(2,1)} %bitcast.3.feats_in.refs_0_), channel_id=1, source_target_pairs={{0,16},{8,24},{16,0},{24,8},{1,17},{9,25},{17,1},{25,9},{2,18},{10... | collective-permute-start | bytes 786440 | tf_op jit(solution)/shard_map/ppermute | solution.py:18
  5.9 14.6 %all-to-all-start = ((bf16[8,64,256]{2,1,0:T(8,128)(2,1)}), bf16[8,64,256]{2,1,0:T(8,128)(2,1)}, u32[]{:S(2)}, u32[]{:S(2)}) async-start(bf16[8,64,256]{2,1,0:T(8,128)(2,1)} %shard_map.121), calls=%async_computation | async-start | bytes 524288 | tf_op jit(solution)/shard_map/all_to_all | solution.py:217
  11.7 3.8 %collective-permute-start = (bf16[512,256]{1,0:T(8,128)(2,1)}, bf16[512,256]{1,0:T(8,128)(2,1)}, u32[]{:S(2)}, u32[]{:S(2)}) collective-permute-start(bf16[512,256]{1,0:T(8,128)(2,1)} %bitcast.3.feats_in.refs_0_), channel_id=1, source_target_pairs={{0,8},{8,0},{16,24},{24,16},{1,9},{9,1},{17,25},{25,17},{2,10},{10... | collective-permute-start | bytes 786440 | tf_op jit(solution)/shard_map/ppermute | solution.py:18
  11.7 3.7 %collective-permute-start.2 = (bf16[512,256]{1,0:T(8,128)(2,1)}, bf16[512,256]{1,0:T(8,128)(2,1)}, u32[]{:S(2)}, u32[]{:S(2)}) collective-permute-start(bf16[512,256]{1,0:T(8,128)(2,1)} %collective-permute-done.1.refs_2_), channel_id=1, source_target_pairs={{0,8},{8,0},{16,24},{24,16},{1,9},{9,1},{17,25},{25,17},{2,10},{10... | collective-permute-start | bytes 786440 | tf_op jit(solution)/shard_map/ppermute | solution.py:18
  15.3 5.2 %copy-start = (bf16[1,512,256]{2,1,0:T(8,128)(2,1)S(1)}, bf16[1,512,256]{2,1,0:T(8,128)(2,1)}, u32[]{:S(2)}) copy-start(bf16[1,512,256]{2,1,0:T(8,128)(2,1)} %param.19) | copy-start | bytes 786436
  15.3 5.2 %copy-start.4 = (s32[1,1,8,32]{3,2,1,0:T(8,128)S(1)}, s32[1,1,8,32]{3,2,1,0:T(8,128)}, u32[]{:S(2)}) copy-start(s32[1,1,8,32]{3,2,1,0:T(8,128)} %param.17) | copy-start | bytes 3076
  15.3 5.2 %copy-start.5 = (f32[1,1,8,32]{3,2,1,0:T(8,128)S(1)}, f32[1,1,8,32]{3,2,1,0:T(8,128)}, u32[]{:S(2)}) copy-start(f32[1,1,8,32]{3,2,1,0:T(8,128)} %param.18) | copy-start | bytes 3076
  15.3 13.6 %collective-permute-start.10 = (bf16[2,256,512]{2,1,0:T(8,128)(2,1)}, bf16[2,256,512]{2,1,0:T(8,128)(2,1)S(1)}, u32[]{:S(2)}, u32[]{:S(2)}) collective-permute-start(bf16[2,256,512]{2,1,0:T(8,128)(2,1)} %get-tuple-element.39), channel_id=1, source_target_pairs={{0,8},{8,0},{16,24},{24,16},{1,9},{9,1},{17,25},{25,17},{2,10},{10... | collective-permute-start | bytes 1572872 | tf_op jit(solution)/shard_map/ppermute | solution.py:18
  20.5 1.0 %copy-start.1 = (f32[512,256]{1,0:T(8,128)S(1)}, f32[512,256]{1,0:T(8,128)}, u32[]{:S(2)}) copy-start(f32[512,256]{1,0:T(8,128)} %shard_map.123.local) | copy-start | bytes 1572868
  21.5 7.4 %copy-start.8 = (bf16[256,512]{1,0:T(8,128)(2,1)S(1)}, bf16[256,512]{1,0:T(8,128)(2,1)}, u32[]{:S(2)}) copy-start(bf16[256,512]{1,0:T(8,128)(2,1)} %get-tuple-element.40) | copy-start | bytes 786436
  23.1 1.3 %collective-permute-start.3 = (bf16[128,256]{1,0:T(8,128)(2,1)S(1)}, bf16[128,256]{1,0:T(8,128)(2,1)S(1)}, u32[]{:S(2)}, u32[]{:S(2)}) collective-permute-start(bf16[128,256]{1,0:T(8,128)(2,1)S(1)} %get-tuple-element.30), channel_id=1, source_target_pairs={{0,8},{8,0},{16,24},{24,16},{1,9},{9,1},{17,25},{25,17},{2,10},{10... | collective-permute-start | bytes 196616 | tf_op jit(solution)/shard_map/ppermute | solution.py:18
  24.4 7.1 %collective-permute-start.4 = (bf16[128,256]{1,0:T(8,128)(2,1)S(1)}, bf16[128,256]{1,0:T(8,128)(2,1)S(1)}, u32[]{:S(2)}, u32[]{:S(2)}) collective-permute-start(bf16[128,256]{1,0:T(8,128)(2,1)S(1)} %add_convert_fusion.2), channel_id=1, source_target_pairs={{0,4},{1,5},{2,6},{3,7},{4,0},{5,1},{6,2},{7,3},{8,12},{9,13},{10,... | collective-permute-start | bytes 196616 | tf_op jit(solution)/shard_map/ppermute | solution.py:30
  25.8 5.8 %collective-permute-start.5 = (bf16[128,256]{1,0:T(8,128)(2,1)S(1)}, bf16[128,256]{1,0:T(8,128)(2,1)S(1)}, u32[]{:S(2)}, u32[]{:S(2)}) collective-permute-start(bf16[128,256]{1,0:T(8,128)(2,1)S(1)} %add_convert_fusion.2), channel_id=1, source_target_pairs={{0,2},{1,3},{2,0},{3,1},{4,6},{5,7},{6,4},{7,5},{8,10},{9,11},{10,... | collective-permute-start | bytes 196616 | tf_op jit(solution)/shard_map/ppermute | solution.py:30
  27.3 6.1 %collective-permute-start.6 = (bf16[128,256]{1,0:T(8,128)(2,1)S(1)}, bf16[128,256]{1,0:T(8,128)(2,1)S(1)}, u32[]{:S(2)}, u32[]{:S(2)}) collective-permute-start(bf16[128,256]{1,0:T(8,128)(2,1)S(1)} %add_convert_fusion.2), channel_id=1, source_target_pairs={{0,6},{1,7},{2,4},{3,5},{4,2},{5,3},{6,0},{7,1},{8,14},{9,15},{10,... | collective-permute-start | bytes 196616 | tf_op jit(solution)/shard_map/ppermute | solution.py:30
  28.9 0.9 %copy-start.2 = (bf16[256,256]{1,0:T(8,128)(2,1)S(1)}, bf16[256,256]{1,0:T(8,128)(2,1)}, u32[]{:S(2)}) copy-start(bf16[256,256]{1,0:T(8,128)(2,1)} %weight.3) | copy-start | bytes 393220
  29.0 8.1 %collective-permute-start.11 = (bf16[256,512]{1,0:T(8,128)(2,1)S(1)}, bf16[256,512]{1,0:T(8,128)(2,1)S(1)}, u32[]{:S(2)}, u32[]{:S(2)}) collective-permute-start(bf16[256,512]{1,0:T(8,128)(2,1)S(1)} %fusion), channel_id=1, source_target_pairs={{0,16},{8,24},{16,0},{24,8},{1,17},{9,25},{17,1},{25,9},{2,18},{10... | collective-permute-start | bytes 786440 | tf_op jit(solution)/shard_map/ppermute | solution.py:18
  30.7 6.3 %copy-start.3 = (bf16[256,512]{1,0:T(8,128)(2,1)S(1)}, bf16[256,512]{1,0:T(8,128)(2,1)}, u32[]{:S(2)}) copy-start(bf16[256,512]{1,0:T(8,128)(2,1)} %get-tuple-element.38.first) | copy-start | bytes 786436
  33.4 3.6 %copy-start.6 = (s32[1,1,8,32]{3,2,1,0:T(8,128)S(1)}, s32[1,1,8,32]{3,2,1,0:T(8,128)}, u32[]{:S(2)}) copy-start(s32[1,1,8,32]{3,2,1,0:T(8,128)} %param.15) | copy-start | bytes 3076
  33.5 3.6 %copy-start.7 = (s32[1,1,8]{2,1,0:T(1,128)S(1)}, s32[1,1,8]{2,1,0:T(1,128)}, u32[]{:S(2)}) copy-start(s32[1,1,8]{2,1,0:T(1,128)} %param.16) | copy-start | bytes 100
  33.5 5.7 %collective-permute-start.7 = (bf16[128,256]{1,0:T(8,128)(2,1)S(1)}, bf16[128,256]{1,0:T(8,128)(2,1)S(1)}, u32[]{:S(2)}, u32[]{:S(2)}) collective-permute-start(bf16[128,256]{1,0:T(8,128)(2,1)S(1)} %add_convert_fusion.1), channel_id=1, source_target_pairs={{0,1},{1,0},{2,3},{3,2},{4,5},{5,4},{6,7},{7,6},{8,9},{9,8},{10,11... | collective-permute-start | bytes 196616 | tf_op jit(solution)/shard_map/ppermute | solution.py:30
  35.0 4.3 %collective-permute-start.8 = (bf16[128,256]{1,0:T(8,128)(2,1)S(1)}, bf16[128,256]{1,0:T(8,128)(2,1)S(1)}, u32[]{:S(2)}, u32[]{:S(2)}) collective-permute-start(bf16[128,256]{1,0:T(8,128)(2,1)S(1)} %add_convert_fusion.1), channel_id=1, source_target_pairs={{0,16},{1,17},{2,18},{3,19},{4,20},{5,21},{6,22},{7,23},{8,24},{9,... | collective-permute-start | bytes 196616 | tf_op jit(solution)/shard_map/ppermute | solution.py:30
  35.5 5.2 %collective-permute-start.9 = (bf16[128,256]{1,0:T(8,128)(2,1)S(1)}, bf16[128,256]{1,0:T(8,128)(2,1)S(1)}, u32[]{:S(2)}, u32[]{:S(2)}) collective-permute-start(bf16[128,256]{1,0:T(8,128)(2,1)S(1)} %add_convert_fusion.1), channel_id=1, source_target_pairs={{0,17},{1,16},{2,19},{3,18},{4,21},{5,20},{6,23},{7,22},{8,25},{9,... | collective-permute-start | bytes 196616 | tf_op jit(solution)/shard_map/ppermute | solution.py:30
  40.7 1.3 %collective-permute-start.12 = (bf16[128,256]{1,0:T(8,128)(2,1)S(1)}, bf16[128,256]{1,0:T(8,128)(2,1)S(1)}, u32[]{:S(2)}, u32[]{:S(2)}) collective-permute-start(bf16[128,256]{1,0:T(8,128)(2,1)S(1)} %add_convert_fusion), channel_id=1, source_target_pairs={{0,8},{8,0},{16,24},{24,16},{1,9},{9,1},{17,25},{25,17},{2,10},{10... | collective-permute-start | bytes 196616 | tf_op jit(solution)/shard_map/ppermute | solution.py:18

commit v3 on v2

--- a/solution.py
+++ b/solution.py
@@ -81,9 +81,18 @@
     out[:, slots:, :] = back.astype(BF16).reshape(peers, slots, width)
 
 
-def build(blk, dense, pos, count, tiles, rows):
-    groups, slots, tile, unused = tiles.shape
+def adjacency_kernel(groups, blk, pos_in, count_in, tiles_in, grad_in, *refs):
+    panels_in, refs = refs[:groups], refs[groups:]
+    (local, send, *keep), refs = refs[: 2 + groups // 2], refs[2 + groups // 2 :]
+    dense, sems, *homes = refs
+    pos, count, tiles, grad, *panels = homes
+    copies = fetch(list(zip((pos_in, count_in, tiles_in, grad_in, *panels_in), homes)), sems)
+    unused, slots, tile, unused = tiles.shape
+    rows, width = grad.shape
     per = rows // tile
+    dense[...] = jnp.zeros_like(dense)
+    for copy in copies:
+        copy.wait()
     for j in range(groups):
         c = blk[0] ^ j
         for t in range(slots):
@@ -94,17 +103,6 @@
             dense[pl.ds(row, tile), pl.ds(column, tile)] = jnp.where(
                 live, tiles[c, t], jnp.zeros((), BF16)
             )
-
-
-def backward_terms_kernel(groups, blk, pos_in, count_in, tiles_in, grad_in, *refs):
-    (send, *keep), (dense, sems, *homes) = refs[: 1 + groups // 2], refs[1 + groups // 2 :]
-    pos, count, tiles, grad = homes
-    copies = fetch(list(zip((pos_in, count_in, tiles_in, grad_in), homes)), sems)
-    rows, width = grad.shape
-    dense[...] = jnp.zeros_like(dense)
-    for copy in copies:
-        copy.wait()
-    build(blk, dense, pos, count, tiles, rows)
     turned = grad[...].T
     for j in range(groups):
         part = matmul(turned, dense[:, j * rows : (j + 1) * rows], 1, 0).astype(BF16)
@@ -112,17 +110,6 @@
             send[j // 2] = part
         else:
             keep[j // 2][...] = part
-
-
-def local_kernel(groups, blk, pos_in, count_in, tiles_in, *refs):
-    panels_in, (local, dense, sems, *homes) = refs[:groups], refs[groups:]
-    pos, count, tiles, *panels = homes
-    copies = fetch(list(zip((pos_in, count_in, tiles_in, *panels_in), homes)), sems)
-    rows, width = local.shape
-    dense[...] = jnp.zeros_like(dense)
-    for copy in copies:
-        copy.wait()
-    build(blk, dense, pos, count, tiles, rows)
     value = matmul(dense[:, :rows], panels[0][...], 1, 0)
     for j in range(1, groups):
         value += matmul(dense[:, j * rows : (j + 1) * rows], panels[j][...], 1, 0)
@@ -160,13 +147,14 @@
     out[...] = matmul(total.astype(BF16), weight[...], 1, 1).astype(BF16)
 
 
-def call(kernel, outs, specs, limit, scratch=()):
+def call(kernel, outs, specs, limit, scratch=(), flops=1):
     return pl.pallas_call(
         kernel,
         out_shape=[jax.ShapeDtypeStruct(shape, dtype) for shape, dtype in outs],
         in_specs=specs,
         out_specs=[VMEM] * len(outs),
         scratch_shapes=list(scratch),
+        cost_estimate=pl.CostEstimate(flops=flops, bytes_accessed=1, transcendentals=0),
         compiler_params=pltpu.CompilerParams(vmem_limit_bytes=limit),
     )
 
@@ -222,35 +210,29 @@
             panels[j ^ bit] = swap(panels[j], "blk", bit)
 
     half = groups // 2
-    tile_scratch = [
-        pltpu.SMEM(tile_pos.shape[2:], jnp.int32),
-        pltpu.SMEM(tile_count.shape[2:], jnp.int32),
-        pltpu.VMEM(tiles.shape[2:], BF16),
-    ]
-    dense = pltpu.VMEM((rows, groups * rows), BF16)
     panel = pltpu.VMEM((rows, width), BF16)
-    send, *keep = call(
-        functools.partial(backward_terms_kernel, groups),
-        [((half, width, rows), BF16)] + [((width, rows), BF16)] * half,
-        [SMEM] + [HBM] * 4,
-        64 * MIB,
-        [dense, pltpu.SemaphoreType.DMA((4,)), *tile_scratch, panel],
-    )(blk, tile_pos[0, 0], tile_count[0, 0], tile_set, grad)
-    send, tile_set = lax.optimization_barrier((send, tile_set))
-    got = swap(send, "blk", 1)
-    (local,) = call(
-        functools.partial(local_kernel, groups),
-        [((rows, width), F32)],
-        [SMEM] + [HBM] * (3 + groups),
+    local, send, *keep = call(
+        functools.partial(adjacency_kernel, groups),
+        [((rows, width), F32), ((half, width, rows), BF16)] + [((width, rows), BF16)] * half,
+        [SMEM] + [HBM] * (4 + groups),
         61 * MIB,
-        [dense, pltpu.SemaphoreType.DMA((3 + groups,)), *tile_scratch] + [panel] * groups,
+        [
+            pltpu.VMEM((rows, groups * rows), BF16),
+            pltpu.SemaphoreType.DMA((4 + groups,)),
+            pltpu.SMEM(tile_pos.shape[2:], jnp.int32),
+            pltpu.SMEM(tile_count.shape[2:], jnp.int32),
+            pltpu.VMEM(tiles.shape[2:], BF16),
+        ]
+        + [panel] * (1 + groups),
     )(
         blk,
         tile_pos[0, 0],
         tile_count[0, 0],
         tile_set,
+        grad,
         *[panels[j] for j in range(groups)],
     )
+    got = swap(send, "blk", 1)
 
     agg, kept, sent = call(
         forward_kernel,
@@ -258,6 +240,7 @@
         [SMEM] + [VMEM] * 5,
         16 * MIB,
         [pltpu.VMEM((width, width), F32)],
+        flops=2 * 10**10,
     )(blk, local, halo, owner, edge, grad)
     other = swap(sent, "blk", 1)
     inner = bits_of(groups)[1:]
@@ -269,7 +252,8 @@
             keep = [add(keep[j], got[j]) for j in range(0, len(keep), 2)]
             got = swap(jnp.stack(later), "blk", bit)
     term = add(kept, other)
-    bits = [("dom", bit) for bit in reversed(bits_of(peers))] + [("blk", bit) for bit in inner]
+    bits = [("dom", bit) for bit in bits_of(peers)]
+    bits[-1:-1] = [("blk", bit) for bit in inner]
     fours = [bits[i : i + 2] for i in range(0, len(bits), 2)]
     for i, four in enumerate(fours):
         first, last = i == 0, i == len(fours) - 1
@@ -286,7 +270,7 @@
         if len(four) == 2:
             others += [swap_bits(term, four[1:]), swap_bits(term, four)]
         if first:
-            others, layer_out = lax.optimization_barrier((others, layer_out))
+            others, layer_out, third = lax.optimization_barrier((others, layer_out, third))
         if last:
             others, feature_grad = lax.optimization_barrier((others, feature_grad))
         wide = [value.astype(F32) for value in (term, *others)]

time: 43.2 us -> 42.6 us (0.986)
  Pallas kernels: 13.2 us -> 9.44 us
  waiting for transfers between devices: 8.38 us -> 10.6 us
  local copies, waits for them, and re-layouts: 1.34 us -> 2.04 us
    pallas_call x2 -> x1, Pallas kernels: 6.31 us -> 3.99 us  [on_device(): call(functools.partial(adjacency_kernel, groups), [((rows, width), F32),...]
    ppermute x6, waiting for transfers between devices: 4.16 us -> 5.55 us  [swap_bits(): return lax.ppermute(value, ('blk', 'dom'), pairs)]
    ppermute x7, waiting for transfers between devices: 2.51 us -> 3.56 us  [swap(): lax.ppermute(value, axis, [(i, i ^ bit) for i in range(lax.axis_size(axis...]
    pallas_call x1, Pallas kernels: 1.58 us -> 0.59 us  [on_device(): call(forward_kernel, [((rows, width), BF16), ((width // 2, width), BF16),...]
    unnamed x18 -> x24, local copies, waits for them, and re-layouts: 1.34 us -> 2.04 us
  transfers between devices with their start and end apart: 14 -> 14, of which waited for: 7 -> 10; matrix products, arithmetic and copies ran while one was open for 0% -> 0% of each run, Pallas kernels for 31% -> 22%
where the time goes in v3:
time: 42.6 us; the launch traced here: 42.3 us
  starting transfers between devices  18.5 us (43%)
  waiting for transfers between devices  10.6 us (25%)
  Pallas kernels  9.44 us (22%)
  local copies, waits for them, and re-layouts  2.04 us (5%)
  other arithmetic  0.89 us (2%)
  between operations  0.78 us (2%)
    ppermute x6, starting transfers between devices, swap_bits(): return lax.ppermute(value, ('blk', 'dom'), pairs)  8.01 us
    all_to_all x1, starting transfers between devices, on_device(): lax.all_to_all(outgoing, 'dom', split_axis=0, concat_axis=0, tiled=True)  5.95 us
    ppermute x6, waiting for transfers between devices, swap_bits(): return lax.ppermute(value, ('blk', 'dom'), pairs)  5.55 us
    ppermute x7, starting transfers between devices, swap(): lax.ppermute(value, axis, [(i, i ^ bit) for i in range(lax.axis_size(axis...  4.51 us
    pallas_call x1, Pallas kernels, on_device(): call(functools.partial(adjacency_kernel, groups), [((rows, width), F32),...  3.99 us
    ppermute x7, waiting for transfers between devices, swap(): lax.ppermute(value, axis, [(i, i ^ bit) for i in range(lax.axis_size(axis...  3.56 us
    pallas_call x1, Pallas kernels, on_device(): call(halo_kernel, [((peers, 2 * slots, width), BF16)], [HBM] * 6, 64 * MI...  2.23 us
    unnamed x24, local copies, waits for them, and re-layouts  2.04 us
  transfers between devices with their start and end apart: 14, of which 10 were waited for; matrix products, arithmetic and copies ran while one was open for 0% of the time, Pallas kernels for 22%

profile of v3, /device:TPU:0, one launch (start us, length us, event | category | flops | bytes accessed | tf_op | source)
XLA Modules:
  0.0 42.3 jit_solution(16086930327125346879)
XLA Ops:
  0.6 3.0 %collective-permute-start.1 = (bf16[512,256]{1,0:T(8,128)(2,1)}, bf16[512,256]{1,0:T(8,128)(2,1)}, u32[]{:S(2)}, u32[]{:S(2)}) collective-permute-start(bf16[512,256]{1,0:T(8,128)(2,1)} %bitcast.28), channel_id=1, source_target_pairs={{0,16},{8,24},{16,0},{24,8},{1,17},{9,25},{17,1},{25,9},{2,18},{10... | collective-permute-start | bytes 786440 | tf_op jit(solution)/shard_map/ppermute | solution.py:18
  3.7 2.2 %shard_map.121 = bf16[8,64,256]{2,1,0:T(8,128)(2,1)} custom-call(bf16[512,256]{1,0:T(8,128)(2,1)} %bitcast.29, bf16[512,256]{1,0:T(8,128)(2,1)} %bitcast.17, s32[8,32]{1,0:T(8,128)} %bitcast.20, s32[8]{0:T(128)} %bitcast.26, s32[8,32]{1,0:T(8,128)} %bitcast.22, f32[8,32]{1,0:T(8,128)} %bitcast.24), custom_call_target="tpu_custom_call" | custom-call | flops 1 | bytes 1 | tf_op jit(solution)/shard_map/pallas_call | solution.py:189
  5.9 0.0 copy-start.8
  5.9 5.9 %all-to-all-start = ((bf16[8,64,256]{2,1,0:T(8,128)(2,1)}), bf16[8,64,256]{2,1,0:T(8,128)(2,1)S(1)}, u32[]{:S(2)}, u32[]{:S(2)}) async-start(bf16[8,64,256]{2,1,0:T(8,128)(2,1)} %shard_map.121), calls=%async_computation | async-start | bytes 524288 | tf_op jit(solution)/shard_map/all_to_all | solution.py:205
  11.9 0.0 copy-done.8
  11.9 0.1 collective-permute-start
  11.9 0.0 collective-permute-done.1.refs_2_
  12.0 0.5 %collective-permute-start.2 = (bf16[512,256]{1,0:T(8,128)(2,1)}, bf16[512,256]{1,0:T(8,128)(2,1)S(1)}, u32[]{:S(2)}, u32[]{:S(2)}) collective-permute-start(bf16[512,256]{1,0:T(8,128)(2,1)} %collective-permute-done.1.refs_2_), channel_id=1, source_target_pairs={{0,8},{8,0},{16,24},{24,16},{1,9},{9,1},{17,25},{25,17},{2,10},{10... | collective-permute-start | bytes 786440 | tf_op jit(solution)/shard_map/ppermute | solution.py:18
  12.4 1.0 %collective-permute-done.refs_1_ = bf16[512,256]{1,0:T(8,128)(2,1)S(1)} collective-permute-done((bf16[512,256]{1,0:T(8,128)(2,1)S(1)}, bf16[512,256]{1,0:T(8,128)(2,1)S(1)}, u32[]{:S(2)}, u32[]{:S(2)}) %collective-permute-start) | collective-permute-done | bytes 262176 | tf_op jit(solution)/shard_map/ppermute | solution.py:18
  13.5 0.0 copy-start.10
  13.5 0.6 %collective-permute-done.2.refs_3_ = bf16[512,256]{1,0:T(8,128)(2,1)S(1)} collective-permute-done((bf16[512,256]{1,0:T(8,128)(2,1)}, bf16[512,256]{1,0:T(8,128)(2,1)S(1)}, u32[]{:S(2)}, u32[]{:S(2)}) %collective-permute-start.2) | collective-permute-done | bytes 262176 | tf_op jit(solution)/shard_map/ppermute | solution.py:18
  14.1 0.0 copy-start.11
  14.1 0.1 copy-done.10
  14.2 0.6 %copy-done.11 = bf16[512,256]{1,0:T(8,128)(2,1)} copy-done((bf16[512,256]{1,0:T(8,128)(2,1)}, bf16[512,256]{1,0:T(8,128)(2,1)S(1)}, u32[]{:S(2)}) %copy-start.11) | copy-done | bytes 262168
  14.8 0.0 copy-start
  14.8 0.0 copy-start.4
  14.8 0.0 copy-start.5
  14.8 4.0 %shard_map.122 = (f32[512,256]{1,0:T(8,128)}, bf16[2,256,512]{2,1,0:T(8,128)(2,1)}, bf16[256,512]{1,0:T(8,128)(2,1)}, bf16[256,512]{1,0:T(8,128)(2,1)}) custom-call(s32[1]{0:T(128)} %bitcast.blk, s32[4,6]{1,0:T(4,128)} %bitcast.35, s32[4]{0:T(128)} %bitcast.36, bf16[4,6,128,128]{3,2,1,0:T(8,128)(2,1)} %bitcast.32, bf16[512,256]{1,0:T(8,128)(2,1)} %bitcast.18, ...), custom_call_target="tpu_custom_call" | custom-call | flops 1 | bytes 1 | tf_op jit(solution)/shard_map/pallas_call | solution.py:214
  18.8 0.2 collective-permute-start.7
  19.0 1.5 %all-to-all-done.halo = bf16[8,64,256]{2,1,0:T(8,128)(2,1)S(1)} async-done(((bf16[8,64,256]{2,1,0:T(8,128)(2,1)}), bf16[8,64,256]{2,1,0:T(8,128)(2,1)S(1)}, u32[]{:S(2)}, u32[]{:S(2)}) %all-to-all-start) | async-done | bytes 262176 | tf_op jit(solution)/shard_map/all_to_all | solution.py:205
  20.5 0.0 copy-done
  20.5 0.0 copy-done.4
  20.5 0.0 copy-done.5
  20.5 0.0 copy-start.7
  20.5 1.0 %copy-done.7 = f32[512,256]{1,0:T(8,128)S(1)} copy-done((f32[512,256]{1,0:T(8,128)S(1)}, f32[512,256]{1,0:T(8,128)}, u32[]{:S(2)}) %copy-start.7) | copy-done | bytes 524312
  21.6 0.0 copy-start.9
  21.6 0.6 %shard_map.123 = (bf16[512,256]{1,0:T(8,128)(2,1)S(1)}, bf16[128,256]{1,0:T(8,128)(2,1)S(1)}, bf16[128,256]{1,0:T(8,128)(2,1)S(1)}) custom-call(s32[1]{0:T(128)} %bitcast.blk, f32[512,256]{1,0:T(8,128)S(1)} %copy-done.7, bf16[8,64,256]{2,1,0:T(8,128)(2,1)S(1)} %all-to-all-done.halo, s32[8,32]{1,0:T(8,128)S(1)} %bitcast.23, f32[8,32]{1,0:T(8,128)S(1)} %bitcast.25, ...), custom_call_target="tpu_custom_call" | custom-call | flops 20000000000 | bytes 1 | tf_op jit(solution)/shard_map/pallas_call | solution.py:237
  22.2 0.1 collective-permute-start.3
  22.2 0.0 collective-permute-done.7.others
  22.2 0.3 copy-done.9
  22.5 0.1 fusion
  22.6 0.0 copy-start.1
  22.6 0.6 %collective-permute-start.8 = (bf16[256,512]{1,0:T(8,128)(2,1)S(1)}, bf16[256,512]{1,0:T(8,128)(2,1)S(1)}, u32[]{:S(2)}, u32[]{:S(2)}) collective-permute-start(bf16[256,512]{1,0:T(8,128)(2,1)S(1)} %fusion), channel_id=1, source_target_pairs={{0,16},{8,24},{16,0},{24,8},{1,17},{9,25},{17,1},{25,9},{2,18},{10... | collective-permute-start | bytes 786440 | tf_op jit(solution)/shard_map/ppermute | solution.py:18
  23.2 0.3 collective-permute-done.3
  23.5 1.5 %collective-permute-start.4 = (bf16[128,256]{1,0:T(8,128)(2,1)S(1)}, bf16[128,256]{1,0:T(8,128)(2,1)S(1)}, u32[]{:S(2)}, u32[]{:S(2)}) collective-permute-start(bf16[128,256]{1,0:T(8,128)(2,1)S(1)} %add_convert_fusion.2), channel_id=1, source_target_pairs={{0,1},{1,0},{2,3},{3,2},{4,5},{5,4},{6,7},{7,6},{8,9},{9,8},{10,11... | collective-permute-start | bytes 196616 | tf_op jit(solution)/shard_map/ppermute | solution.py:30
  25.0 0.5 %collective-permute-start.5 = (bf16[128,256]{1,0:T(8,128)(2,1)S(1)}, bf16[128,256]{1,0:T(8,128)(2,1)S(1)}, u32[]{:S(2)}, u32[]{:S(2)}) collective-permute-start(bf16[128,256]{1,0:T(8,128)(2,1)S(1)} %add_convert_fusion.2), channel_id=1, source_target_pairs={{0,2},{1,3},{2,0},{3,1},{4,6},{5,7},{6,4},{7,5},{8,10},{9,11},{10,... | collective-permute-start | bytes 196616 | tf_op jit(solution)/shard_map/ppermute | solution.py:30
  25.5 1.6 %collective-permute-start.6 = (bf16[128,256]{1,0:T(8,128)(2,1)S(1)}, bf16[128,256]{1,0:T(8,128)(2,1)S(1)}, u32[]{:S(2)}, u32[]{:S(2)}) collective-permute-start(bf16[128,256]{1,0:T(8,128)(2,1)S(1)} %add_convert_fusion.2), channel_id=1, source_target_pairs={{0,3},{1,2},{2,1},{3,0},{4,7},{5,6},{6,5},{7,4},{8,11},{9,10},{10,... | collective-permute-start | bytes 196616 | tf_op jit(solution)/shard_map/ppermute | solution.py:30
  27.0 0.0 copy-done.1
  27.1 0.9 %shard_map.124 = bf16[512,256]{1,0:T(8,128)(2,1)} custom-call(bf16[512,256]{1,0:T(8,128)(2,1)S(1)} %get-tuple-element.32.agg, bf16[256,256]{1,0:T(8,128)(2,1)S(1)} %copy-done.1), custom_call_target="tpu_custom_call" | custom-call | flops 1 | bytes 1 | tf_op jit(solution)/shard_map/pallas_call | solution.py:262
  28.0 0.0 copy-start.2
  28.0 0.0 collective-permute-done.4
  28.0 1.7 %collective-permute-done.5 = bf16[128,256]{1,0:T(8,128)(2,1)S(1)} collective-permute-done((bf16[128,256]{1,0:T(8,128)(2,1)S(1)}, bf16[128,256]{1,0:T(8,128)(2,1)S(1)}, u32[]{:S(2)}, u32[]{:S(2)}) %collective-permute-start.5) | collective-permute-done | bytes 65568 | tf_op jit(solution)/shard_map/ppermute | solution.py:30
  29.7 1.0 %collective-permute-done.6 = bf16[128,256]{1,0:T(8,128)(2,1)S(1)} collective-permute-done((bf16[128,256]{1,0:T(8,128)(2,1)S(1)}, bf16[128,256]{1,0:T(8,128)(2,1)S(1)}, u32[]{:S(2)}, u32[]{:S(2)}) %collective-permute-start.6) | collective-permute-done | bytes 65568 | tf_op jit(solution)/shard_map/ppermute | solution.py:30
  30.7 0.4 collective-permute-done.8.third
  31.1 0.0 copy-start.3
  31.1 0.0 copy-start.6
  31.1 2.0 %collective-permute-start.10 = (bf16[128,256]{1,0:T(8,128)(2,1)S(1)}, bf16[128,256]{1,0:T(8,128)(2,1)S(1)}, u32[]{:S(2)}, u32[]{:S(2)}) collective-permute-start(bf16[128,256]{1,0:T(8,128)(2,1)S(1)} %add_convert_fusion.1), channel_id=1, source_target_pairs={{0,4},{1,5},{2,6},{3,7},{4,0},{5,1},{6,2},{7,3},{8,12},{9,13},{10,... | collective-permute-start | bytes 196616 | tf_op jit(solution)/shard_map/ppermute | solution.py:30
  33.1 1.3 %collective-permute-start.11 = (bf16[128,256]{1,0:T(8,128)(2,1)S(1)}, bf16[128,256]{1,0:T(8,128)(2,1)S(1)}, u32[]{:S(2)}, u32[]{:S(2)}) collective-permute-start(bf16[128,256]{1,0:T(8,128)(2,1)S(1)} %add_convert_fusion.1), channel_id=1, source_target_pairs={{0,20},{1,21},{2,22},{3,23},{4,16},{5,17},{6,18},{7,19},{8,28},{9,... | collective-permute-start | bytes 196616 | tf_op jit(solution)/shard_map/ppermute | solution.py:30
  34.4 1.2 %collective-permute-start.9 = (bf16[128,256]{1,0:T(8,128)(2,1)S(1)}, bf16[128,256]{1,0:T(8,128)(2,1)S(1)}, u32[]{:S(2)}, u32[]{:S(2)}) collective-permute-start(bf16[128,256]{1,0:T(8,128)(2,1)S(1)} %add_convert_fusion.1), channel_id=1, source_target_pairs={{0,16},{1,17},{2,18},{3,19},{4,20},{5,21},{6,22},{7,23},{8,24},{9,... | collective-permute-start | bytes 196616 | tf_op jit(solution)/shard_map/ppermute | solution.py:30
  35.6 0.0 copy-done.2
  35.6 0.0 copy-done.3
  35.6 0.0 copy-done.6
  35.6 1.7 %shard_map.125 = bf16[512,256]{1,0:T(8,128)(2,1)} custom-call(s32[8]{0:T(128)S(1)} %bitcast.27, bf16[256,512]{1,0:T(8,128)(2,1)S(1)} %copy-done.2, bf16[2,256,512]{2,1,0:T(8,128)(2,1)S(1)} %collective-permute-done.7.others, bf16[256,512]{1,0:T(8,128)(2,1)S(1)} %collective-permute-done.8.third, bf16[8,64,256]{2,1,0:T(8,128)(2,1)S(1)} %all-to-all-done.halo, ...), custom_call_target="tpu_custom_call" | custom-call | flops 1 | bytes 1 | tf_op jit(solution)/shard_map/pallas_call | solution.py:266
  37.3 1.0 %collective-permute-done.10 = bf16[128,256]{1,0:T(8,128)(2,1)S(1)} collective-permute-done((bf16[128,256]{1,0:T(8,128)(2,1)S(1)}, bf16[128,256]{1,0:T(8,128)(2,1)S(1)}, u32[]{:S(2)}, u32[]{:S(2)}) %collective-permute-start.10) | collective-permute-done | bytes 65568 | tf_op jit(solution)/shard_map/ppermute | solution.py:30
  38.3 1.8 %collective-permute-done.11 = bf16[128,256]{1,0:T(8,128)(2,1)S(1)} collective-permute-done((bf16[128,256]{1,0:T(8,128)(2,1)S(1)}, bf16[128,256]{1,0:T(8,128)(2,1)S(1)}, u32[]{:S(2)}, u32[]{:S(2)}) %collective-permute-start.11) | collective-permute-done | bytes 65568 | tf_op jit(solution)/shard_map/ppermute | solution.py:30
  40.2 0.0 collective-permute-done.9
  40.2 0.1 collective-permute-start.12
  40.3 1.2 %collective-permute-done.12 = bf16[128,256]{1,0:T(8,128)(2,1)S(1)} collective-permute-done((bf16[128,256]{1,0:T(8,128)(2,1)S(1)}, bf16[128,256]{1,0:T(8,128)(2,1)S(1)}, u32[]{:S(2)}, u32[]{:S(2)}) %collective-permute-start.12) | collective-permute-done | bytes 65568 | tf_op jit(solution)/shard_map/ppermute | solution.py:18
  41.5 0.7 %convert_multiply_fusion = f32[256,256]{1,0:T(8,128)} fusion(bf16[128,256]{1,0:T(8,128)(2,1)S(1)} %get-tuple-element.46, bf16[128,256]{1,0:T(8,128)(2,1)S(1)} %get-tuple-element.45), kind=kLoop, calls=%fused_computation.3 | loop fusion | flops 327680 | bytes 393216 | tf_op jit(solution)/shard_map/mul | solution.py:285
  (4 shorter events, 0.1 us)
Async XLA Ops:
  0.6 11.3 %collective-permute-start.1 = (bf16[512,256]{1,0:T(8,128)(2,1)}, bf16[512,256]{1,0:T(8,128)(2,1)}, u32[]{:S(2)}, u32[]{:S(2)}) collective-permute-start(bf16[512,256]{1,0:T(8,128)(2,1)} %bitcast.28), channel_id=1, source_target_pairs={{0,16},{8,24},{16,0},{24,8},{1,17},{9,25},{17,1},{25,9},{2,18},{10... | collective-permute-start | bytes 786440 | tf_op jit(solution)/shard_map/ppermute | solution.py:18
  5.9 6.0 %copy-start.8 = (bf16[1,512,256]{2,1,0:T(8,128)(2,1)S(1)}, bf16[1,512,256]{2,1,0:T(8,128)(2,1)}, u32[]{:S(2)}) copy-start(bf16[1,512,256]{2,1,0:T(8,128)(2,1)} %param.10) | copy-start | bytes 786436
  5.9 14.6 %all-to-all-start = ((bf16[8,64,256]{2,1,0:T(8,128)(2,1)}), bf16[8,64,256]{2,1,0:T(8,128)(2,1)S(1)}, u32[]{:S(2)}, u32[]{:S(2)}) async-start(bf16[8,64,256]{2,1,0:T(8,128)(2,1)} %shard_map.121), calls=%async_computation | async-start | bytes 524288 | tf_op jit(solution)/shard_map/all_to_all | solution.py:205
  11.9 1.6 %collective-permute-start = (bf16[512,256]{1,0:T(8,128)(2,1)S(1)}, bf16[512,256]{1,0:T(8,128)(2,1)S(1)}, u32[]{:S(2)}, u32[]{:S(2)}) collective-permute-start(bf16[512,256]{1,0:T(8,128)(2,1)S(1)} %bitcast.31), channel_id=1, source_target_pairs={{0,8},{8,0},{16,24},{24,16},{1,9},{9,1},{17,25},{25,17},{2,10},{10... | collective-permute-start | bytes 786440 | tf_op jit(solution)/shard_map/ppermute | solution.py:18
  12.0 2.1 %collective-permute-start.2 = (bf16[512,256]{1,0:T(8,128)(2,1)}, bf16[512,256]{1,0:T(8,128)(2,1)S(1)}, u32[]{:S(2)}, u32[]{:S(2)}) collective-permute-start(bf16[512,256]{1,0:T(8,128)(2,1)} %collective-permute-done.1.refs_2_), channel_id=1, source_target_pairs={{0,8},{8,0},{16,24},{24,16},{1,9},{9,1},{17,25},{25,17},{2,10},{10... | collective-permute-start | bytes 786440 | tf_op jit(solution)/shard_map/ppermute | solution.py:18
  13.5 0.7 %copy-start.10 = (bf16[512,256]{1,0:T(8,128)(2,1)}, bf16[512,256]{1,0:T(8,128)(2,1)S(1)}, u32[]{:S(2)}) copy-start(bf16[512,256]{1,0:T(8,128)(2,1)S(1)} %collective-permute-done.refs_1_) | copy-start | bytes 786436
  14.1 0.7 %copy-start.11 = (bf16[512,256]{1,0:T(8,128)(2,1)}, bf16[512,256]{1,0:T(8,128)(2,1)S(1)}, u32[]{:S(2)}) copy-start(bf16[512,256]{1,0:T(8,128)(2,1)S(1)} %collective-permute-done.2.refs_3_) | copy-start | bytes 786436
  14.8 5.7 %copy-start = (bf16[1,512,256]{2,1,0:T(8,128)(2,1)S(1)}, bf16[1,512,256]{2,1,0:T(8,128)(2,1)}, u32[]{:S(2)}) copy-start(bf16[1,512,256]{2,1,0:T(8,128)(2,1)} %param.19) | copy-start | bytes 786436
  14.8 5.7 %copy-start.4 = (s32[1,1,8,32]{3,2,1,0:T(8,128)S(1)}, s32[1,1,8,32]{3,2,1,0:T(8,128)}, u32[]{:S(2)}) copy-start(s32[1,1,8,32]{3,2,1,0:T(8,128)} %param.17) | copy-start | bytes 3076
  14.8 5.7 %copy-start.5 = (f32[1,1,8,32]{3,2,1,0:T(8,128)S(1)}, f32[1,1,8,32]{3,2,1,0:T(8,128)}, u32[]{:S(2)}) copy-start(f32[1,1,8,32]{3,2,1,0:T(8,128)} %param.18) | copy-start | bytes 3076
  18.8 3.5 %collective-permute-start.7 = (bf16[2,256,512]{2,1,0:T(8,128)(2,1)}, bf16[2,256,512]{2,1,0:T(8,128)(2,1)S(1)}, u32[]{:S(2)}, u32[]{:S(2)}) collective-permute-start(bf16[2,256,512]{2,1,0:T(8,128)(2,1)} %get-tuple-element.34), channel_id=1, source_target_pairs={{0,8},{8,0},{16,24},{24,16},{1,9},{9,1},{17,25},{25,17},{2,10},{10... | collective-permute-start | bytes 1572872 | tf_op jit(solution)/shard_map/ppermute | solution.py:18
  20.5 1.0 %copy-start.7 = (f32[512,256]{1,0:T(8,128)S(1)}, f32[512,256]{1,0:T(8,128)}, u32[]{:S(2)}) copy-start(f32[512,256]{1,0:T(8,128)} %get-tuple-element.26.local) | copy-start | bytes 1572868
  21.6 0.9 %copy-start.9 = (bf16[256,512]{1,0:T(8,128)(2,1)S(1)}, bf16[256,512]{1,0:T(8,128)(2,1)}, u32[]{:S(2)}) copy-start(bf16[256,512]{1,0:T(8,128)(2,1)} %get-tuple-element.33) | copy-start | bytes 786436
  22.2 1.3 %collective-permute-start.3 = (bf16[128,256]{1,0:T(8,128)(2,1)S(1)}, bf16[128,256]{1,0:T(8,128)(2,1)S(1)}, u32[]{:S(2)}, u32[]{:S(2)}) collective-permute-start(bf16[128,256]{1,0:T(8,128)(2,1)S(1)} %get-tuple-element.29), channel_id=1, source_target_pairs={{0,8},{8,0},{16,24},{24,16},{1,9},{9,1},{17,25},{25,17},{2,10},{10... | collective-permute-start | bytes 196616 | tf_op jit(solution)/shard_map/ppermute | solution.py:18
  22.6 4.5 %copy-start.1 = (bf16[256,256]{1,0:T(8,128)(2,1)S(1)}, bf16[256,256]{1,0:T(8,128)(2,1)}, u32[]{:S(2)}) copy-start(bf16[256,256]{1,0:T(8,128)(2,1)} %weight.3) | copy-start | bytes 393220
  22.6 8.5 %collective-permute-start.8 = (bf16[256,512]{1,0:T(8,128)(2,1)S(1)}, bf16[256,512]{1,0:T(8,128)(2,1)S(1)}, u32[]{:S(2)}, u32[]{:S(2)}) collective-permute-start(bf16[256,512]{1,0:T(8,128)(2,1)S(1)} %fusion), channel_id=1, source_target_pairs={{0,16},{8,24},{16,0},{24,8},{1,17},{9,25},{17,1},{25,9},{2,18},{10... | collective-permute-start | bytes 786440 | tf_op jit(solution)/shard_map/ppermute | solution.py:18
  23.5 4.5 %collective-permute-start.4 = (bf16[128,256]{1,0:T(8,128)(2,1)S(1)}, bf16[128,256]{1,0:T(8,128)(2,1)S(1)}, u32[]{:S(2)}, u32[]{:S(2)}) collective-permute-start(bf16[128,256]{1,0:T(8,128)(2,1)S(1)} %add_convert_fusion.2), channel_id=1, source_target_pairs={{0,1},{1,0},{2,3},{3,2},{4,5},{5,4},{6,7},{7,6},{8,9},{9,8},{10,11... | collective-permute-start | bytes 196616 | tf_op jit(solution)/shard_map/ppermute | solution.py:30
  25.0 4.7 %collective-permute-start.5 = (bf16[128,256]{1,0:T(8,128)(2,1)S(1)}, bf16[128,256]{1,0:T(8,128)(2,1)S(1)}, u32[]{:S(2)}, u32[]{:S(2)}) collective-permute-start(bf16[128,256]{1,0:T(8,128)(2,1)S(1)} %add_convert_fusion.2), channel_id=1, source_target_pairs={{0,2},{1,3},{2,0},{3,1},{4,6},{5,7},{6,4},{7,5},{8,10},{9,11},{10,... | collective-permute-start | bytes 196616 | tf_op jit(solution)/shard_map/ppermute | solution.py:30
  25.5 5.2 %collective-permute-start.6 = (bf16[128,256]{1,0:T(8,128)(2,1)S(1)}, bf16[128,256]{1,0:T(8,128)(2,1)S(1)}, u32[]{:S(2)}, u32[]{:S(2)}) collective-permute-start(bf16[128,256]{1,0:T(8,128)(2,1)S(1)} %add_convert_fusion.2), channel_id=1, source_target_pairs={{0,3},{1,2},{2,1},{3,0},{4,7},{5,6},{6,5},{7,4},{8,11},{9,10},{10,... | collective-permute-start | bytes 196616 | tf_op jit(solution)/shard_map/ppermute | solution.py:30
  28.0 7.6 %copy-start.2 = (bf16[256,512]{1,0:T(8,128)(2,1)S(1)}, bf16[256,512]{1,0:T(8,128)(2,1)}, u32[]{:S(2)}) copy-start(bf16[256,512]{1,0:T(8,128)(2,1)} %get-tuple-element.39.first) | copy-start | bytes 786436
  31.1 4.5 %copy-start.3 = (s32[1,1,8,32]{3,2,1,0:T(8,128)S(1)}, s32[1,1,8,32]{3,2,1,0:T(8,128)}, u32[]{:S(2)}) copy-start(s32[1,1,8,32]{3,2,1,0:T(8,128)} %param.15) | copy-start | bytes 3076
  31.1 4.5 %copy-start.6 = (s32[1,1,8]{2,1,0:T(1,128)S(1)}, s32[1,1,8]{2,1,0:T(1,128)}, u32[]{:S(2)}) copy-start(s32[1,1,8]{2,1,0:T(1,128)} %param.16) | copy-start | bytes 100
  31.1 7.2 %collective-permute-start.10 = (bf16[128,256]{1,0:T(8,128)(2,1)S(1)}, bf16[128,256]{1,0:T(8,128)(2,1)S(1)}, u32[]{:S(2)}, u32[]{:S(2)}) collective-permute-start(bf16[128,256]{1,0:T(8,128)(2,1)S(1)} %add_convert_fusion.1), channel_id=1, source_target_pairs={{0,4},{1,5},{2,6},{3,7},{4,0},{5,1},{6,2},{7,3},{8,12},{9,13},{10,... | collective-permute-start | bytes 196616 | tf_op jit(solution)/shard_map/ppermute | solution.py:30
  33.1 7.0 %collective-permute-start.11 = (bf16[128,256]{1,0:T(8,128)(2,1)S(1)}, bf16[128,256]{1,0:T(8,128)(2,1)S(1)}, u32[]{:S(2)}, u32[]{:S(2)}) collective-permute-start(bf16[128,256]{1,0:T(8,128)(2,1)S(1)} %add_convert_fusion.1), channel_id=1, source_target_pairs={{0,20},{1,21},{2,22},{3,23},{4,16},{5,17},{6,18},{7,19},{8,28},{9,... | collective-permute-start | bytes 196616 | tf_op jit(solution)/shard_map/ppermute | solution.py:30
  34.4 5.8 %collective-permute-start.9 = (bf16[128,256]{1,0:T(8,128)(2,1)S(1)}, bf16[128,256]{1,0:T(8,128)(2,1)S(1)}, u32[]{:S(2)}, u32[]{:S(2)}) collective-permute-start(bf16[128,256]{1,0:T(8,128)(2,1)S(1)} %add_convert_fusion.1), channel_id=1, source_target_pairs={{0,16},{1,17},{2,18},{3,19},{4,20},{5,21},{6,22},{7,23},{8,24},{9,... | collective-permute-start | bytes 196616 | tf_op jit(solution)/shard_map/ppermute | solution.py:30
  40.2 1.3 %collective-permute-start.12 = (bf16[128,256]{1,0:T(8,128)(2,1)S(1)}, bf16[128,256]{1,0:T(8,128)(2,1)S(1)}, u32[]{:S(2)}, u32[]{:S(2)}) collective-permute-start(bf16[128,256]{1,0:T(8,128)(2,1)S(1)} %add_convert_fusion), channel_id=1, source_target_pairs={{0,8},{8,0},{16,24},{24,16},{1,9},{9,1},{17,25},{25,17},{2,10},{10... | collective-permute-start | bytes 196616 | tf_op jit(solution)/shard_map/ppermute | solution.py:18

commit v4 on v3

--- a/solution.py
+++ b/solution.py
@@ -10,7 +10,7 @@
 F32 = jnp.float32
 VMEM = pl.BlockSpec(memory_space=pltpu.VMEM)
 SMEM = pl.BlockSpec(memory_space=pltpu.SMEM)
-HBM = pl.BlockSpec(memory_space=pltpu.HBM)
+HBM = pl.BlockSpec(memory_space=pl.ANY)
 MIB = 1 << 20
 
 
@@ -76,25 +76,35 @@
     pick = one_hot(rows, send_index_of(send, count)).astype(BF16)
     sent = matmul(pick, feats[...], 0, 0)
     out[:, :slots, :] = sent.astype(BF16).reshape(peers, slots, width)
-    weights = jnp.where(one_hot(rows, flat(owner)), flat(edge), 0.0).astype(BF16)
-    back = matmul(weights, grad[...], 0, 0)
+    back = matmul(weights_of(rows, owner, edge), grad[...], 0, 0)
     out[:, slots:, :] = back.astype(BF16).reshape(peers, slots, width)
+
+
+def split_halves(blk, term, kept, sent):
+    half = term.shape[0] // 2
+    core = blk[0] % 2
+    kept[...] = term[pl.ds(pl.multiple_of(core * half, half), half), :].astype(BF16)
+    sent[...] = term[pl.ds(pl.multiple_of((1 - core) * half, half), half), :].astype(BF16)
 
 
 def adjacency_kernel(groups, blk, pos_in, count_in, tiles_in, grad_in, *refs):
     panels_in, refs = refs[:groups], refs[groups:]
-    (local, send, *keep), refs = refs[: 2 + groups // 2], refs[2 + groups // 2 :]
-    dense, sems, *homes = refs
+    (local, kept, sent, send, *keep), refs = refs[: 4 + groups // 2], refs[4 + groups // 2 :]
+    dense, term, sems, *homes = refs
     pos, count, tiles, grad, *panels = homes
-    copies = fetch(list(zip((pos_in, count_in, tiles_in, grad_in, *panels_in), homes)), sems)
     unused, slots, tile, unused = tiles.shape
     rows, width = grad.shape
     per = rows // tile
+    order = [blk[0] ^ j for j in range(groups)]
+    few = fetch([(pos_in, pos), (count_in, count), (grad_in, grad)], sems)
+    blocks = fetch([(tiles_in, tiles)], sems.at[pl.ds(3, 1)])
+    others = fetch(list(zip(panels_in, panels)), sems.at[pl.ds(4, groups)])
     dense[...] = jnp.zeros_like(dense)
-    for copy in copies:
+    for copy in few:
         copy.wait()
-    for j in range(groups):
-        c = blk[0] ^ j
+    for copy in blocks:
+        copy.wait()
+    for j, c in enumerate(order):
         for t in range(slots):
             spot = pos[c, t]
             row = pl.multiple_of((spot // per) * tile, tile)
@@ -103,6 +113,8 @@
             dense[pl.ds(row, tile), pl.ds(column, tile)] = jnp.where(
                 live, tiles[c, t], jnp.zeros((), BF16)
             )
+    for copy in others:
+        copy.wait()
     turned = grad[...].T
     for j in range(groups):
         part = matmul(turned, dense[:, j * rows : (j + 1) * rows], 1, 0).astype(BF16)
@@ -113,25 +125,32 @@
     value = matmul(dense[:, :rows], panels[0][...], 1, 0)
     for j in range(1, groups):
         value += matmul(dense[:, j * rows : (j + 1) * rows], panels[j][...], 1, 0)
-    local[...] = value
-
-
-def forward_kernel(blk, local, halo, owner, edge, grad, agg, keep, send, term):
+    rounded = value.astype(BF16)
+    local[...] = rounded
+    term[...] = matmul(rounded, grad[...], 0, 0)
+    split_halves(blk, term, kept, sent)
+
+
+def weights_of(rows, owner, edge):
+    return jnp.where(one_hot(rows, flat(owner)), flat(edge), 0.0).astype(BF16)
+
+
+def halo_sum(halo, owner, edge, rows):
+    peers, both, width = halo.shape
+    received = halo[:, : both // 2, :].reshape(-1, width)
+    return matmul(weights_of(rows, owner, edge), received, 1, 0)
+
+
+def halo_term_kernel(blk, halo, owner, edge, grad, kept, sent, term):
     rows, width = grad.shape
-    slots = halo.shape[1] // 2
-    weights = jnp.where(one_hot(rows, flat(owner)), flat(edge), 0.0).astype(BF16)
-    total = local[...] + matmul(weights, halo[:, :slots, :].reshape(-1, width), 1, 0)
-    rounded = total.astype(BF16)
-    agg[...] = rounded
-    term[...] = matmul(rounded, grad[...], 0, 0)
-    half = width // 2
-    core = blk[0] % 2
-    keep[...] = term[pl.ds(pl.multiple_of(core * half, half), half), :].astype(BF16)
-    send[...] = term[pl.ds(pl.multiple_of((1 - core) * half, half), half), :].astype(BF16)
-
-
-def output_kernel(agg, weight, out):
-    out[...] = matmul(agg[...], weight[...], 1, 0).astype(BF16)
+    term[...] = matmul(halo_sum(halo, owner, edge, rows).astype(BF16), grad[...], 0, 0)
+    split_halves(blk, term, kept, sent)
+
+
+def output_kernel(local, halo, owner, edge, weight, out):
+    rows, width = out.shape
+    total = local[...].astype(F32) + halo_sum(halo, owner, edge, rows)
+    out[...] = matmul(total.astype(BF16), weight[...], 1, 0).astype(BF16)
 
 
 def backward_kernel(send_count, first, others, third, halo, send_list, weight, out):
@@ -159,8 +178,8 @@
     )
 
 
-def add(left, right):
-    return (left.astype(F32) + right.astype(F32)).astype(BF16)
+def add(*values):
+    return sum(value.astype(F32) for value in values).astype(BF16)
 
 
 def on_device(
@@ -211,13 +230,16 @@
 
     half = groups // 2
     panel = pltpu.VMEM((rows, width), BF16)
-    local, send, *keep = call(
+    half_term = ((width // 2, width), BF16)
+    local, kept, sent, send, *keep = call(
         functools.partial(adjacency_kernel, groups),
-        [((rows, width), F32), ((half, width, rows), BF16)] + [((width, rows), BF16)] * half,
+        [((rows, width), BF16), half_term, half_term, ((half, width, rows), BF16)]
+        + [((width, rows), BF16)] * half,
         [SMEM] + [HBM] * (4 + groups),
         61 * MIB,
         [
             pltpu.VMEM((rows, groups * rows), BF16),
+            pltpu.VMEM((width, width), F32),
             pltpu.SemaphoreType.DMA((4 + groups,)),
             pltpu.SMEM(tile_pos.shape[2:], jnp.int32),
             pltpu.SMEM(tile_count.shape[2:], jnp.int32),
@@ -234,14 +256,15 @@
     )
     got = swap(send, "blk", 1)
 
-    agg, kept, sent = call(
-        forward_kernel,
-        [((rows, width), BF16), ((width // 2, width), BF16), ((width // 2, width), BF16)],
-        [SMEM] + [VMEM] * 5,
+    near_term = (kept, swap(sent, "blk", 1))
+    kept, sent = call(
+        halo_term_kernel,
+        [half_term, half_term],
+        [SMEM] + [VMEM] * 4,
         16 * MIB,
         [pltpu.VMEM((width, width), F32)],
         flops=2 * 10**10,
-    )(blk, local, halo, owner, edge, grad)
+    )(blk, halo, owner, edge, grad)
     other = swap(sent, "blk", 1)
     inner = bits_of(groups)[1:]
     for bit in inner:
@@ -251,28 +274,28 @@
         else:
             keep = [add(keep[j], got[j]) for j in range(0, len(keep), 2)]
             got = swap(jnp.stack(later), "blk", bit)
-    term = add(kept, other)
+    term = add(*near_term, kept, other)
     bits = [("dom", bit) for bit in bits_of(peers)]
     bits[-1:-1] = [("blk", bit) for bit in inner]
     fours = [bits[i : i + 2] for i in range(0, len(bits), 2)]
     for i, four in enumerate(fours):
         first, last = i == 0, i == len(fours) - 1
         if first:
-            term, agg = lax.optimization_barrier((term, agg))
-            (layer_out,) = call(output_kernel, [((rows, width), BF16)], [VMEM] * 2, 16 * MIB)(
-                agg, weight
+            term, local = lax.optimization_barrier((term, local))
+            (layer_out,) = call(output_kernel, [((rows, width), BF16)], [VMEM] * 5, 16 * MIB)(
+                local, halo, owner, edge, weight
             )
         if last:
             (feature_grad,) = call(
                 backward_kernel, [((rows, width), BF16)], [SMEM] + [VMEM] * 6, 16 * MIB
             )(send_live, keep[0], got, third, halo, sends, weight)
-        others = [swap_bits(term, four[:1])]
-        if len(four) == 2:
-            others += [swap_bits(term, four[1:]), swap_bits(term, four)]
+        ways = [four[1:], four, four[:1]] if len(four) == 2 else [four]
+        others = [swap_bits(term, way) for way in ways]
         if first:
             others, layer_out, third = lax.optimization_barrier((others, layer_out, third))
         if last:
             others, feature_grad = lax.optimization_barrier((others, feature_grad))
+        others = others[-1:] + others[:-1]
         wide = [value.astype(F32) for value in (term, *others)]
         total = wide[0] + wide[1]
         if len(four) == 2:

time: 42.6 us -> 41.5 us (0.974)
  local copies, waits for them, and re-layouts: 2.04 us -> 0.75 us
  starting transfers between devices: 18.5 us -> 19 us
  waiting for transfers between devices: 10.6 us -> 10.1 us
    unnamed x24 -> x28, local copies, waits for them, and re-layouts: 2.04 us -> 0.75 us
    ppermute x7 -> x8, starting transfers between devices: 4.51 us -> 5.01 us  [swap(): lax.ppermute(value, axis, [(i, i ^ bit) for i in range(lax.axis_size(axis...]
    ppermute x7 -> x8, waiting for transfers between devices: 3.56 us -> 3.09 us  [swap(): lax.ppermute(value, axis, [(i, i ^ bit) for i in range(lax.axis_size(axis...]
  transfers between devices with their start and end apart: 14 -> 15, of which waited for: 10 -> 11; matrix products, arithmetic and copies ran while one was open for 0% -> 0% of each run, Pallas kernels for 22% -> 23%
where the time goes in v4:
time: 41.5 us; the launch traced here: 41.2 us
  starting transfers between devices  19 us (46%)
  waiting for transfers between devices  10.1 us (24%)
  Pallas kernels  9.63 us (23%)
  other arithmetic  0.91 us (2%)
  between operations  0.79 us (2%)
  local copies, waits for them, and re-layouts  0.75 us (2%)
    ppermute x6, starting transfers between devices, swap_bits(): return lax.ppermute(value, ('blk', 'dom'), pairs)  8.01 us
    all_to_all x1, starting transfers between devices, on_device(): lax.all_to_all(outgoing, 'dom', split_axis=0, concat_axis=0, tiled=True)  5.95 us
    ppermute x6, waiting for transfers between devices, swap_bits(): return lax.ppermute(value, ('blk', 'dom'), pairs)  5.48 us
    ppermute x8, starting transfers between devices, swap(): lax.ppermute(value, axis, [(i, i ^ bit) for i in range(lax.axis_size(axis...  5.01 us
    pallas_call x1, Pallas kernels, on_device(): call(functools.partial(adjacency_kernel, groups), [((rows, width), BF16),...  3.93 us
    ppermute x8, waiting for transfers between devices, swap(): lax.ppermute(value, axis, [(i, i ^ bit) for i in range(lax.axis_size(axis...  3.09 us
    pallas_call x1, Pallas kernels, on_device(): call(halo_kernel, [((peers, 2 * slots, width), BF16)], [HBM] * 6, 64 * MI...  2.25 us
    pallas_call x1, Pallas kernels, on_device(): call(backward_kernel, [((rows, width), BF16)], [SMEM] + [VMEM] * 6, 16 *...  1.7 us
  transfers between devices with their start and end apart: 15, of which 11 were waited for; matrix products, arithmetic and copies ran while one was open for 0% of the time, Pallas kernels for 23%

profile of v4, /device:TPU:0, one launch (start us, length us, event | category | flops | bytes accessed | tf_op | source)
XLA Modules:
  0.0 41.2 jit_solution(12878016398292213266)
XLA Ops:
  0.6 3.0 %collective-permute-start.1 = (bf16[512,256]{1,0:T(8,128)(2,1)}, bf16[512,256]{1,0:T(8,128)(2,1)}, u32[]{:S(2)}, u32[]{:S(2)}) collective-permute-start(bf16[512,256]{1,0:T(8,128)(2,1)} %bitcast.30), channel_id=1, source_target_pairs={{0,16},{8,24},{16,0},{24,8},{1,17},{9,25},{17,1},{25,9},{2,18},{10... | collective-permute-start | bytes 786440 | tf_op jit(solution)/shard_map/ppermute | solution.py:18
  3.7 2.2 %shard_map.121 = bf16[8,64,256]{2,1,0:T(8,128)(2,1)} custom-call(bf16[512,256]{1,0:T(8,128)(2,1)} %bitcast.31, bf16[512,256]{1,0:T(8,128)(2,1)} %bitcast.17, s32[8,32]{1,0:T(8,128)} %bitcast.26, s32[8]{0:T(128)} %bitcast.28, s32[8,32]{1,0:T(8,128)} %bitcast.20, f32[8,32]{1,0:T(8,128)} %bitcast.23), custom_call_target="tpu_custom_call" | custom-call | flops 1 | bytes 1 | tf_op jit(solution)/shard_map/pallas_call | solution.py:208
  5.9 0.0 copy-start.8
  5.9 5.9 %all-to-all-start = ((bf16[8,64,256]{2,1,0:T(8,128)(2,1)}), bf16[8,64,256]{2,1,0:T(8,128)(2,1)S(1)}, u32[]{:S(2)}, u32[]{:S(2)}) async-start(bf16[8,64,256]{2,1,0:T(8,128)(2,1)} %shard_map.121), calls=%async_computation | async-start | bytes 524288 | tf_op jit(solution)/shard_map/all_to_all | solution.py:224
  11.9 0.0 copy-done.8
  11.9 0.1 collective-permute-start
  12.0 0.0 collective-permute-done.1.refs_2_
  12.0 0.5 %collective-permute-start.2 = (bf16[512,256]{1,0:T(8,128)(2,1)}, bf16[512,256]{1,0:T(8,128)(2,1)S(1)}, u32[]{:S(2)}, u32[]{:S(2)}) collective-permute-start(bf16[512,256]{1,0:T(8,128)(2,1)} %collective-permute-done.1.refs_2_), channel_id=1, source_target_pairs={{0,8},{8,0},{16,24},{24,16},{1,9},{9,1},{17,25},{25,17},{2,10},{10... | collective-permute-start | bytes 786440 | tf_op jit(solution)/shard_map/ppermute | solution.py:18
  12.5 1.0 %collective-permute-done.refs_1_ = bf16[512,256]{1,0:T(8,128)(2,1)S(1)} collective-permute-done((bf16[512,256]{1,0:T(8,128)(2,1)S(1)}, bf16[512,256]{1,0:T(8,128)(2,1)S(1)}, u32[]{:S(2)}, u32[]{:S(2)}) %collective-permute-start) | collective-permute-done | bytes 262176 | tf_op jit(solution)/shard_map/ppermute | solution.py:18
  13.5 0.0 copy-start.10
  13.5 0.6 %collective-permute-done.2.refs_3_ = bf16[512,256]{1,0:T(8,128)(2,1)S(1)} collective-permute-done((bf16[512,256]{1,0:T(8,128)(2,1)}, bf16[512,256]{1,0:T(8,128)(2,1)S(1)}, u32[]{:S(2)}, u32[]{:S(2)}) %collective-permute-start.2) | collective-permute-done | bytes 262176 | tf_op jit(solution)/shard_map/ppermute | solution.py:18
  14.1 0.0 copy-start.11
  14.1 0.1 copy-done.10
  14.2 0.6 %copy-done.11 = bf16[512,256]{1,0:T(8,128)(2,1)} copy-done((bf16[512,256]{1,0:T(8,128)(2,1)}, bf16[512,256]{1,0:T(8,128)(2,1)S(1)}, u32[]{:S(2)}) %copy-start.11) | copy-done | bytes 262168
  14.8 0.0 copy-start
  14.8 0.0 copy-start.5
  14.8 3.9 %shard_map.122 = (bf16[512,256]{1,0:T(8,128)(2,1)}, bf16[128,256]{1,0:T(8,128)(2,1)}, bf16[128,256]{1,0:T(8,128)(2,1)}, bf16[2,256,512]{2,1,0:T(8,128)(2,1)}, bf...) custom-call(s32[1]{0:T(128)} %bitcast.blk, s32[4,6]{1,0:T(4,128)} %bitcast.37, s32[4]{0:T(128)} %bitcast.38, ...), custom_call_target="tpu_custom_call" | custom-call | flops 1 | bytes 1 | tf_op jit(solution)/shard_map/pallas_call | solution.py:234
  18.7 0.0 copy-start.13
  18.7 0.0 copy-start.9
  18.7 0.2 collective-permute-start.8
  19.0 1.6 %all-to-all-done.halo = bf16[8,64,256]{2,1,0:T(8,128)(2,1)S(1)} async-done(((bf16[8,64,256]{2,1,0:T(8,128)(2,1)}), bf16[8,64,256]{2,1,0:T(8,128)(2,1)S(1)}, u32[]{:S(2)}, u32[]{:S(2)}) %all-to-all-start) | async-done | bytes 262176 | tf_op jit(solution)/shard_map/all_to_all | solution.py:224
  20.5 0.0 copy-done
  20.5 0.0 copy-done.4
  20.5 0.0 copy-done.5
  20.5 0.6 %shard_map.123 = (bf16[128,256]{1,0:T(8,128)(2,1)S(1)}, bf16[128,256]{1,0:T(8,128)(2,1)S(1)}) custom-call(s32[1]{0:T(128)} %bitcast.blk, bf16[8,64,256]{2,1,0:T(8,128)(2,1)S(1)} %all-to-all-done.halo, s32[8,32]{1,0:T(8,128)S(1)} %bitcast.21, f32[8,32]{1,0:T(8,128)S(1)} %bitcast.24, bf16[512,256]{1,0:T(8,128)(2,1)S(1)} %bitcast.19), custom_call_target="tpu_custom_call" | custom-call | flops 20000000000 | bytes 1 | tf_op jit(solution)/shard_map/pallas_call | solution.py:260
  21.1 0.1 collective-permute-start.4
  21.2 0.0 copy-done.13
  21.2 0.5 %collective-permute-start.3 = (bf16[128,256]{1,0:T(8,128)(2,1)S(1)}, bf16[128,256]{1,0:T(8,128)(2,1)S(1)}, u32[]{:S(2)}, u32[]{:S(2)}) collective-permute-start(bf16[128,256]{1,0:T(8,128)(2,1)S(1)} %copy-done.13), channel_id=1, source_target_pairs={{0,8},{8,0},{16,24},{24,16},{1,9},{9,1},{17,25},{25,17},{2,10},{10... | collective-permute-start | bytes 196616 | tf_op jit(solution)/shard_map/ppermute | solution.py:18
  21.7 0.0 collective-permute-done.8.others
  21.7 0.0 copy-done.9
  21.7 0.0 copy-start.12
  21.7 0.0 copy-start.3
  21.7 0.1 fusion
  21.8 0.6 %collective-permute-start.9 = (bf16[256,512]{1,0:T(8,128)(2,1)S(1)}, bf16[256,512]{1,0:T(8,128)(2,1)S(1)}, u32[]{:S(2)}, u32[]{:S(2)}) collective-permute-start(bf16[256,512]{1,0:T(8,128)(2,1)S(1)} %fusion), channel_id=1, source_target_pairs={{0,16},{8,24},{16,0},{24,8},{1,17},{9,25},{17,1},{25,9},{2,18},{10... | collective-permute-start | bytes 786440 | tf_op jit(solution)/shard_map/ppermute | solution.py:18
  22.4 0.1 collective-permute-done.4
  22.5 0.2 collective-permute-done.3
  22.6 0.0 copy-done.12
  22.6 0.0 copy-start.1
  22.7 1.2 %collective-permute-start.5 = (bf16[128,256]{1,0:T(8,128)(2,1)S(1)}, bf16[128,256]{1,0:T(8,128)(2,1)S(1)}, u32[]{:S(2)}, u32[]{:S(2)}) collective-permute-start(bf16[128,256]{1,0:T(8,128)(2,1)S(1)} %add_convert_fusion.2), channel_id=1, source_target_pairs={{0,2},{1,3},{2,0},{3,1},{4,6},{5,7},{6,4},{7,5},{8,10},{9,11},{10,... | collective-permute-start | bytes 196616 | tf_op jit(solution)/shard_map/ppermute | solution.py:30
  23.8 1.8 %collective-permute-start.6 = (bf16[128,256]{1,0:T(8,128)(2,1)S(1)}, bf16[128,256]{1,0:T(8,128)(2,1)S(1)}, u32[]{:S(2)}, u32[]{:S(2)}) collective-permute-start(bf16[128,256]{1,0:T(8,128)(2,1)S(1)} %add_convert_fusion.2), channel_id=1, source_target_pairs={{0,3},{1,2},{2,1},{3,0},{4,7},{5,6},{6,5},{7,4},{8,11},{9,10},{10,... | collective-permute-start | bytes 196616 | tf_op jit(solution)/shard_map/ppermute | solution.py:30
  25.6 0.6 %collective-permute-start.7 = (bf16[128,256]{1,0:T(8,128)(2,1)S(1)}, bf16[128,256]{1,0:T(8,128)(2,1)S(1)}, u32[]{:S(2)}, u32[]{:S(2)}) collective-permute-start(bf16[128,256]{1,0:T(8,128)(2,1)S(1)} %add_convert_fusion.2), channel_id=1, source_target_pairs={{0,1},{1,0},{2,3},{3,2},{4,5},{5,4},{6,7},{7,6},{8,9},{9,8},{10,11... | collective-permute-start | bytes 196616 | tf_op jit(solution)/shard_map/ppermute | solution.py:30
  26.2 0.0 copy-done.3
  26.2 0.0 copy-done.1
  26.2 1.2 %shard_map.124 = bf16[512,256]{1,0:T(8,128)(2,1)} custom-call(bf16[512,256]{1,0:T(8,128)(2,1)S(1)} %copy-done.3, bf16[8,64,256]{2,1,0:T(8,128)(2,1)S(1)} %all-to-all-done.halo, s32[8,32]{1,0:T(8,128)S(1)} %bitcast.22, f32[8,32]{1,0:T(8,128)S(1)} %bitcast.25, bf16[256,256]{1,0:T(8,128)(2,1)S(1)} %copy-done.1), custom_call_target="tpu_custom_call" | custom-call | flops 1 | bytes 1 | tf_op jit(solution)/shard_map/pallas_call | solution.py:285
  27.4 0.0 copy-start.2
  27.4 0.0 collective-permute-done.5
  27.4 2.1 %collective-permute-done.6 = bf16[128,256]{1,0:T(8,128)(2,1)S(1)} collective-permute-done((bf16[128,256]{1,0:T(8,128)(2,1)S(1)}, bf16[128,256]{1,0:T(8,128)(2,1)S(1)}, u32[]{:S(2)}, u32[]{:S(2)}) %collective-permute-start.6) | collective-permute-done | bytes 65568 | tf_op jit(solution)/shard_map/ppermute | solution.py:30
  29.5 1.0 %collective-permute-done.7 = bf16[128,256]{1,0:T(8,128)(2,1)S(1)} collective-permute-done((bf16[128,256]{1,0:T(8,128)(2,1)S(1)}, bf16[128,256]{1,0:T(8,128)(2,1)S(1)}, u32[]{:S(2)}, u32[]{:S(2)}) %collective-permute-start.7) | collective-permute-done | bytes 65568 | tf_op jit(solution)/shard_map/ppermute | solution.py:30
  30.5 0.0 collective-permute-done.9.third
  30.5 0.0 copy-start.6
  30.6 0.0 copy-start.7
  30.6 2.0 %collective-permute-start.10 = (bf16[128,256]{1,0:T(8,128)(2,1)S(1)}, bf16[128,256]{1,0:T(8,128)(2,1)S(1)}, u32[]{:S(2)}, u32[]{:S(2)}) collective-permute-start(bf16[128,256]{1,0:T(8,128)(2,1)S(1)} %add_convert_fusion.1), channel_id=1, source_target_pairs={{0,4},{1,5},{2,6},{3,7},{4,0},{5,1},{6,2},{7,3},{8,12},{9,13},{10,... | collective-permute-start | bytes 196616 | tf_op jit(solution)/shard_map/ppermute | solution.py:30
  32.6 1.1 %collective-permute-start.11 = (bf16[128,256]{1,0:T(8,128)(2,1)S(1)}, bf16[128,256]{1,0:T(8,128)(2,1)S(1)}, u32[]{:S(2)}, u32[]{:S(2)}) collective-permute-start(bf16[128,256]{1,0:T(8,128)(2,1)S(1)} %add_convert_fusion.1), channel_id=1, source_target_pairs={{0,20},{1,21},{2,22},{3,23},{4,16},{5,17},{6,18},{7,19},{8,28},{9,... | collective-permute-start | bytes 196616 | tf_op jit(solution)/shard_map/ppermute | solution.py:30
  33.7 1.3 %collective-permute-start.12 = (bf16[128,256]{1,0:T(8,128)(2,1)S(1)}, bf16[128,256]{1,0:T(8,128)(2,1)S(1)}, u32[]{:S(2)}, u32[]{:S(2)}) collective-permute-start(bf16[128,256]{1,0:T(8,128)(2,1)S(1)} %add_convert_fusion.1), channel_id=1, source_target_pairs={{0,16},{1,17},{2,18},{3,19},{4,20},{5,21},{6,22},{7,23},{8,24},{9,... | collective-permute-start | bytes 196616 | tf_op jit(solution)/shard_map/ppermute | solution.py:30
  35.0 0.0 copy-done.2
  35.0 0.0 copy-done.6
  35.0 0.0 copy-done.7
  35.0 1.7 %shard_map.125 = bf16[512,256]{1,0:T(8,128)(2,1)} custom-call(s32[8]{0:T(128)S(1)} %bitcast.29, bf16[256,512]{1,0:T(8,128)(2,1)S(1)} %copy-done.2, bf16[2,256,512]{2,1,0:T(8,128)(2,1)S(1)} %collective-permute-done.8.others, bf16[256,512]{1,0:T(8,128)(2,1)S(1)} %collective-permute-done.9.third, bf16[8,64,256]{2,1,0:T(8,128)(2,1)S(1)} %all-to-all-done.halo, ...), custom_call_target="tpu_custom_call" | custom-call | flops 1 | bytes 1 | tf_op jit(solution)/shard_map/pallas_call | solution.py:289
  36.7 1.1 %collective-permute-done.10 = bf16[128,256]{1,0:T(8,128)(2,1)S(1)} collective-permute-done((bf16[128,256]{1,0:T(8,128)(2,1)S(1)}, bf16[128,256]{1,0:T(8,128)(2,1)S(1)}, u32[]{:S(2)}, u32[]{:S(2)}) %collective-permute-start.10) | collective-permute-done | bytes 65568 | tf_op jit(solution)/shard_map/ppermute | solution.py:30
  37.8 1.1 %collective-permute-done.11 = bf16[128,256]{1,0:T(8,128)(2,1)S(1)} collective-permute-done((bf16[128,256]{1,0:T(8,128)(2,1)S(1)}, bf16[128,256]{1,0:T(8,128)(2,1)S(1)}, u32[]{:S(2)}, u32[]{:S(2)}) %collective-permute-start.11) | collective-permute-done | bytes 65568 | tf_op jit(solution)/shard_map/ppermute | solution.py:30
  38.9 0.2 collective-permute-done.12
  39.1 0.1 collective-permute-start.13
  39.2 1.2 %collective-permute-done.13 = bf16[128,256]{1,0:T(8,128)(2,1)S(1)} collective-permute-done((bf16[128,256]{1,0:T(8,128)(2,1)S(1)}, bf16[128,256]{1,0:T(8,128)(2,1)S(1)}, u32[]{:S(2)}, u32[]{:S(2)}) %collective-permute-start.13) | collective-permute-done | bytes 65568 | tf_op jit(solution)/shard_map/ppermute | solution.py:18
  40.5 0.7 %convert_multiply_fusion = f32[256,256]{1,0:T(8,128)} fusion(bf16[128,256]{1,0:T(8,128)(2,1)S(1)} %get-tuple-element.48, bf16[128,256]{1,0:T(8,128)(2,1)S(1)} %get-tuple-element.47), kind=kLoop, calls=%fused_computation.3 | loop fusion | flops 327680 | bytes 393216 | tf_op jit(solution)/shard_map/mul | solution.py:308
  (5 shorter events, 0.1 us)
Async XLA Ops:
  0.6 11.3 %collective-permute-start.1 = (bf16[512,256]{1,0:T(8,128)(2,1)}, bf16[512,256]{1,0:T(8,128)(2,1)}, u32[]{:S(2)}, u32[]{:S(2)}) collective-permute-start(bf16[512,256]{1,0:T(8,128)(2,1)} %bitcast.30), channel_id=1, source_target_pairs={{0,16},{8,24},{16,0},{24,8},{1,17},{9,25},{17,1},{25,9},{2,18},{10... | collective-permute-start | bytes 786440 | tf_op jit(solution)/shard_map/ppermute | solution.py:18
  5.9 6.0 %copy-start.8 = (bf16[1,512,256]{2,1,0:T(8,128)(2,1)S(1)}, bf16[1,512,256]{2,1,0:T(8,128)(2,1)}, u32[]{:S(2)}) copy-start(bf16[1,512,256]{2,1,0:T(8,128)(2,1)} %param.10) | copy-start | bytes 786436
  5.9 14.6 %all-to-all-start = ((bf16[8,64,256]{2,1,0:T(8,128)(2,1)}), bf16[8,64,256]{2,1,0:T(8,128)(2,1)S(1)}, u32[]{:S(2)}, u32[]{:S(2)}) async-start(bf16[8,64,256]{2,1,0:T(8,128)(2,1)} %shard_map.121), calls=%async_computation | async-start | bytes 524288 | tf_op jit(solution)/shard_map/all_to_all | solution.py:224
  11.9 1.6 %collective-permute-start = (bf16[512,256]{1,0:T(8,128)(2,1)S(1)}, bf16[512,256]{1,0:T(8,128)(2,1)S(1)}, u32[]{:S(2)}, u32[]{:S(2)}) collective-permute-start(bf16[512,256]{1,0:T(8,128)(2,1)S(1)} %bitcast.33), channel_id=1, source_target_pairs={{0,8},{8,0},{16,24},{24,16},{1,9},{9,1},{17,25},{25,17},{2,10},{10... | collective-permute-start | bytes 786440 | tf_op jit(solution)/shard_map/ppermute | solution.py:18
  12.0 2.1 %collective-permute-start.2 = (bf16[512,256]{1,0:T(8,128)(2,1)}, bf16[512,256]{1,0:T(8,128)(2,1)S(1)}, u32[]{:S(2)}, u32[]{:S(2)}) collective-permute-start(bf16[512,256]{1,0:T(8,128)(2,1)} %collective-permute-done.1.refs_2_), channel_id=1, source_target_pairs={{0,8},{8,0},{16,24},{24,16},{1,9},{9,1},{17,25},{25,17},{2,10},{10... | collective-permute-start | bytes 786440 | tf_op jit(solution)/shard_map/ppermute | solution.py:18
  13.5 0.7 %copy-start.10 = (bf16[512,256]{1,0:T(8,128)(2,1)}, bf16[512,256]{1,0:T(8,128)(2,1)S(1)}, u32[]{:S(2)}) copy-start(bf16[512,256]{1,0:T(8,128)(2,1)S(1)} %collective-permute-done.refs_1_) | copy-start | bytes 786436
  14.1 0.7 %copy-start.11 = (bf16[512,256]{1,0:T(8,128)(2,1)}, bf16[512,256]{1,0:T(8,128)(2,1)S(1)}, u32[]{:S(2)}) copy-start(bf16[512,256]{1,0:T(8,128)(2,1)S(1)} %collective-permute-done.2.refs_3_) | copy-start | bytes 786436
  14.8 5.7 %copy-start = (bf16[1,512,256]{2,1,0:T(8,128)(2,1)S(1)}, bf16[1,512,256]{2,1,0:T(8,128)(2,1)}, u32[]{:S(2)}) copy-start(bf16[1,512,256]{2,1,0:T(8,128)(2,1)} %param.19) | copy-start | bytes 786436
  14.8 5.7 %copy-start.4 = (s32[1,1,8,32]{3,2,1,0:T(8,128)S(1)}, s32[1,1,8,32]{3,2,1,0:T(8,128)}, u32[]{:S(2)}) copy-start(s32[1,1,8,32]{3,2,1,0:T(8,128)} %param.17) | copy-start | bytes 3076
  14.8 5.7 %copy-start.5 = (f32[1,1,8,32]{3,2,1,0:T(8,128)S(1)}, f32[1,1,8,32]{3,2,1,0:T(8,128)}, u32[]{:S(2)}) copy-start(f32[1,1,8,32]{3,2,1,0:T(8,128)} %param.18) | copy-start | bytes 3076
  18.7 2.5 %copy-start.13 = (bf16[128,256]{1,0:T(8,128)(2,1)S(1)}, bf16[128,256]{1,0:T(8,128)(2,1)}, u32[]{:S(2)}) copy-start(bf16[128,256]{1,0:T(8,128)(2,1)} %get-tuple-element.28) | copy-start | bytes 196612
  18.7 3.0 %copy-start.9 = (bf16[256,512]{1,0:T(8,128)(2,1)S(1)}, bf16[256,512]{1,0:T(8,128)(2,1)}, u32[]{:S(2)}) copy-start(bf16[256,512]{1,0:T(8,128)(2,1)} %get-tuple-element.35) | copy-start | bytes 786436
  18.7 3.0 %collective-permute-start.8 = (bf16[2,256,512]{2,1,0:T(8,128)(2,1)}, bf16[2,256,512]{2,1,0:T(8,128)(2,1)S(1)}, u32[]{:S(2)}, u32[]{:S(2)}) collective-permute-start(bf16[2,256,512]{2,1,0:T(8,128)(2,1)} %get-tuple-element.36), channel_id=1, source_target_pairs={{0,8},{8,0},{16,24},{24,16},{1,9},{9,1},{17,25},{25,17},{2,10},{10... | collective-permute-start | bytes 1572872 | tf_op jit(solution)/shard_map/ppermute | solution.py:18
  21.1 1.3 %collective-permute-start.4 = (bf16[128,256]{1,0:T(8,128)(2,1)S(1)}, bf16[128,256]{1,0:T(8,128)(2,1)S(1)}, u32[]{:S(2)}, u32[]{:S(2)}) collective-permute-start(bf16[128,256]{1,0:T(8,128)(2,1)S(1)} %get-tuple-element.31), channel_id=1, source_target_pairs={{0,8},{8,0},{16,24},{24,16},{1,9},{9,1},{17,25},{25,17},{2,10},{10... | collective-permute-start | bytes 196616 | tf_op jit(solution)/shard_map/ppermute | solution.py:18
  21.2 1.4 %collective-permute-start.3 = (bf16[128,256]{1,0:T(8,128)(2,1)S(1)}, bf16[128,256]{1,0:T(8,128)(2,1)S(1)}, u32[]{:S(2)}, u32[]{:S(2)}) collective-permute-start(bf16[128,256]{1,0:T(8,128)(2,1)S(1)} %copy-done.13), channel_id=1, source_target_pairs={{0,8},{8,0},{16,24},{24,16},{1,9},{9,1},{17,25},{25,17},{2,10},{10... | collective-permute-start | bytes 196616 | tf_op jit(solution)/shard_map/ppermute | solution.py:18
  21.7 0.9 %copy-start.12 = (bf16[128,256]{1,0:T(8,128)(2,1)S(1)}, bf16[128,256]{1,0:T(8,128)(2,1)}, u32[]{:S(2)}) copy-start(bf16[128,256]{1,0:T(8,128)(2,1)} %get-tuple-element.27) | copy-start | bytes 196612
  21.7 4.5 %copy-start.3 = (bf16[512,256]{1,0:T(8,128)(2,1)S(1)}, bf16[512,256]{1,0:T(8,128)(2,1)}, u32[]{:S(2)}) copy-start(bf16[512,256]{1,0:T(8,128)(2,1)} %get-tuple-element.34.local) | copy-start | bytes 786436
  21.8 8.7 %collective-permute-start.9 = (bf16[256,512]{1,0:T(8,128)(2,1)S(1)}, bf16[256,512]{1,0:T(8,128)(2,1)S(1)}, u32[]{:S(2)}, u32[]{:S(2)}) collective-permute-start(bf16[256,512]{1,0:T(8,128)(2,1)S(1)} %fusion), channel_id=1, source_target_pairs={{0,16},{8,24},{16,0},{24,8},{1,17},{9,25},{17,1},{25,9},{2,18},{10... | collective-permute-start | bytes 786440 | tf_op jit(solution)/shard_map/ppermute | solution.py:18
  22.6 3.6 %copy-start.1 = (bf16[256,256]{1,0:T(8,128)(2,1)S(1)}, bf16[256,256]{1,0:T(8,128)(2,1)}, u32[]{:S(2)}) copy-start(bf16[256,256]{1,0:T(8,128)(2,1)} %weight.3) | copy-start | bytes 393220
  22.7 4.7 %collective-permute-start.5 = (bf16[128,256]{1,0:T(8,128)(2,1)S(1)}, bf16[128,256]{1,0:T(8,128)(2,1)S(1)}, u32[]{:S(2)}, u32[]{:S(2)}) collective-permute-start(bf16[128,256]{1,0:T(8,128)(2,1)S(1)} %add_convert_fusion.2), channel_id=1, source_target_pairs={{0,2},{1,3},{2,0},{3,1},{4,6},{5,7},{6,4},{7,5},{8,10},{9,11},{10,... | collective-permute-start | bytes 196616 | tf_op jit(solution)/shard_map/ppermute | solution.py:30
  23.8 5.6 %collective-permute-start.6 = (bf16[128,256]{1,0:T(8,128)(2,1)S(1)}, bf16[128,256]{1,0:T(8,128)(2,1)S(1)}, u32[]{:S(2)}, u32[]{:S(2)}) collective-permute-start(bf16[128,256]{1,0:T(8,128)(2,1)S(1)} %add_convert_fusion.2), channel_id=1, source_target_pairs={{0,3},{1,2},{2,1},{3,0},{4,7},{5,6},{6,5},{7,4},{8,11},{9,10},{10,... | collective-permute-start | bytes 196616 | tf_op jit(solution)/shard_map/ppermute | solution.py:30
  25.6 4.9 %collective-permute-start.7 = (bf16[128,256]{1,0:T(8,128)(2,1)S(1)}, bf16[128,256]{1,0:T(8,128)(2,1)S(1)}, u32[]{:S(2)}, u32[]{:S(2)}) collective-permute-start(bf16[128,256]{1,0:T(8,128)(2,1)S(1)} %add_convert_fusion.2), channel_id=1, source_target_pairs={{0,1},{1,0},{2,3},{3,2},{4,5},{5,4},{6,7},{7,6},{8,9},{9,8},{10,11... | collective-permute-start | bytes 196616 | tf_op jit(solution)/shard_map/ppermute | solution.py:30
  27.4 7.7 %copy-start.2 = (bf16[256,512]{1,0:T(8,128)(2,1)S(1)}, bf16[256,512]{1,0:T(8,128)(2,1)}, u32[]{:S(2)}) copy-start(bf16[256,512]{1,0:T(8,128)(2,1)} %get-tuple-element.41.first) | copy-start | bytes 786436
  30.5 4.5 %copy-start.6 = (s32[1,1,8,32]{3,2,1,0:T(8,128)S(1)}, s32[1,1,8,32]{3,2,1,0:T(8,128)}, u32[]{:S(2)}) copy-start(s32[1,1,8,32]{3,2,1,0:T(8,128)} %param.15) | copy-start | bytes 3076
  30.6 4.5 %copy-start.7 = (s32[1,1,8]{2,1,0:T(1,128)S(1)}, s32[1,1,8]{2,1,0:T(1,128)}, u32[]{:S(2)}) copy-start(s32[1,1,8]{2,1,0:T(1,128)} %param.16) | copy-start | bytes 100
  30.6 7.2 %collective-permute-start.10 = (bf16[128,256]{1,0:T(8,128)(2,1)S(1)}, bf16[128,256]{1,0:T(8,128)(2,1)S(1)}, u32[]{:S(2)}, u32[]{:S(2)}) collective-permute-start(bf16[128,256]{1,0:T(8,128)(2,1)S(1)} %add_convert_fusion.1), channel_id=1, source_target_pairs={{0,4},{1,5},{2,6},{3,7},{4,0},{5,1},{6,2},{7,3},{8,12},{9,13},{10,... | collective-permute-start | bytes 196616 | tf_op jit(solution)/shard_map/ppermute | solution.py:30
  32.6 6.3 %collective-permute-start.11 = (bf16[128,256]{1,0:T(8,128)(2,1)S(1)}, bf16[128,256]{1,0:T(8,128)(2,1)S(1)}, u32[]{:S(2)}, u32[]{:S(2)}) collective-permute-start(bf16[128,256]{1,0:T(8,128)(2,1)S(1)} %add_convert_fusion.1), channel_id=1, source_target_pairs={{0,20},{1,21},{2,22},{3,23},{4,16},{5,17},{6,18},{7,19},{8,28},{9,... | collective-permute-start | bytes 196616 | tf_op jit(solution)/shard_map/ppermute | solution.py:30
  33.7 5.4 %collective-permute-start.12 = (bf16[128,256]{1,0:T(8,128)(2,1)S(1)}, bf16[128,256]{1,0:T(8,128)(2,1)S(1)}, u32[]{:S(2)}, u32[]{:S(2)}) collective-permute-start(bf16[128,256]{1,0:T(8,128)(2,1)S(1)} %add_convert_fusion.1), channel_id=1, source_target_pairs={{0,16},{1,17},{2,18},{3,19},{4,20},{5,21},{6,22},{7,23},{8,24},{9,... | collective-permute-start | bytes 196616 | tf_op jit(solution)/shard_map/ppermute | solution.py:30
  39.1 1.3 %collective-permute-start.13 = (bf16[128,256]{1,0:T(8,128)(2,1)S(1)}, bf16[128,256]{1,0:T(8,128)(2,1)S(1)}, u32[]{:S(2)}, u32[]{:S(2)}) collective-permute-start(bf16[128,256]{1,0:T(8,128)(2,1)S(1)} %add_convert_fusion), channel_id=1, source_target_pairs={{0,8},{8,0},{16,24},{24,16},{1,9},{9,1},{17,25},{25,17},{2,10},{10... | collective-permute-start | bytes 196616 | tf_op jit(solution)/shard_map/ppermute | solution.py:18

commit v5 on v4

--- a/solution.py
+++ b/solution.py
@@ -18,15 +18,14 @@
     return lax.ppermute(value, axis, [(i, i ^ bit) for i in range(lax.axis_size(axis))])
 
 
-def swap_bits(value, bits):
+def swap_bits(value, even, odd):
     groups, peers = lax.axis_size("blk"), lax.axis_size("dom")
-    b_bits = sum(bit for axis, bit in bits if axis == "blk")
-    d_bits = sum(bit for axis, bit in bits if axis == "dom")
-    pairs = [
-        (b * peers + d, (b ^ b_bits) * peers + (d ^ d_bits))
-        for b in range(groups)
-        for d in range(peers)
-    ]
+    pairs = []
+    for b in range(groups):
+        bits = odd if b % 2 else even
+        b_bits = sum(bit for axis, bit in bits if axis == "blk")
+        d_bits = sum(bit for axis, bit in bits if axis == "dom")
+        pairs += [(b * peers + d, (b ^ b_bits) * peers + (d ^ d_bits)) for d in range(peers)]
     return lax.ppermute(value, ("blk", "dom"), pairs)
 
 
@@ -87,34 +86,18 @@
     sent[...] = term[pl.ds(pl.multiple_of((1 - core) * half, half), half), :].astype(BF16)
 
 
-def adjacency_kernel(groups, blk, pos_in, count_in, tiles_in, grad_in, *refs):
-    panels_in, refs = refs[:groups], refs[groups:]
-    (local, kept, sent, send, *keep), refs = refs[: 4 + groups // 2], refs[4 + groups // 2 :]
-    dense, term, sems, *homes = refs
-    pos, count, tiles, grad, *panels = homes
+def adjacency_kernel(groups, blk, spots, tiles, grad, *refs):
+    panels, refs = refs[:groups], refs[groups:]
+    (local, kept, sent, send, *keep), (dense, term) = refs[:-2], refs[-2:]
     unused, slots, tile, unused = tiles.shape
     rows, width = grad.shape
-    per = rows // tile
-    order = [blk[0] ^ j for j in range(groups)]
-    few = fetch([(pos_in, pos), (count_in, count), (grad_in, grad)], sems)
-    blocks = fetch([(tiles_in, tiles)], sems.at[pl.ds(3, 1)])
-    others = fetch(list(zip(panels_in, panels)), sems.at[pl.ds(4, groups)])
     dense[...] = jnp.zeros_like(dense)
-    for copy in few:
-        copy.wait()
-    for copy in blocks:
-        copy.wait()
-    for j, c in enumerate(order):
+    for j in range(groups):
+        c = blk[0] ^ j
         for t in range(slots):
-            spot = pos[c, t]
-            row = pl.multiple_of((spot // per) * tile, tile)
-            column = pl.multiple_of(j * rows + (spot % per) * tile, tile)
-            live = t < count[c]
-            dense[pl.ds(row, tile), pl.ds(column, tile)] = jnp.where(
-                live, tiles[c, t], jnp.zeros((), BF16)
-            )
-    for copy in others:
-        copy.wait()
+            row = pl.multiple_of(spots[0, c, t], tile)
+            column = pl.multiple_of(j * rows + spots[1, c, t], tile)
+            dense[pl.ds(row, tile), pl.ds(column, tile)] = tiles[c, t]
     turned = grad[...].T
     for j in range(groups):
         part = matmul(turned, dense[:, j * rows : (j + 1) * rows], 1, 0).astype(BF16)
@@ -220,40 +203,32 @@
             pltpu.SemaphoreType.DMA((6,)),
         ],
     )(feats, grad, sends, send_live, owner, edge)
-    outgoing, near, tile_set = lax.optimization_barrier((outgoing, feats, tiles[0, 0]))
+    outgoing, near, tile_set, place = lax.optimization_barrier(
+        (outgoing, feats, tiles[0, 0], tile_pos[0, 0])
+    )
     halo = lax.all_to_all(outgoing, "dom", split_axis=0, concat_axis=0, tiled=True)
 
+    near, feats_far = lax.optimization_barrier((near, feats_far))
     panels = {0: near, groups // 2: feats_far}
     for bit in reversed(bits_of(groups // 2)):
         for j in list(panels):
             panels[j ^ bit] = swap(panels[j], "blk", bit)
 
     half = groups // 2
-    panel = pltpu.VMEM((rows, width), BF16)
     half_term = ((width // 2, width), BF16)
+    tile = tiles.shape[-1]
+    per = rows // tile
+    live = jnp.arange(tiles.shape[3])[None, :] < tile_count[0, 0][:, None]
+    live_tiles = jnp.where(live[..., None, None], tile_set, jnp.zeros((), BF16))
+    spots = jnp.stack([place // per, place % per]) * tile
     local, kept, sent, send, *keep = call(
         functools.partial(adjacency_kernel, groups),
         [((rows, width), BF16), half_term, half_term, ((half, width, rows), BF16)]
         + [((width, rows), BF16)] * half,
-        [SMEM] + [HBM] * (4 + groups),
-        61 * MIB,
-        [
-            pltpu.VMEM((rows, groups * rows), BF16),
-            pltpu.VMEM((width, width), F32),
-            pltpu.SemaphoreType.DMA((4 + groups,)),
-            pltpu.SMEM(tile_pos.shape[2:], jnp.int32),
-            pltpu.SMEM(tile_count.shape[2:], jnp.int32),
-            pltpu.VMEM(tiles.shape[2:], BF16),
-        ]
-        + [panel] * (1 + groups),
-    )(
-        blk,
-        tile_pos[0, 0],
-        tile_count[0, 0],
-        tile_set,
-        grad,
-        *[panels[j] for j in range(groups)],
-    )
+        [SMEM] * 2 + [VMEM] * (2 + groups),
+        40 * MIB,
+        [pltpu.VMEM((rows, groups * rows), BF16), pltpu.VMEM((width, width), F32)],
+    )(blk, spots, live_tiles, grad, *[panels[j] for j in range(groups)])
     got = swap(send, "blk", 1)
 
     near_term = (kept, swap(sent, "blk", 1))
@@ -269,6 +244,8 @@
     inner = bits_of(groups)[1:]
     for bit in inner:
         later = [add(keep[j], got[j]) for j in range(1, len(keep), 2)]
+        if bit == inner[0]:
+            other, later[0] = lax.optimization_barrier((other, later[0]))
         if len(keep) == 2:
             third = swap(later[0], "blk", bit)
         else:
@@ -282,17 +259,18 @@
         first, last = i == 0, i == len(fours) - 1
         if first:
             term, local = lax.optimization_barrier((term, local))
-            (layer_out,) = call(output_kernel, [((rows, width), BF16)], [VMEM] * 5, 16 * MIB)(
-                local, halo, owner, edge, weight
-            )
+            (layer_out,) = call(
+                output_kernel, [((rows, width), BF16)], [VMEM] * 5, 16 * MIB, flops=2 * 10**10
+            )(local, halo, owner, edge, weight)
         if last:
             (feature_grad,) = call(
                 backward_kernel, [((rows, width), BF16)], [SMEM] + [VMEM] * 6, 16 * MIB
             )(send_live, keep[0], got, third, halo, sends, weight)
-        ways = [four[1:], four, four[:1]] if len(four) == 2 else [four]
-        others = [swap_bits(term, way) for way in ways]
+        mate = fours[i ^ 1] if i ^ 1 < len(fours) and len(fours[i ^ 1]) == len(four) else four
+        ways = [slice(1, 2), slice(0, 2), slice(0, 1)] if len(four) == 2 else [slice(0, 1)]
+        others = [swap_bits(term, four[way], mate[way]) for way in ways]
         if first:
-            others, layer_out, third = lax.optimization_barrier((others, layer_out, third))
+            others, layer_out = lax.optimization_barrier((others, layer_out))
         if last:
             others, feature_grad = lax.optimization_barrier((others, feature_grad))
         others = others[-1:] + others[:-1]

time: 41.5 us -> 40.1 us (0.966)
  waiting for transfers between devices: 10.1 us -> 8.53 us
  other arithmetic: 0.91 us -> 2.26 us
  Pallas kernels: 9.63 us -> 8.6 us
    ppermute x6, waiting for transfers between devices: 5.48 us -> 3.46 us  [swap_bits(): return lax.ppermute(value, ('blk', 'dom'), pairs)]
    select_n x0 -> x1, other arithmetic: none -> 1.25 us  [on_device(): live_tiles = jnp.where(live[..., None, None], tile_set, jnp.zeros((), BF16))]
    pallas_call x1, Pallas kernels: 3.93 us -> 2.93 us  [on_device(): call(functools.partial(adjacency_kernel, groups), [((rows, width), BF16),...]
    all_to_all x1, waiting for transfers between devices: 1.56 us -> 2.52 us  [on_device(): lax.all_to_all(outgoing, 'dom', split_axis=0, concat_axis=0, tiled=True)]
    ppermute x8, waiting for transfers between devices: 3.09 us -> 2.55 us  [swap(): lax.ppermute(value, axis, [(i, i ^ bit) for i in range(lax.axis_size(axis...]
  transfers between devices with their start and end apart: 15 -> 15, of which waited for: 11 -> 11; matrix products, arithmetic and copies ran while one was open for 0% -> 4% of each run, Pallas kernels for 23% -> 22%
where the time goes in v5:
time: 40.1 us; the launch traced here: 39.8 us
  starting transfers between devices  18.9 us (47%)
  Pallas kernels  8.6 us (21%)
  waiting for transfers between devices  8.53 us (21%)
  other arithmetic  2.26 us (6%)
  between operations  0.79 us (2%)
  local copies, waits for them, and re-layouts  0.69 us (2%)
    ppermute x6, starting transfers between devices, swap_bits(): return lax.ppermute(value, ('blk', 'dom'), pairs)  8.01 us
    all_to_all x1, starting transfers between devices, on_device(): lax.all_to_all(outgoing, 'dom', split_axis=0, concat_axis=0, tiled=True)  5.95 us
    ppermute x8, starting transfers between devices, swap(): lax.ppermute(value, axis, [(i, i ^ bit) for i in range(lax.axis_size(axis...  4.95 us
    ppermute x6, waiting for transfers between devices, swap_bits(): return lax.ppermute(value, ('blk', 'dom'), pairs)  3.46 us
    pallas_call x1, Pallas kernels, on_device(): call(functools.partial(adjacency_kernel, groups), [((rows, width), BF16),...  2.93 us
    ppermute x8, waiting for transfers between devices, swap(): lax.ppermute(value, axis, [(i, i ^ bit) for i in range(lax.axis_size(axis...  2.55 us
    all_to_all x1, waiting for transfers between devices, on_device(): lax.all_to_all(outgoing, 'dom', split_axis=0, concat_axis=0, tiled=True)  2.52 us
    pallas_call x1, Pallas kernels, on_device(): call(halo_kernel, [((peers, 2 * slots, width), BF16)], [HBM] * 6, 64 * MI...  2.23 us
  transfers between devices with their start and end apart: 15, of which 11 were waited for; matrix products, arithmetic and copies ran while one was open for 4% of the time, Pallas kernels for 22%

profile of v5, /device:TPU:0, one launch (start us, length us, event | category | flops | bytes accessed | tf_op | source)
XLA Modules:
  0.0 39.8 jit_solution(10791871686687309096)
XLA Ops:
  0.6 3.0 %collective-permute-start = (bf16[512,256]{1,0:T(8,128)(2,1)}, bf16[512,256]{1,0:T(8,128)(2,1)}, u32[]{:S(2)}, u32[]{:S(2)}) collective-permute-start(bf16[512,256]{1,0:T(8,128)(2,1)} %bitcast.21), channel_id=1, source_target_pairs={{0,16},{8,24},{16,0},{24,8},{1,17},{9,25},{17,1},{25,9},{2,18},{10... | collective-permute-start | bytes 786440 | tf_op jit(solution)/shard_map/ppermute | solution.py:18
  3.7 2.2 %shard_map.121 = bf16[8,64,256]{2,1,0:T(8,128)(2,1)} custom-call(bf16[512,256]{1,0:T(8,128)(2,1)} %bitcast.22, bf16[512,256]{1,0:T(8,128)(2,1)} %bitcast.25, s32[8,32]{1,0:T(8,128)} %bitcast.28, s32[8]{0:T(128)} %bitcast.36, s32[8,32]{1,0:T(8,128)} %bitcast.30, f32[8,32]{1,0:T(8,128)} %bitcast.33), custom_call_target="tpu_custom_call" | custom-call | flops 1 | bytes 1 | tf_op jit(solution)/shard_map/pallas_call | solution.py:191
  5.9 0.0 copy-start.7
  5.9 0.0 copy-start
  5.9 5.9 %all-to-all-start = ((bf16[8,64,256]{2,1,0:T(8,128)(2,1)}), bf16[8,64,256]{2,1,0:T(8,128)(2,1)S(1)}, u32[]{:S(2)}, u32[]{:S(2)}) async-start(bf16[8,64,256]{2,1,0:T(8,128)(2,1)} %shard_map.121), calls=%async_computation | async-start | bytes 524288 | tf_op jit(solution)/shard_map/all_to_all | solution.py:209
  11.9 0.0 copy-done.7
  11.9 0.0 copy-start.8
  11.9 0.6 %copy-done.8 = s32[1,1,4]{2,1,0:T(1,128)S(1)} copy-done((s32[1,1,4]{2,1,0:T(1,128)S(1)}, s32[1,1,4]{2,1,0:T(1,128)}, u32[]{:S(2)}) %copy-start.8) | copy-done | bytes 40
  12.6 0.1 iota_compare_fusion
  12.6 0.0 copy-start.1
  12.6 0.0 collective-permute-done.refs_2_
  12.6 0.0 copy-done
  12.7 0.1 collective-permute-start.1
  12.7 0.5 %collective-permute-start.2 = (bf16[512,256]{1,0:T(8,128)(2,1)}, bf16[512,256]{1,0:T(8,128)(2,1)S(1)}, u32[]{:S(2)}, u32[]{:S(2)}) collective-permute-start(bf16[512,256]{1,0:T(8,128)(2,1)} %collective-permute-done.refs_2_), channel_id=1, source_target_pairs={{0,8},{8,0},{16,24},{24,16},{1,9},{9,1},{17,25},{25,17},{2,10},{10... | collective-permute-start | bytes 786440 | tf_op jit(solution)/shard_map/ppermute | solution.py:18
  13.2 1.3 %broadcast_select_fusion.tiles = bf16[4,6,128,128]{3,2,1,0:T(8,128)(2,1)S(1)} fusion(bf16[4,6,128,128]{3,2,1,0:T(8,128)(2,1)} %bitcast.38, pred[4,6]{1,0:T(4,128)(4,1)S(1)} %iota_compare_fusion), kind=kLoop, calls=%fused_computation | loop fusion | flops 393216 | bytes 1572888 | tf_op jit(solution)/shard_map/jit(_where)/select_n | solution.py:222
  14.5 0.0 collective-permute-done.1.refs_1_
  14.5 0.3 collective-permute-done.2.refs_3_
  14.8 0.0 copy-done.1
  14.8 0.0 copy-start.4
  14.8 0.0 copy-start.5
  14.8 2.9 %shard_map.122 = (bf16[512,256]{1,0:T(8,128)(2,1)S(1)}, bf16[128,256]{1,0:T(8,128)(2,1)S(1)}, bf16[128,256]{1,0:T(8,128)(2,1)S(1)}, bf16[2,256,512]{2,1,0:T(8,12...) custom-call(s32[1]{0:T(128)} %bitcast.blk, s32[2,4,6]{2,1,0:T(4,128)S(1)} %add_multiply_fusion.spots, ...), custom_call_target="tpu_custom_call" | custom-call | flops 1 | bytes 1 | tf_op jit(solution)/shard_map/pallas_call | solution.py:224
  17.8 0.2 collective-permute-start.5
  18.0 2.5 %all-to-all-done.halo = bf16[8,64,256]{2,1,0:T(8,128)(2,1)S(1)} async-done(((bf16[8,64,256]{2,1,0:T(8,128)(2,1)}), bf16[8,64,256]{2,1,0:T(8,128)(2,1)S(1)}, u32[]{:S(2)}, u32[]{:S(2)}) %all-to-all-start) | async-done | bytes 262176 | tf_op jit(solution)/shard_map/all_to_all | solution.py:209
  20.5 0.0 copy-done.4
  20.5 0.0 copy-done.5
  20.5 0.6 %shard_map.123 = (bf16[128,256]{1,0:T(8,128)(2,1)S(1)}, bf16[128,256]{1,0:T(8,128)(2,1)S(1)}) custom-call(s32[1]{0:T(128)} %bitcast.blk, bf16[8,64,256]{2,1,0:T(8,128)(2,1)S(1)} %all-to-all-done.halo, s32[8,32]{1,0:T(8,128)S(1)} %bitcast.31, f32[8,32]{1,0:T(8,128)S(1)} %bitcast.34, bf16[512,256]{1,0:T(8,128)(2,1)S(1)} %bitcast.27), custom_call_target="tpu_custom_call" | custom-call | flops 20000000000 | bytes 1 | tf_op jit(solution)/shard_map/pallas_call | solution.py:235
  21.1 0.1 collective-permute-start.4
  21.2 0.5 %collective-permute-start.3 = (bf16[128,256]{1,0:T(8,128)(2,1)S(1)}, bf16[128,256]{1,0:T(8,128)(2,1)S(1)}, u32[]{:S(2)}, u32[]{:S(2)}) collective-permute-start(bf16[128,256]{1,0:T(8,128)(2,1)S(1)} %get-tuple-element.35), channel_id=1, source_target_pairs={{0,8},{8,0},{16,24},{24,16},{1,9},{9,1},{17,25},{25,17},{2,10},{10... | collective-permute-start | bytes 196616 | tf_op jit(solution)/shard_map/ppermute | solution.py:18
  21.7 0.0 collective-permute-done.5.others
  21.7 0.1 fusion
  21.8 0.7 %collective-permute-done.4 = bf16[128,256]{1,0:T(8,128)(2,1)S(1)} collective-permute-done((bf16[128,256]{1,0:T(8,128)(2,1)S(1)}, bf16[128,256]{1,0:T(8,128)(2,1)S(1)}, u32[]{:S(2)}, u32[]{:S(2)}) %collective-permute-start.4) | collective-permute-done | bytes 65568 | tf_op jit(solution)/shard_map/ppermute | solution.py:18
  22.4 0.2 collective-permute-done.3
  22.6 0.0 copy-start.2
  22.6 1.2 %collective-permute-start.6 = (bf16[128,256]{1,0:T(8,128)(2,1)S(1)}, bf16[128,256]{1,0:T(8,128)(2,1)S(1)}, u32[]{:S(2)}, u32[]{:S(2)}) collective-permute-start(bf16[128,256]{1,0:T(8,128)(2,1)S(1)} %add_convert_fusion.2), channel_id=1, source_target_pairs={{0,2},{1,3},{2,0},{3,1},{4,6},{5,7},{6,4},{7,5},{8,12},{9,13},{10,... | collective-permute-start | bytes 196616 | tf_op jit(solution)/shard_map/ppermute | solution.py:29
  23.8 1.8 %collective-permute-start.7 = (bf16[128,256]{1,0:T(8,128)(2,1)S(1)}, bf16[128,256]{1,0:T(8,128)(2,1)S(1)}, u32[]{:S(2)}, u32[]{:S(2)}) collective-permute-start(bf16[128,256]{1,0:T(8,128)(2,1)S(1)} %add_convert_fusion.2), channel_id=1, source_target_pairs={{0,3},{1,2},{2,1},{3,0},{4,7},{5,6},{6,5},{7,4},{8,28},{9,29},{10,... | collective-permute-start | bytes 196616 | tf_op jit(solution)/shard_map/ppermute | solution.py:29
  25.6 0.6 %collective-permute-start.8 = (bf16[128,256]{1,0:T(8,128)(2,1)S(1)}, bf16[128,256]{1,0:T(8,128)(2,1)S(1)}, u32[]{:S(2)}, u32[]{:S(2)}) collective-permute-start(bf16[128,256]{1,0:T(8,128)(2,1)S(1)} %add_convert_fusion.2), channel_id=1, source_target_pairs={{0,1},{1,0},{2,3},{3,2},{4,5},{5,4},{6,7},{7,6},{8,24},{9,25},{10,... | collective-permute-start | bytes 196616 | tf_op jit(solution)/shard_map/ppermute | solution.py:29
  26.2 0.5 %collective-permute-start.12 = (bf16[256,512]{1,0:T(8,128)(2,1)S(1)}, bf16[256,512]{1,0:T(8,128)(2,1)S(1)}, u32[]{:S(2)}, u32[]{:S(2)}) collective-permute-start(bf16[256,512]{1,0:T(8,128)(2,1)S(1)} %fusion), channel_id=1, source_target_pairs={{0,16},{8,24},{16,0},{24,8},{1,17},{9,25},{17,1},{25,9},{2,18},{10... | collective-permute-start | bytes 786440 | tf_op jit(solution)/shard_map/ppermute | solution.py:18
  26.7 0.0 copy-done.2
  26.7 1.2 %shard_map.124 = bf16[512,256]{1,0:T(8,128)(2,1)} custom-call(bf16[512,256]{1,0:T(8,128)(2,1)S(1)} %get-tuple-element.44.local, bf16[8,64,256]{2,1,0:T(8,128)(2,1)S(1)} %all-to-all-done.halo, s32[8,32]{1,0:T(8,128)S(1)} %bitcast.32, f32[8,32]{1,0:T(8,128)S(1)} %bitcast.35, bf16[256,256]{1,0:T(8,128)(2,1)S(1)} %copy-done.2), custom_call_target="tpu_custom_call" | custom-call | flops 20000000000 | bytes 1 | tf_op jit(solution)/shard_map/pallas_call | solution.py:262
  27.9 0.1 collective-permute-done.6
  28.0 2.1 %collective-permute-done.7 = bf16[128,256]{1,0:T(8,128)(2,1)S(1)} collective-permute-done((bf16[128,256]{1,0:T(8,128)(2,1)S(1)}, bf16[128,256]{1,0:T(8,128)(2,1)S(1)}, u32[]{:S(2)}, u32[]{:S(2)}) %collective-permute-start.7) | collective-permute-done | bytes 65568 | tf_op jit(solution)/shard_map/ppermute | solution.py:29
  30.1 0.3 collective-permute-done.8
  30.3 0.0 copy-start.3
  30.4 0.0 copy-start.6
  30.4 0.3 collective-permute-start.10
  30.7 1.8 %collective-permute-start.11 = (bf16[128,256]{1,0:T(8,128)(2,1)S(1)}, bf16[128,256]{1,0:T(8,128)(2,1)S(1)}, u32[]{:S(2)}, u32[]{:S(2)}) collective-permute-start(bf16[128,256]{1,0:T(8,128)(2,1)S(1)} %add_convert_fusion.1), channel_id=1, source_target_pairs={{0,16},{1,17},{2,18},{3,19},{4,20},{5,21},{6,22},{7,23},{8,9},{9,8... | collective-permute-start | bytes 196616 | tf_op jit(solution)/shard_map/ppermute | solution.py:29
  32.5 2.3 %collective-permute-start.9 = (bf16[128,256]{1,0:T(8,128)(2,1)S(1)}, bf16[128,256]{1,0:T(8,128)(2,1)S(1)}, u32[]{:S(2)}, u32[]{:S(2)}) collective-permute-start(bf16[128,256]{1,0:T(8,128)(2,1)S(1)} %add_convert_fusion.1), channel_id=1, source_target_pairs={{0,4},{1,5},{2,6},{3,7},{4,0},{5,1},{6,2},{7,3},{8,10},{9,11},{10,... | collective-permute-start | bytes 196616 | tf_op jit(solution)/shard_map/ppermute | solution.py:29
  34.8 0.1 collective-permute-done.12.third
  35.0 0.0 copy-done.3
  35.0 0.0 copy-done.6
  35.0 1.7 %shard_map.125 = bf16[512,256]{1,0:T(8,128)(2,1)} custom-call(s32[8]{0:T(128)S(1)} %bitcast.37, bf16[256,512]{1,0:T(8,128)(2,1)S(1)} %get-tuple-element.49.first, bf16[2,256,512]{2,1,0:T(8,128)(2,1)S(1)} %collective-permute-done.5.others, bf16[256,512]{1,0:T(8,128)(2,1)S(1)} %collective-permute-done.12.third, bf16[8,64,256]{2,1,0:T(8,128)(2,1)S(1)} %all-to-all-done.halo, ...), custom_call_target="tpu_custom_call" | custom-call | flops 1 | bytes 1 | tf_op jit(solution)/shard_map/pallas_call | solution.py:266
  36.7 0.4 collective-permute-done.10
  37.1 0.0 collective-permute-done.11
  37.1 0.6 %collective-permute-done.9 = bf16[128,256]{1,0:T(8,128)(2,1)S(1)} collective-permute-done((bf16[128,256]{1,0:T(8,128)(2,1)S(1)}, bf16[128,256]{1,0:T(8,128)(2,1)S(1)}, u32[]{:S(2)}, u32[]{:S(2)}) %collective-permute-start.9) | collective-permute-done | bytes 65568 | tf_op jit(solution)/shard_map/ppermute | solution.py:29
  37.7 0.1 collective-permute-start.13
  37.8 1.2 %collective-permute-done.13 = bf16[128,256]{1,0:T(8,128)(2,1)S(1)} collective-permute-done((bf16[128,256]{1,0:T(8,128)(2,1)S(1)}, bf16[128,256]{1,0:T(8,128)(2,1)S(1)}, u32[]{:S(2)}, u32[]{:S(2)}) %collective-permute-start.13) | collective-permute-done | bytes 65568 | tf_op jit(solution)/shard_map/ppermute | solution.py:18
  39.1 0.7 %convert_multiply_fusion = f32[256,256]{1,0:T(8,128)} fusion(bf16[128,256]{1,0:T(8,128)(2,1)S(1)} %get-tuple-element.56, bf16[128,256]{1,0:T(8,128)(2,1)S(1)} %get-tuple-element.55), kind=kLoop, calls=%fused_computation.4 | loop fusion | flops 327680 | bytes 393216 | tf_op jit(solution)/shard_map/mul | solution.py:286
  (6 shorter events, 0.1 us)
Async XLA Ops:
  0.6 12.0 %collective-permute-start = (bf16[512,256]{1,0:T(8,128)(2,1)}, bf16[512,256]{1,0:T(8,128)(2,1)}, u32[]{:S(2)}, u32[]{:S(2)}) collective-permute-start(bf16[512,256]{1,0:T(8,128)(2,1)} %bitcast.21), channel_id=1, source_target_pairs={{0,16},{8,24},{16,0},{24,8},{1,17},{9,25},{17,1},{25,9},{2,18},{10... | collective-permute-start | bytes 786440 | tf_op jit(solution)/shard_map/ppermute | solution.py:18
  5.9 6.0 %copy-start.7 = (s32[1,1,4,6]{3,2,1,0:T(4,128)S(1)}, s32[1,1,4,6]{3,2,1,0:T(4,128)}, u32[]{:S(2)}) copy-start(s32[1,1,4,6]{3,2,1,0:T(4,128)} %param.13) | copy-start | bytes 292
  5.9 6.7 %copy-start = (bf16[1,512,256]{2,1,0:T(8,128)(2,1)S(1)}, bf16[1,512,256]{2,1,0:T(8,128)(2,1)}, u32[]{:S(2)}) copy-start(bf16[1,512,256]{2,1,0:T(8,128)(2,1)} %param.10) | copy-start | bytes 786436
  5.9 14.6 %all-to-all-start = ((bf16[8,64,256]{2,1,0:T(8,128)(2,1)}), bf16[8,64,256]{2,1,0:T(8,128)(2,1)S(1)}, u32[]{:S(2)}, u32[]{:S(2)}) async-start(bf16[8,64,256]{2,1,0:T(8,128)(2,1)} %shard_map.121), calls=%async_computation | async-start | bytes 524288 | tf_op jit(solution)/shard_map/all_to_all | solution.py:209
  11.9 0.7 %copy-start.8 = (s32[1,1,4]{2,1,0:T(1,128)S(1)}, s32[1,1,4]{2,1,0:T(1,128)}, u32[]{:S(2)}) copy-start(s32[1,1,4]{2,1,0:T(1,128)} %param.14) | copy-start | bytes 52
  12.6 2.2 %copy-start.1 = (bf16[1,512,256]{2,1,0:T(8,128)(2,1)S(1)}, bf16[1,512,256]{2,1,0:T(8,128)(2,1)}, u32[]{:S(2)}) copy-start(bf16[1,512,256]{2,1,0:T(8,128)(2,1)} %param.19) | copy-start | bytes 786436
  12.7 1.8 %collective-permute-start.1 = (bf16[512,256]{1,0:T(8,128)(2,1)S(1)}, bf16[512,256]{1,0:T(8,128)(2,1)S(1)}, u32[]{:S(2)}, u32[]{:S(2)}) collective-permute-start(bf16[512,256]{1,0:T(8,128)(2,1)S(1)} %bitcast.23), channel_id=1, source_target_pairs={{0,8},{8,0},{16,24},{24,16},{1,9},{9,1},{17,25},{25,17},{2,10},{10... | collective-permute-start | bytes 786440 | tf_op jit(solution)/shard_map/ppermute | solution.py:18
  12.7 2.1 %collective-permute-start.2 = (bf16[512,256]{1,0:T(8,128)(2,1)}, bf16[512,256]{1,0:T(8,128)(2,1)S(1)}, u32[]{:S(2)}, u32[]{:S(2)}) collective-permute-start(bf16[512,256]{1,0:T(8,128)(2,1)} %collective-permute-done.refs_2_), channel_id=1, source_target_pairs={{0,8},{8,0},{16,24},{24,16},{1,9},{9,1},{17,25},{25,17},{2,10},{10... | collective-permute-start | bytes 786440 | tf_op jit(solution)/shard_map/ppermute | solution.py:18
  14.8 5.7 %copy-start.4 = (s32[1,1,8,32]{3,2,1,0:T(8,128)S(1)}, s32[1,1,8,32]{3,2,1,0:T(8,128)}, u32[]{:S(2)}) copy-start(s32[1,1,8,32]{3,2,1,0:T(8,128)} %param.17) | copy-start | bytes 3076
  14.8 5.7 %copy-start.5 = (f32[1,1,8,32]{3,2,1,0:T(8,128)S(1)}, f32[1,1,8,32]{3,2,1,0:T(8,128)}, u32[]{:S(2)}) copy-start(f32[1,1,8,32]{3,2,1,0:T(8,128)} %param.18) | copy-start | bytes 3076
  17.8 3.9 %collective-permute-start.5 = (bf16[2,256,512]{2,1,0:T(8,128)(2,1)S(1)}, bf16[2,256,512]{2,1,0:T(8,128)(2,1)S(1)}, u32[]{:S(2)}, u32[]{:S(2)}) collective-permute-start(bf16[2,256,512]{2,1,0:T(8,128)(2,1)S(1)} %get-tuple-element.40), channel_id=1, source_target_pairs={{0,8},{8,0},{16,24},{24,16},{1,9},{9,1},{17,25},{25,17},{2,10},{10... | collective-permute-start | bytes 1572872 | tf_op jit(solution)/shard_map/ppermute | solution.py:18
  21.1 1.3 %collective-permute-start.4 = (bf16[128,256]{1,0:T(8,128)(2,1)S(1)}, bf16[128,256]{1,0:T(8,128)(2,1)S(1)}, u32[]{:S(2)}, u32[]{:S(2)}) collective-permute-start(bf16[128,256]{1,0:T(8,128)(2,1)S(1)} %get-tuple-element.38), channel_id=1, source_target_pairs={{0,8},{8,0},{16,24},{24,16},{1,9},{9,1},{17,25},{25,17},{2,10},{10... | collective-permute-start | bytes 196616 | tf_op jit(solution)/shard_map/ppermute | solution.py:18
  21.2 1.4 %collective-permute-start.3 = (bf16[128,256]{1,0:T(8,128)(2,1)S(1)}, bf16[128,256]{1,0:T(8,128)(2,1)S(1)}, u32[]{:S(2)}, u32[]{:S(2)}) collective-permute-start(bf16[128,256]{1,0:T(8,128)(2,1)S(1)} %get-tuple-element.35), channel_id=1, source_target_pairs={{0,8},{8,0},{16,24},{24,16},{1,9},{9,1},{17,25},{25,17},{2,10},{10... | collective-permute-start | bytes 196616 | tf_op jit(solution)/shard_map/ppermute | solution.py:18
  22.6 4.1 %copy-start.2 = (bf16[256,256]{1,0:T(8,128)(2,1)S(1)}, bf16[256,256]{1,0:T(8,128)(2,1)}, u32[]{:S(2)}) copy-start(bf16[256,256]{1,0:T(8,128)(2,1)} %weight.3) | copy-start | bytes 393220
  22.6 5.4 %collective-permute-start.6 = (bf16[128,256]{1,0:T(8,128)(2,1)S(1)}, bf16[128,256]{1,0:T(8,128)(2,1)S(1)}, u32[]{:S(2)}, u32[]{:S(2)}) collective-permute-start(bf16[128,256]{1,0:T(8,128)(2,1)S(1)} %add_convert_fusion.2), channel_id=1, source_target_pairs={{0,2},{1,3},{2,0},{3,1},{4,6},{5,7},{6,4},{7,5},{8,12},{9,13},{10,... | collective-permute-start | bytes 196616 | tf_op jit(solution)/shard_map/ppermute | solution.py:29
  23.8 6.3 %collective-permute-start.7 = (bf16[128,256]{1,0:T(8,128)(2,1)S(1)}, bf16[128,256]{1,0:T(8,128)(2,1)S(1)}, u32[]{:S(2)}, u32[]{:S(2)}) collective-permute-start(bf16[128,256]{1,0:T(8,128)(2,1)S(1)} %add_convert_fusion.2), channel_id=1, source_target_pairs={{0,3},{1,2},{2,1},{3,0},{4,7},{5,6},{6,5},{7,4},{8,28},{9,29},{10,... | collective-permute-start | bytes 196616 | tf_op jit(solution)/shard_map/ppermute | solution.py:29
  25.6 4.7 %collective-permute-start.8 = (bf16[128,256]{1,0:T(8,128)(2,1)S(1)}, bf16[128,256]{1,0:T(8,128)(2,1)S(1)}, u32[]{:S(2)}, u32[]{:S(2)}) collective-permute-start(bf16[128,256]{1,0:T(8,128)(2,1)S(1)} %add_convert_fusion.2), channel_id=1, source_target_pairs={{0,1},{1,0},{2,3},{3,2},{4,5},{5,4},{6,7},{7,6},{8,24},{9,25},{10,... | collective-permute-start | bytes 196616 | tf_op jit(solution)/shard_map/ppermute | solution.py:29
  26.2 8.8 %collective-permute-start.12 = (bf16[256,512]{1,0:T(8,128)(2,1)S(1)}, bf16[256,512]{1,0:T(8,128)(2,1)S(1)}, u32[]{:S(2)}, u32[]{:S(2)}) collective-permute-start(bf16[256,512]{1,0:T(8,128)(2,1)S(1)} %fusion), channel_id=1, source_target_pairs={{0,16},{8,24},{16,0},{24,8},{1,17},{9,25},{17,1},{25,9},{2,18},{10... | collective-permute-start | bytes 786440 | tf_op jit(solution)/shard_map/ppermute | solution.py:18
  30.3 4.7 %copy-start.3 = (s32[1,1,8,32]{3,2,1,0:T(8,128)S(1)}, s32[1,1,8,32]{3,2,1,0:T(8,128)}, u32[]{:S(2)}) copy-start(s32[1,1,8,32]{3,2,1,0:T(8,128)} %param.15) | copy-start | bytes 3076
  30.4 4.6 %copy-start.6 = (s32[1,1,8]{2,1,0:T(1,128)S(1)}, s32[1,1,8]{2,1,0:T(1,128)}, u32[]{:S(2)}) copy-start(s32[1,1,8]{2,1,0:T(1,128)} %param.16) | copy-start | bytes 100
  30.4 6.7 %collective-permute-start.10 = (bf16[128,256]{1,0:T(8,128)(2,1)S(1)}, bf16[128,256]{1,0:T(8,128)(2,1)S(1)}, u32[]{:S(2)}, u32[]{:S(2)}) collective-permute-start(bf16[128,256]{1,0:T(8,128)(2,1)S(1)} %add_convert_fusion.1), channel_id=1, source_target_pairs={{0,20},{1,21},{2,22},{3,23},{4,16},{5,17},{6,18},{7,19},{8,11},{9,... | collective-permute-start | bytes 196616 | tf_op jit(solution)/shard_map/ppermute | solution.py:29
  30.7 6.3 %collective-permute-start.11 = (bf16[128,256]{1,0:T(8,128)(2,1)S(1)}, bf16[128,256]{1,0:T(8,128)(2,1)S(1)}, u32[]{:S(2)}, u32[]{:S(2)}) collective-permute-start(bf16[128,256]{1,0:T(8,128)(2,1)S(1)} %add_convert_fusion.1), channel_id=1, source_target_pairs={{0,16},{1,17},{2,18},{3,19},{4,20},{5,21},{6,22},{7,23},{8,9},{9,8... | collective-permute-start | bytes 196616 | tf_op jit(solution)/shard_map/ppermute | solution.py:29
  32.5 5.2 %collective-permute-start.9 = (bf16[128,256]{1,0:T(8,128)(2,1)S(1)}, bf16[128,256]{1,0:T(8,128)(2,1)S(1)}, u32[]{:S(2)}, u32[]{:S(2)}) collective-permute-start(bf16[128,256]{1,0:T(8,128)(2,1)S(1)} %add_convert_fusion.1), channel_id=1, source_target_pairs={{0,4},{1,5},{2,6},{3,7},{4,0},{5,1},{6,2},{7,3},{8,10},{9,11},{10,... | collective-permute-start | bytes 196616 | tf_op jit(solution)/shard_map/ppermute | solution.py:29
  37.7 1.3 %collective-permute-start.13 = (bf16[128,256]{1,0:T(8,128)(2,1)S(1)}, bf16[128,256]{1,0:T(8,128)(2,1)S(1)}, u32[]{:S(2)}, u32[]{:S(2)}) collective-permute-start(bf16[128,256]{1,0:T(8,128)(2,1)S(1)} %add_convert_fusion), channel_id=1, source_target_pairs={{0,8},{8,0},{16,24},{24,16},{1,9},{9,1},{17,25},{25,17},{2,10},{10... | collective-permute-start | bytes 196616 | tf_op jit(solution)/shard_map/ppermute | solution.py:18

commit v6 on v5

--- a/solution.py
+++ b/solution.py
@@ -253,7 +253,7 @@
             got = swap(jnp.stack(later), "blk", bit)
     term = add(*near_term, kept, other)
     bits = [("dom", bit) for bit in bits_of(peers)]
-    bits[-1:-1] = [("blk", bit) for bit in inner]
+    bits = bits[1:] + bits[:1] + [("blk", bit) for bit in inner]
     fours = [bits[i : i + 2] for i in range(0, len(bits), 2)]
     for i, four in enumerate(fours):
         first, last = i == 0, i == len(fours) - 1

time: 40.1 us -> 39.4 us (0.983)
  starting transfers between devices: 18.9 us -> 18 us
    ppermute x6, starting transfers between devices: 8.01 us -> 7.11 us  [swap_bits(): return lax.ppermute(value, ('blk', 'dom'), pairs)]
  transfers between devices with their start and end apart: 15 -> 15, of which waited for: 11 -> 9; matrix products, arithmetic and copies ran while one was open for 4% -> 4% of each run, Pallas kernels for 22% -> 22%
where the time goes in v6:
time: 39.4 us; the launch traced here: 39.1 us
  starting transfers between devices  18 us (46%)
  waiting for transfers between devices  8.75 us (22%)
  Pallas kernels  8.61 us (22%)
  other arithmetic  2.26 us (6%)
  between operations  0.8 us (2%)
  local copies, waits for them, and re-layouts  0.69 us (2%)
    ppermute x6, starting transfers between devices, swap_bits(): return lax.ppermute(value, ('blk', 'dom'), pairs)  7.11 us
    all_to_all x1, starting transfers between devices, on_device(): lax.all_to_all(outgoing, 'dom', split_axis=0, concat_axis=0, tiled=True)  5.95 us
    ppermute x8, starting transfers between devices, swap(): lax.ppermute(value, axis, [(i, i ^ bit) for i in range(lax.axis_size(axis...  4.94 us
    ppermute x6, waiting for transfers between devices, swap_bits(): return lax.ppermute(value, ('blk', 'dom'), pairs)  3.81 us
    pallas_call x1, Pallas kernels, on_device(): call(functools.partial(adjacency_kernel, groups), [((rows, width), BF16),...  2.94 us
    all_to_all x1, waiting for transfers between devices, on_device(): lax.all_to_all(outgoing, 'dom', split_axis=0, concat_axis=0, tiled=True)  2.53 us
    ppermute x8, waiting for transfers between devices, swap(): lax.ppermute(value, axis, [(i, i ^ bit) for i in range(lax.axis_size(axis...  2.41 us
    pallas_call x1, Pallas kernels, on_device(): call(halo_kernel, [((peers, 2 * slots, width), BF16)], [HBM] * 6, 64 * MI...  2.23 us
  transfers between devices with their start and end apart: 15, of which 9 were waited for; matrix products, arithmetic and copies ran while one was open for 4% of the time, Pallas kernels for 22%

profile of v6, /device:TPU:0, one launch (start us, length us, event | category | flops | bytes accessed | tf_op | source)
XLA Modules:
  0.0 39.1 jit_solution(3280408323814208503)
XLA Ops:
  0.6 3.0 %collective-permute-start = (bf16[512,256]{1,0:T(8,128)(2,1)}, bf16[512,256]{1,0:T(8,128)(2,1)}, u32[]{:S(2)}, u32[]{:S(2)}) collective-permute-start(bf16[512,256]{1,0:T(8,128)(2,1)} %bitcast.21), channel_id=1, source_target_pairs={{0,16},{8,24},{16,0},{24,8},{1,17},{9,25},{17,1},{25,9},{2,18},{10... | collective-permute-start | bytes 786440 | tf_op jit(solution)/shard_map/ppermute | solution.py:18
  3.7 2.2 %shard_map.121 = bf16[8,64,256]{2,1,0:T(8,128)(2,1)} custom-call(bf16[512,256]{1,0:T(8,128)(2,1)} %bitcast.22, bf16[512,256]{1,0:T(8,128)(2,1)} %bitcast.25, s32[8,32]{1,0:T(8,128)} %bitcast.28, s32[8]{0:T(128)} %bitcast.36, s32[8,32]{1,0:T(8,128)} %bitcast.30, f32[8,32]{1,0:T(8,128)} %bitcast.33), custom_call_target="tpu_custom_call" | custom-call | flops 1 | bytes 1 | tf_op jit(solution)/shard_map/pallas_call | solution.py:191
  5.9 0.0 copy-start.7
  5.9 0.0 copy-start
  5.9 5.9 %all-to-all-start = ((bf16[8,64,256]{2,1,0:T(8,128)(2,1)}), bf16[8,64,256]{2,1,0:T(8,128)(2,1)S(1)}, u32[]{:S(2)}, u32[]{:S(2)}) async-start(bf16[8,64,256]{2,1,0:T(8,128)(2,1)} %shard_map.121), calls=%async_computation | async-start | bytes 524288 | tf_op jit(solution)/shard_map/all_to_all | solution.py:209
  11.9 0.0 copy-done.7
  11.9 0.0 copy-start.8
  11.9 0.6 %copy-done.8 = s32[1,1,4]{2,1,0:T(1,128)S(1)} copy-done((s32[1,1,4]{2,1,0:T(1,128)S(1)}, s32[1,1,4]{2,1,0:T(1,128)}, u32[]{:S(2)}) %copy-start.8) | copy-done | bytes 40
  12.6 0.1 iota_compare_fusion
  12.6 0.0 copy-start.1
  12.6 0.0 collective-permute-done.refs_2_
  12.6 0.0 copy-done
  12.7 0.1 collective-permute-start.1
  12.7 0.5 %collective-permute-start.2 = (bf16[512,256]{1,0:T(8,128)(2,1)}, bf16[512,256]{1,0:T(8,128)(2,1)S(1)}, u32[]{:S(2)}, u32[]{:S(2)}) collective-permute-start(bf16[512,256]{1,0:T(8,128)(2,1)} %collective-permute-done.refs_2_), channel_id=1, source_target_pairs={{0,8},{8,0},{16,24},{24,16},{1,9},{9,1},{17,25},{25,17},{2,10},{10... | collective-permute-start | bytes 786440 | tf_op jit(solution)/shard_map/ppermute | solution.py:18
  13.2 1.3 %broadcast_select_fusion.tiles = bf16[4,6,128,128]{3,2,1,0:T(8,128)(2,1)S(1)} fusion(bf16[4,6,128,128]{3,2,1,0:T(8,128)(2,1)} %bitcast.38, pred[4,6]{1,0:T(4,128)(4,1)S(1)} %iota_compare_fusion), kind=kLoop, calls=%fused_computation | loop fusion | flops 393216 | bytes 1572888 | tf_op jit(solution)/shard_map/jit(_where)/select_n | solution.py:222
  14.5 0.0 collective-permute-done.1.refs_1_
  14.5 0.3 collective-permute-done.2.refs_3_
  14.8 0.0 copy-done.1
  14.8 0.0 copy-start.4
  14.8 0.0 copy-start.5
  14.8 2.9 %shard_map.122 = (bf16[512,256]{1,0:T(8,128)(2,1)S(1)}, bf16[128,256]{1,0:T(8,128)(2,1)S(1)}, bf16[128,256]{1,0:T(8,128)(2,1)S(1)}, bf16[2,256,512]{2,1,0:T(8,12...) custom-call(s32[1]{0:T(128)} %bitcast.blk, s32[2,4,6]{2,1,0:T(4,128)S(1)} %add_multiply_fusion.spots, ...), custom_call_target="tpu_custom_call" | custom-call | flops 1 | bytes 1 | tf_op jit(solution)/shard_map/pallas_call | solution.py:224
  17.8 0.2 collective-permute-start.5
  18.0 2.5 %all-to-all-done.halo = bf16[8,64,256]{2,1,0:T(8,128)(2,1)S(1)} async-done(((bf16[8,64,256]{2,1,0:T(8,128)(2,1)}), bf16[8,64,256]{2,1,0:T(8,128)(2,1)S(1)}, u32[]{:S(2)}, u32[]{:S(2)}) %all-to-all-start) | async-done | bytes 262176 | tf_op jit(solution)/shard_map/all_to_all | solution.py:209
  20.5 0.0 copy-done.4
  20.5 0.0 copy-done.5
  20.5 0.6 %shard_map.123 = (bf16[128,256]{1,0:T(8,128)(2,1)S(1)}, bf16[128,256]{1,0:T(8,128)(2,1)S(1)}) custom-call(s32[1]{0:T(128)} %bitcast.blk, bf16[8,64,256]{2,1,0:T(8,128)(2,1)S(1)} %all-to-all-done.halo, s32[8,32]{1,0:T(8,128)S(1)} %bitcast.31, f32[8,32]{1,0:T(8,128)S(1)} %bitcast.34, bf16[512,256]{1,0:T(8,128)(2,1)S(1)} %bitcast.27), custom_call_target="tpu_custom_call" | custom-call | flops 20000000000 | bytes 1 | tf_op jit(solution)/shard_map/pallas_call | solution.py:235
  21.1 0.1 collective-permute-start.4
  21.2 0.5 %collective-permute-start.3 = (bf16[128,256]{1,0:T(8,128)(2,1)S(1)}, bf16[128,256]{1,0:T(8,128)(2,1)S(1)}, u32[]{:S(2)}, u32[]{:S(2)}) collective-permute-start(bf16[128,256]{1,0:T(8,128)(2,1)S(1)} %get-tuple-element.35), channel_id=1, source_target_pairs={{0,8},{8,0},{16,24},{24,16},{1,9},{9,1},{17,25},{25,17},{2,10},{10... | collective-permute-start | bytes 196616 | tf_op jit(solution)/shard_map/ppermute | solution.py:18
  21.7 0.0 collective-permute-done.5.others
  21.7 0.1 fusion
  21.8 0.7 %collective-permute-done.4 = bf16[128,256]{1,0:T(8,128)(2,1)S(1)} collective-permute-done((bf16[128,256]{1,0:T(8,128)(2,1)S(1)}, bf16[128,256]{1,0:T(8,128)(2,1)S(1)}, u32[]{:S(2)}, u32[]{:S(2)}) %collective-permute-start.4) | collective-permute-done | bytes 65568 | tf_op jit(solution)/shard_map/ppermute | solution.py:18
  22.4 0.2 collective-permute-done.3
  22.6 0.0 copy-start.2
  22.6 1.1 %collective-permute-start.6 = (bf16[128,256]{1,0:T(8,128)(2,1)S(1)}, bf16[128,256]{1,0:T(8,128)(2,1)S(1)}, u32[]{:S(2)}, u32[]{:S(2)}) collective-permute-start(bf16[128,256]{1,0:T(8,128)(2,1)S(1)} %add_convert_fusion.2), channel_id=1, source_target_pairs={{0,4},{1,5},{2,6},{3,7},{4,0},{5,1},{6,2},{7,3},{8,24},{9,25},{10,... | collective-permute-start | bytes 196616 | tf_op jit(solution)/shard_map/ppermute | solution.py:29
  23.8 2.4 %collective-permute-start.7 = (bf16[128,256]{1,0:T(8,128)(2,1)S(1)}, bf16[128,256]{1,0:T(8,128)(2,1)S(1)}, u32[]{:S(2)}, u32[]{:S(2)}) collective-permute-start(bf16[128,256]{1,0:T(8,128)(2,1)S(1)} %add_convert_fusion.2), channel_id=1, source_target_pairs={{0,6},{1,7},{2,4},{3,5},{4,2},{5,3},{6,0},{7,1},{8,25},{9,24},{10,... | collective-permute-start | bytes 196616 | tf_op jit(solution)/shard_map/ppermute | solution.py:29
  26.2 0.0 collective-permute-start.8
  26.2 0.5 %collective-permute-start.12 = (bf16[256,512]{1,0:T(8,128)(2,1)S(1)}, bf16[256,512]{1,0:T(8,128)(2,1)S(1)}, u32[]{:S(2)}, u32[]{:S(2)}) collective-permute-start(bf16[256,512]{1,0:T(8,128)(2,1)S(1)} %fusion), channel_id=1, source_target_pairs={{0,16},{8,24},{16,0},{24,8},{1,17},{9,25},{17,1},{25,9},{2,18},{10... | collective-permute-start | bytes 786440 | tf_op jit(solution)/shard_map/ppermute | solution.py:18
  26.7 0.0 copy-done.2
  26.7 1.2 %shard_map.124 = bf16[512,256]{1,0:T(8,128)(2,1)} custom-call(bf16[512,256]{1,0:T(8,128)(2,1)S(1)} %get-tuple-element.44.local, bf16[8,64,256]{2,1,0:T(8,128)(2,1)S(1)} %all-to-all-done.halo, s32[8,32]{1,0:T(8,128)S(1)} %bitcast.32, f32[8,32]{1,0:T(8,128)S(1)} %bitcast.35, bf16[256,256]{1,0:T(8,128)(2,1)S(1)} %copy-done.2), custom_call_target="tpu_custom_call" | custom-call | flops 20000000000 | bytes 1 | tf_op jit(solution)/shard_map/pallas_call | solution.py:262
  27.9 0.7 %collective-permute-done.6 = bf16[128,256]{1,0:T(8,128)(2,1)S(1)} collective-permute-done((bf16[128,256]{1,0:T(8,128)(2,1)S(1)}, bf16[128,256]{1,0:T(8,128)(2,1)S(1)}, u32[]{:S(2)}, u32[]{:S(2)}) %collective-permute-start.6) | collective-permute-done | bytes 65568 | tf_op jit(solution)/shard_map/ppermute | solution.py:29
  28.6 1.4 %collective-permute-done.7 = bf16[128,256]{1,0:T(8,128)(2,1)S(1)} collective-permute-done((bf16[128,256]{1,0:T(8,128)(2,1)S(1)}, bf16[128,256]{1,0:T(8,128)(2,1)S(1)}, u32[]{:S(2)}, u32[]{:S(2)}) %collective-permute-start.7) | collective-permute-done | bytes 65568 | tf_op jit(solution)/shard_map/ppermute | solution.py:29
  29.9 0.7 %collective-permute-done.8 = bf16[128,256]{1,0:T(8,128)(2,1)S(1)} collective-permute-done((bf16[128,256]{1,0:T(8,128)(2,1)S(1)}, bf16[128,256]{1,0:T(8,128)(2,1)S(1)}, u32[]{:S(2)}, u32[]{:S(2)}) %collective-permute-start.8) | collective-permute-done | bytes 65568 | tf_op jit(solution)/shard_map/ppermute | solution.py:29
  30.6 0.0 copy-start.3
  30.7 0.0 copy-start.6
  30.7 0.9 %collective-permute-start.10 = (bf16[128,256]{1,0:T(8,128)(2,1)S(1)}, bf16[128,256]{1,0:T(8,128)(2,1)S(1)}, u32[]{:S(2)}, u32[]{:S(2)}) collective-permute-start(bf16[128,256]{1,0:T(8,128)(2,1)S(1)} %add_convert_fusion.1), channel_id=1, source_target_pairs={{0,17},{1,16},{2,19},{3,18},{4,21},{5,20},{6,23},{7,22},{8,14},{9,... | collective-permute-start | bytes 196616 | tf_op jit(solution)/shard_map/ppermute | solution.py:29
  31.6 1.2 %collective-permute-start.11 = (bf16[128,256]{1,0:T(8,128)(2,1)S(1)}, bf16[128,256]{1,0:T(8,128)(2,1)S(1)}, u32[]{:S(2)}, u32[]{:S(2)}) collective-permute-start(bf16[128,256]{1,0:T(8,128)(2,1)S(1)} %add_convert_fusion.1), channel_id=1, source_target_pairs={{0,1},{1,0},{2,3},{3,2},{4,5},{5,4},{6,7},{7,6},{8,10},{9,11},{10,... | collective-permute-start | bytes 196616 | tf_op jit(solution)/shard_map/ppermute | solution.py:29
  32.7 1.5 %collective-permute-start.9 = (bf16[128,256]{1,0:T(8,128)(2,1)S(1)}, bf16[128,256]{1,0:T(8,128)(2,1)S(1)}, u32[]{:S(2)}, u32[]{:S(2)}) collective-permute-start(bf16[128,256]{1,0:T(8,128)(2,1)S(1)} %add_convert_fusion.1), channel_id=1, source_target_pairs={{0,16},{1,17},{2,18},{3,19},{4,20},{5,21},{6,22},{7,23},{8,12},{9,... | collective-permute-start | bytes 196616 | tf_op jit(solution)/shard_map/ppermute | solution.py:29
  34.2 0.0 collective-permute-done.12.third
  34.2 0.0 copy-done.3
  34.2 0.0 copy-done.6
  34.3 1.7 %shard_map.125 = bf16[512,256]{1,0:T(8,128)(2,1)} custom-call(s32[8]{0:T(128)S(1)} %bitcast.37, bf16[256,512]{1,0:T(8,128)(2,1)S(1)} %get-tuple-element.49.first, bf16[2,256,512]{2,1,0:T(8,128)(2,1)S(1)} %collective-permute-done.5.others, bf16[256,512]{1,0:T(8,128)(2,1)S(1)} %collective-permute-done.12.third, bf16[8,64,256]{2,1,0:T(8,128)(2,1)S(1)} %all-to-all-done.halo, ...), custom_call_target="tpu_custom_call" | custom-call | flops 1 | bytes 1 | tf_op jit(solution)/shard_map/pallas_call | solution.py:266
  36.0 0.0 collective-permute-done.10
  36.0 0.0 collective-permute-done.11
  36.0 1.0 %collective-permute-done.9 = bf16[128,256]{1,0:T(8,128)(2,1)S(1)} collective-permute-done((bf16[128,256]{1,0:T(8,128)(2,1)S(1)}, bf16[128,256]{1,0:T(8,128)(2,1)S(1)}, u32[]{:S(2)}, u32[]{:S(2)}) %collective-permute-start.9) | collective-permute-done | bytes 65568 | tf_op jit(solution)/shard_map/ppermute | solution.py:29
  37.0 0.1 collective-permute-start.13
  37.1 1.2 %collective-permute-done.13 = bf16[128,256]{1,0:T(8,128)(2,1)S(1)} collective-permute-done((bf16[128,256]{1,0:T(8,128)(2,1)S(1)}, bf16[128,256]{1,0:T(8,128)(2,1)S(1)}, u32[]{:S(2)}, u32[]{:S(2)}) %collective-permute-start.13) | collective-permute-done | bytes 65568 | tf_op jit(solution)/shard_map/ppermute | solution.py:18
  38.4 0.7 %convert_multiply_fusion = f32[256,256]{1,0:T(8,128)} fusion(bf16[128,256]{1,0:T(8,128)(2,1)S(1)} %get-tuple-element.56, bf16[128,256]{1,0:T(8,128)(2,1)S(1)} %get-tuple-element.55), kind=kLoop, calls=%fused_computation.4 | loop fusion | flops 327680 | bytes 393216 | tf_op jit(solution)/shard_map/mul | solution.py:286
  (6 shorter events, 0.1 us)
Async XLA Ops:
  0.6 12.0 %collective-permute-start = (bf16[512,256]{1,0:T(8,128)(2,1)}, bf16[512,256]{1,0:T(8,128)(2,1)}, u32[]{:S(2)}, u32[]{:S(2)}) collective-permute-start(bf16[512,256]{1,0:T(8,128)(2,1)} %bitcast.21), channel_id=1, source_target_pairs={{0,16},{8,24},{16,0},{24,8},{1,17},{9,25},{17,1},{25,9},{2,18},{10... | collective-permute-start | bytes 786440 | tf_op jit(solution)/shard_map/ppermute | solution.py:18
  5.9 6.0 %copy-start.7 = (s32[1,1,4,6]{3,2,1,0:T(4,128)S(1)}, s32[1,1,4,6]{3,2,1,0:T(4,128)}, u32[]{:S(2)}) copy-start(s32[1,1,4,6]{3,2,1,0:T(4,128)} %param.13) | copy-start | bytes 292
  5.9 6.7 %copy-start = (bf16[1,512,256]{2,1,0:T(8,128)(2,1)S(1)}, bf16[1,512,256]{2,1,0:T(8,128)(2,1)}, u32[]{:S(2)}) copy-start(bf16[1,512,256]{2,1,0:T(8,128)(2,1)} %param.10) | copy-start | bytes 786436
  5.9 14.6 %all-to-all-start = ((bf16[8,64,256]{2,1,0:T(8,128)(2,1)}), bf16[8,64,256]{2,1,0:T(8,128)(2,1)S(1)}, u32[]{:S(2)}, u32[]{:S(2)}) async-start(bf16[8,64,256]{2,1,0:T(8,128)(2,1)} %shard_map.121), calls=%async_computation | async-start | bytes 524288 | tf_op jit(solution)/shard_map/all_to_all | solution.py:209
  11.9 0.7 %copy-start.8 = (s32[1,1,4]{2,1,0:T(1,128)S(1)}, s32[1,1,4]{2,1,0:T(1,128)}, u32[]{:S(2)}) copy-start(s32[1,1,4]{2,1,0:T(1,128)} %param.14) | copy-start | bytes 52
  12.6 2.2 %copy-start.1 = (bf16[1,512,256]{2,1,0:T(8,128)(2,1)S(1)}, bf16[1,512,256]{2,1,0:T(8,128)(2,1)}, u32[]{:S(2)}) copy-start(bf16[1,512,256]{2,1,0:T(8,128)(2,1)} %param.19) | copy-start | bytes 786436
  12.7 1.8 %collective-permute-start.1 = (bf16[512,256]{1,0:T(8,128)(2,1)S(1)}, bf16[512,256]{1,0:T(8,128)(2,1)S(1)}, u32[]{:S(2)}, u32[]{:S(2)}) collective-permute-start(bf16[512,256]{1,0:T(8,128)(2,1)S(1)} %bitcast.23), channel_id=1, source_target_pairs={{0,8},{8,0},{16,24},{24,16},{1,9},{9,1},{17,25},{25,17},{2,10},{10... | collective-permute-start | bytes 786440 | tf_op jit(solution)/shard_map/ppermute | solution.py:18
  12.7 2.1 %collective-permute-start.2 = (bf16[512,256]{1,0:T(8,128)(2,1)}, bf16[512,256]{1,0:T(8,128)(2,1)S(1)}, u32[]{:S(2)}, u32[]{:S(2)}) collective-permute-start(bf16[512,256]{1,0:T(8,128)(2,1)} %collective-permute-done.refs_2_), channel_id=1, source_target_pairs={{0,8},{8,0},{16,24},{24,16},{1,9},{9,1},{17,25},{25,17},{2,10},{10... | collective-permute-start | bytes 786440 | tf_op jit(solution)/shard_map/ppermute | solution.py:18
  14.8 5.7 %copy-start.4 = (s32[1,1,8,32]{3,2,1,0:T(8,128)S(1)}, s32[1,1,8,32]{3,2,1,0:T(8,128)}, u32[]{:S(2)}) copy-start(s32[1,1,8,32]{3,2,1,0:T(8,128)} %param.17) | copy-start | bytes 3076
  14.8 5.7 %copy-start.5 = (f32[1,1,8,32]{3,2,1,0:T(8,128)S(1)}, f32[1,1,8,32]{3,2,1,0:T(8,128)}, u32[]{:S(2)}) copy-start(f32[1,1,8,32]{3,2,1,0:T(8,128)} %param.18) | copy-start | bytes 3076
  17.8 3.9 %collective-permute-start.5 = (bf16[2,256,512]{2,1,0:T(8,128)(2,1)S(1)}, bf16[2,256,512]{2,1,0:T(8,128)(2,1)S(1)}, u32[]{:S(2)}, u32[]{:S(2)}) collective-permute-start(bf16[2,256,512]{2,1,0:T(8,128)(2,1)S(1)} %get-tuple-element.40), channel_id=1, source_target_pairs={{0,8},{8,0},{16,24},{24,16},{1,9},{9,1},{17,25},{25,17},{2,10},{10... | collective-permute-start | bytes 1572872 | tf_op jit(solution)/shard_map/ppermute | solution.py:18
  21.1 1.3 %collective-permute-start.4 = (bf16[128,256]{1,0:T(8,128)(2,1)S(1)}, bf16[128,256]{1,0:T(8,128)(2,1)S(1)}, u32[]{:S(2)}, u32[]{:S(2)}) collective-permute-start(bf16[128,256]{1,0:T(8,128)(2,1)S(1)} %get-tuple-element.38), channel_id=1, source_target_pairs={{0,8},{8,0},{16,24},{24,16},{1,9},{9,1},{17,25},{25,17},{2,10},{10... | collective-permute-start | bytes 196616 | tf_op jit(solution)/shard_map/ppermute | solution.py:18
  21.2 1.4 %collective-permute-start.3 = (bf16[128,256]{1,0:T(8,128)(2,1)S(1)}, bf16[128,256]{1,0:T(8,128)(2,1)S(1)}, u32[]{:S(2)}, u32[]{:S(2)}) collective-permute-start(bf16[128,256]{1,0:T(8,128)(2,1)S(1)} %get-tuple-element.35), channel_id=1, source_target_pairs={{0,8},{8,0},{16,24},{24,16},{1,9},{9,1},{17,25},{25,17},{2,10},{10... | collective-permute-start | bytes 196616 | tf_op jit(solution)/shard_map/ppermute | solution.py:18
  22.6 4.1 %copy-start.2 = (bf16[256,256]{1,0:T(8,128)(2,1)S(1)}, bf16[256,256]{1,0:T(8,128)(2,1)}, u32[]{:S(2)}) copy-start(bf16[256,256]{1,0:T(8,128)(2,1)} %weight.3) | copy-start | bytes 393220
  22.6 5.9 %collective-permute-start.6 = (bf16[128,256]{1,0:T(8,128)(2,1)S(1)}, bf16[128,256]{1,0:T(8,128)(2,1)S(1)}, u32[]{:S(2)}, u32[]{:S(2)}) collective-permute-start(bf16[128,256]{1,0:T(8,128)(2,1)S(1)} %add_convert_fusion.2), channel_id=1, source_target_pairs={{0,4},{1,5},{2,6},{3,7},{4,0},{5,1},{6,2},{7,3},{8,24},{9,25},{10,... | collective-permute-start | bytes 196616 | tf_op jit(solution)/shard_map/ppermute | solution.py:29
  23.8 6.2 %collective-permute-start.7 = (bf16[128,256]{1,0:T(8,128)(2,1)S(1)}, bf16[128,256]{1,0:T(8,128)(2,1)S(1)}, u32[]{:S(2)}, u32[]{:S(2)}) collective-permute-start(bf16[128,256]{1,0:T(8,128)(2,1)S(1)} %add_convert_fusion.2), channel_id=1, source_target_pairs={{0,6},{1,7},{2,4},{3,5},{4,2},{5,3},{6,0},{7,1},{8,25},{9,24},{10,... | collective-permute-start | bytes 196616 | tf_op jit(solution)/shard_map/ppermute | solution.py:29
  26.2 4.5 %collective-permute-start.8 = (bf16[128,256]{1,0:T(8,128)(2,1)S(1)}, bf16[128,256]{1,0:T(8,128)(2,1)S(1)}, u32[]{:S(2)}, u32[]{:S(2)}) collective-permute-start(bf16[128,256]{1,0:T(8,128)(2,1)S(1)} %add_convert_fusion.2), channel_id=1, source_target_pairs={{0,2},{1,3},{2,0},{3,1},{4,6},{5,7},{6,4},{7,5},{8,9},{9,8},{10,11... | collective-permute-start | bytes 196616 | tf_op jit(solution)/shard_map/ppermute | solution.py:29
  26.2 8.1 %collective-permute-start.12 = (bf16[256,512]{1,0:T(8,128)(2,1)S(1)}, bf16[256,512]{1,0:T(8,128)(2,1)S(1)}, u32[]{:S(2)}, u32[]{:S(2)}) collective-permute-start(bf16[256,512]{1,0:T(8,128)(2,1)S(1)} %fusion), channel_id=1, source_target_pairs={{0,16},{8,24},{16,0},{24,8},{1,17},{9,25},{17,1},{25,9},{2,18},{10... | collective-permute-start | bytes 786440 | tf_op jit(solution)/shard_map/ppermute | solution.py:18
  30.6 3.6 %copy-start.3 = (s32[1,1,8,32]{3,2,1,0:T(8,128)S(1)}, s32[1,1,8,32]{3,2,1,0:T(8,128)}, u32[]{:S(2)}) copy-start(s32[1,1,8,32]{3,2,1,0:T(8,128)} %param.15) | copy-start | bytes 3076
  30.7 3.6 %copy-start.6 = (s32[1,1,8]{2,1,0:T(1,128)S(1)}, s32[1,1,8]{2,1,0:T(1,128)}, u32[]{:S(2)}) copy-start(s32[1,1,8]{2,1,0:T(1,128)} %param.16) | copy-start | bytes 100
  30.7 5.3 %collective-permute-start.10 = (bf16[128,256]{1,0:T(8,128)(2,1)S(1)}, bf16[128,256]{1,0:T(8,128)(2,1)S(1)}, u32[]{:S(2)}, u32[]{:S(2)}) collective-permute-start(bf16[128,256]{1,0:T(8,128)(2,1)S(1)} %add_convert_fusion.1), channel_id=1, source_target_pairs={{0,17},{1,16},{2,19},{3,18},{4,21},{5,20},{6,23},{7,22},{8,14},{9,... | collective-permute-start | bytes 196616 | tf_op jit(solution)/shard_map/ppermute | solution.py:29
  31.6 4.4 %collective-permute-start.11 = (bf16[128,256]{1,0:T(8,128)(2,1)S(1)}, bf16[128,256]{1,0:T(8,128)(2,1)S(1)}, u32[]{:S(2)}, u32[]{:S(2)}) collective-permute-start(bf16[128,256]{1,0:T(8,128)(2,1)S(1)} %add_convert_fusion.1), channel_id=1, source_target_pairs={{0,1},{1,0},{2,3},{3,2},{4,5},{5,4},{6,7},{7,6},{8,10},{9,11},{10,... | collective-permute-start | bytes 196616 | tf_op jit(solution)/shard_map/ppermute | solution.py:29
  32.7 4.3 %collective-permute-start.9 = (bf16[128,256]{1,0:T(8,128)(2,1)S(1)}, bf16[128,256]{1,0:T(8,128)(2,1)S(1)}, u32[]{:S(2)}, u32[]{:S(2)}) collective-permute-start(bf16[128,256]{1,0:T(8,128)(2,1)S(1)} %add_convert_fusion.1), channel_id=1, source_target_pairs={{0,16},{1,17},{2,18},{3,19},{4,20},{5,21},{6,22},{7,23},{8,12},{9,... | collective-permute-start | bytes 196616 | tf_op jit(solution)/shard_map/ppermute | solution.py:29
  37.0 1.3 %collective-permute-start.13 = (bf16[128,256]{1,0:T(8,128)(2,1)S(1)}, bf16[128,256]{1,0:T(8,128)(2,1)S(1)}, u32[]{:S(2)}, u32[]{:S(2)}) collective-permute-start(bf16[128,256]{1,0:T(8,128)(2,1)S(1)} %add_convert_fusion), channel_id=1, source_target_pairs={{0,8},{8,0},{16,24},{24,16},{1,9},{9,1},{17,25},{25,17},{2,10},{10... | collective-permute-start | bytes 196616 | tf_op jit(solution)/shard_map/ppermute | solution.py:18

commit v7 on v6

--- a/solution.py
+++ b/solution.py
@@ -124,9 +124,11 @@
     return matmul(weights_of(rows, owner, edge), received, 1, 0)
 
 
-def halo_term_kernel(blk, halo, owner, edge, grad, kept, sent, term):
-    rows, width = grad.shape
-    term[...] = matmul(halo_sum(halo, owner, edge, rows).astype(BF16), grad[...], 0, 0)
+def halo_term_kernel(blk, halo, outgoing, kept, sent, term):
+    peers, both, width = halo.shape
+    received = halo[:, : both // 2, :].reshape(-1, width)
+    weighted = outgoing[:, both // 2 :, :].reshape(-1, width)
+    term[...] = matmul(received, weighted, 0, 0)
     split_halves(blk, term, kept, sent)
 
 
@@ -235,11 +237,11 @@
     kept, sent = call(
         halo_term_kernel,
         [half_term, half_term],
-        [SMEM] + [VMEM] * 4,
+        [SMEM] + [VMEM] * 2,
         16 * MIB,
         [pltpu.VMEM((width, width), F32)],
         flops=2 * 10**10,
-    )(blk, halo, owner, edge, grad)
+    )(blk, halo, outgoing)
     other = swap(sent, "blk", 1)
     inner = bits_of(groups)[1:]
     for bit in inner:

time: 39.4 us -> 39.1 us (level)
  transfers between devices with their start and end apart: 15 -> 15, of which waited for: 9 -> 9; matrix products, arithmetic and copies ran while one was open for 4% -> 4% of each run, Pallas kernels for 22% -> 21%
where the time goes in v7:
time: 39.1 us; the launch traced here: 38.8 us
  starting transfers between devices  18 us (46%)
  waiting for transfers between devices  8.72 us (22%)
  Pallas kernels  8.3 us (21%)
  other arithmetic  2.25 us (6%)
  between operations  0.8 us (2%)
  local copies, waits for them, and re-layouts  0.69 us (2%)
    ppermute x6, starting transfers between devices, swap_bits(): return lax.ppermute(value, ('blk', 'dom'), pairs)  7.11 us
    all_to_all x1, starting transfers between devices, on_device(): lax.all_to_all(outgoing, 'dom', split_axis=0, concat_axis=0, tiled=True)  5.95 us
    ppermute x8, starting transfers between devices, swap(): lax.ppermute(value, axis, [(i, i ^ bit) for i in range(lax.axis_size(axis...  4.94 us
    ppermute x6, waiting for transfers between devices, swap_bits(): return lax.ppermute(value, ('blk', 'dom'), pairs)  3.81 us
    pallas_call x1, Pallas kernels, on_device(): call(functools.partial(adjacency_kernel, groups), [((rows, width), BF16),...  2.94 us
    all_to_all x1, waiting for transfers between devices, on_device(): lax.all_to_all(outgoing, 'dom', split_axis=0, concat_axis=0, tiled=True)  2.51 us
    ppermute x8, waiting for transfers between devices, swap(): lax.ppermute(value, axis, [(i, i ^ bit) for i in range(lax.axis_size(axis...  2.41 us
    pallas_call x1, Pallas kernels, on_device(): call(halo_kernel, [((peers, 2 * slots, width), BF16)], [HBM] * 6, 64 * MI...  2.23 us
  transfers between devices with their start and end apart: 15, of which 9 were waited for; matrix products, arithmetic and copies ran while one was open for 4% of the time, Pallas kernels for 21%

profile of v7, /device:TPU:0, one launch (start us, length us, event | category | flops | bytes accessed | tf_op | source)
XLA Modules:
  0.0 38.8 jit_solution(4547225003160356379)
XLA Ops:
  0.6 3.0 %collective-permute-start = (bf16[512,256]{1,0:T(8,128)(2,1)}, bf16[512,256]{1,0:T(8,128)(2,1)}, u32[]{:S(2)}, u32[]{:S(2)}) collective-permute-start(bf16[512,256]{1,0:T(8,128)(2,1)} %bitcast.23), channel_id=1, source_target_pairs={{0,16},{8,24},{16,0},{24,8},{1,17},{9,25},{17,1},{25,9},{2,18},{10... | collective-permute-start | bytes 786440 | tf_op jit(solution)/shard_map/ppermute | solution.py:18
  3.7 2.2 %shard_map.121.outgoing = bf16[8,64,256]{2,1,0:T(8,128)(2,1)} custom-call(bf16[512,256]{1,0:T(8,128)(2,1)} %bitcast.24, bf16[512,256]{1,0:T(8,128)(2,1)} %bitcast.21, s32[8,32]{1,0:T(8,128)} %bitcast.27, s32[8]{0:T(128)} %bitcast.33, s32[8,32]{1,0:T(8,128)} %bitcast.29, f32[8,32]{1,0:T(8,128)} %bitcast.31), custom_call_target="tpu_custom_call" | custom-call | flops 1 | bytes 1 | tf_op jit(solution)/shard_map/pallas_call | solution.py:193
  5.9 0.0 copy-start.8
  5.9 0.0 copy-start.1
  5.9 5.9 %all-to-all-start = ((bf16[8,64,256]{2,1,0:T(8,128)(2,1)}), bf16[8,64,256]{2,1,0:T(8,128)(2,1)S(1)}, u32[]{:S(2)}, u32[]{:S(2)}) async-start(bf16[8,64,256]{2,1,0:T(8,128)(2,1)} %shard_map.121.outgoing), calls=%async_computation | async-start | bytes 524288 | tf_op jit(solution)/shard_map/all_to_all | solution.py:211
  11.9 0.0 copy-done.8
  11.9 0.0 copy-start.9
  11.9 0.6 %copy-done.9 = s32[1,1,4]{2,1,0:T(1,128)S(1)} copy-done((s32[1,1,4]{2,1,0:T(1,128)S(1)}, s32[1,1,4]{2,1,0:T(1,128)}, u32[]{:S(2)}) %copy-start.9) | copy-done | bytes 40
  12.6 0.1 iota_compare_fusion
  12.6 0.0 copy-start
  12.6 0.0 collective-permute-done.refs_2_
  12.6 0.0 copy-done.1
  12.7 0.1 collective-permute-start.1
  12.7 0.5 %collective-permute-start.2 = (bf16[512,256]{1,0:T(8,128)(2,1)}, bf16[512,256]{1,0:T(8,128)(2,1)S(1)}, u32[]{:S(2)}, u32[]{:S(2)}) collective-permute-start(bf16[512,256]{1,0:T(8,128)(2,1)} %collective-permute-done.refs_2_), channel_id=1, source_target_pairs={{0,8},{8,0},{16,24},{24,16},{1,9},{9,1},{17,25},{25,17},{2,10},{10... | collective-permute-start | bytes 786440 | tf_op jit(solution)/shard_map/ppermute | solution.py:18
  13.2 1.3 %broadcast_select_fusion.tiles = bf16[4,6,128,128]{3,2,1,0:T(8,128)(2,1)S(1)} fusion(bf16[4,6,128,128]{3,2,1,0:T(8,128)(2,1)} %bitcast.35, pred[4,6]{1,0:T(4,128)(4,1)S(1)} %iota_compare_fusion), kind=kLoop, calls=%fused_computation | loop fusion | flops 393216 | bytes 1572888 | tf_op jit(solution)/shard_map/jit(_where)/select_n | solution.py:224
  14.5 0.0 collective-permute-done.1.refs_1_
  14.5 0.3 collective-permute-done.2.refs_3_
  14.8 0.0 copy-done
  14.8 0.0 copy-start.2
  14.8 2.9 %shard_map.122 = (bf16[512,256]{1,0:T(8,128)(2,1)S(1)}, bf16[128,256]{1,0:T(8,128)(2,1)S(1)}, bf16[128,256]{1,0:T(8,128)(2,1)S(1)}, bf16[2,256,512]{2,1,0:T(8,12...) custom-call(s32[1]{0:T(128)} %bitcast.blk, s32[2,4,6]{2,1,0:T(4,128)S(1)} %add_multiply_fusion.spots, ...), custom_call_target="tpu_custom_call" | custom-call | flops 1 | bytes 1 | tf_op jit(solution)/shard_map/pallas_call | solution.py:226
  17.8 0.2 collective-permute-start.5
  18.0 2.5 %all-to-all-done.halo = bf16[8,64,256]{2,1,0:T(8,128)(2,1)S(1)} async-done(((bf16[8,64,256]{2,1,0:T(8,128)(2,1)}), bf16[8,64,256]{2,1,0:T(8,128)(2,1)S(1)}, u32[]{:S(2)}, u32[]{:S(2)}) %all-to-all-start) | async-done | bytes 262176 | tf_op jit(solution)/shard_map/all_to_all | solution.py:211
  20.5 0.0 copy-done.2
  20.5 0.3 shard_map.123
  20.8 0.1 collective-permute-start.4
  20.9 0.5 %collective-permute-start.3 = (bf16[128,256]{1,0:T(8,128)(2,1)S(1)}, bf16[128,256]{1,0:T(8,128)(2,1)S(1)}, u32[]{:S(2)}, u32[]{:S(2)}) collective-permute-start(bf16[128,256]{1,0:T(8,128)(2,1)S(1)} %get-tuple-element.35), channel_id=1, source_target_pairs={{0,8},{8,0},{16,24},{24,16},{1,9},{9,1},{17,25},{25,17},{2,10},{10... | collective-permute-start | bytes 196616 | tf_op jit(solution)/shard_map/ppermute | solution.py:18
  21.4 0.0 collective-permute-done.5.others
  21.4 0.1 fusion
  21.4 0.7 %collective-permute-done.4 = bf16[128,256]{1,0:T(8,128)(2,1)S(1)} collective-permute-done((bf16[128,256]{1,0:T(8,128)(2,1)S(1)}, bf16[128,256]{1,0:T(8,128)(2,1)S(1)}, u32[]{:S(2)}, u32[]{:S(2)}) %collective-permute-start.4) | collective-permute-done | bytes 65568 | tf_op jit(solution)/shard_map/ppermute | solution.py:18
  22.1 0.2 collective-permute-done.3
  22.3 0.0 copy-start.3
  22.3 0.0 copy-start.5
  22.3 0.0 copy-start.6
  22.3 1.1 %collective-permute-start.6 = (bf16[128,256]{1,0:T(8,128)(2,1)S(1)}, bf16[128,256]{1,0:T(8,128)(2,1)S(1)}, u32[]{:S(2)}, u32[]{:S(2)}) collective-permute-start(bf16[128,256]{1,0:T(8,128)(2,1)S(1)} %add_convert_fusion.2), channel_id=1, source_target_pairs={{0,4},{1,5},{2,6},{3,7},{4,0},{5,1},{6,2},{7,3},{8,24},{9,25},{10,... | collective-permute-start | bytes 196616 | tf_op jit(solution)/shard_map/ppermute | solution.py:29
  23.4 2.4 %collective-permute-start.7 = (bf16[128,256]{1,0:T(8,128)(2,1)S(1)}, bf16[128,256]{1,0:T(8,128)(2,1)S(1)}, u32[]{:S(2)}, u32[]{:S(2)}) collective-permute-start(bf16[128,256]{1,0:T(8,128)(2,1)S(1)} %add_convert_fusion.2), channel_id=1, source_target_pairs={{0,6},{1,7},{2,4},{3,5},{4,2},{5,3},{6,0},{7,1},{8,25},{9,24},{10,... | collective-permute-start | bytes 196616 | tf_op jit(solution)/shard_map/ppermute | solution.py:29
  25.8 0.0 collective-permute-start.8
  25.9 0.5 %collective-permute-start.12 = (bf16[256,512]{1,0:T(8,128)(2,1)S(1)}, bf16[256,512]{1,0:T(8,128)(2,1)S(1)}, u32[]{:S(2)}, u32[]{:S(2)}) collective-permute-start(bf16[256,512]{1,0:T(8,128)(2,1)S(1)} %fusion), channel_id=1, source_target_pairs={{0,16},{8,24},{16,0},{24,8},{1,17},{9,25},{17,1},{25,9},{2,18},{10... | collective-permute-start | bytes 786440 | tf_op jit(solution)/shard_map/ppermute | solution.py:18
  26.4 0.0 copy-done.3
  26.4 0.0 copy-done.5
  26.4 0.0 copy-done.6
  26.4 1.2 %shard_map.124 = bf16[512,256]{1,0:T(8,128)(2,1)} custom-call(bf16[512,256]{1,0:T(8,128)(2,1)S(1)} %get-tuple-element.44.local, bf16[8,64,256]{2,1,0:T(8,128)(2,1)S(1)} %all-to-all-done.halo, s32[8,32]{1,0:T(8,128)S(1)} %bitcast.30, f32[8,32]{1,0:T(8,128)S(1)} %bitcast.32, bf16[256,256]{1,0:T(8,128)(2,1)S(1)} %copy-done.3), custom_call_target="tpu_custom_call" | custom-call | flops 20000000000 | bytes 1 | tf_op jit(solution)/shard_map/pallas_call | solution.py:264
  27.5 0.7 %collective-permute-done.6 = bf16[128,256]{1,0:T(8,128)(2,1)S(1)} collective-permute-done((bf16[128,256]{1,0:T(8,128)(2,1)S(1)}, bf16[128,256]{1,0:T(8,128)(2,1)S(1)}, u32[]{:S(2)}, u32[]{:S(2)}) %collective-permute-start.6) | collective-permute-done | bytes 65568 | tf_op jit(solution)/shard_map/ppermute | solution.py:29
  28.2 1.4 %collective-permute-done.7 = bf16[128,256]{1,0:T(8,128)(2,1)S(1)} collective-permute-done((bf16[128,256]{1,0:T(8,128)(2,1)S(1)}, bf16[128,256]{1,0:T(8,128)(2,1)S(1)}, u32[]{:S(2)}, u32[]{:S(2)}) %collective-permute-start.7) | collective-permute-done | bytes 65568 | tf_op jit(solution)/shard_map/ppermute | solution.py:29
  29.6 0.7 %collective-permute-done.8 = bf16[128,256]{1,0:T(8,128)(2,1)S(1)} collective-permute-done((bf16[128,256]{1,0:T(8,128)(2,1)S(1)}, bf16[128,256]{1,0:T(8,128)(2,1)S(1)}, u32[]{:S(2)}, u32[]{:S(2)}) %collective-permute-start.8) | collective-permute-done | bytes 65568 | tf_op jit(solution)/shard_map/ppermute | solution.py:29
  30.3 0.0 copy-start.4
  30.3 0.0 copy-start.7
  30.4 0.9 %collective-permute-start.10 = (bf16[128,256]{1,0:T(8,128)(2,1)S(1)}, bf16[128,256]{1,0:T(8,128)(2,1)S(1)}, u32[]{:S(2)}, u32[]{:S(2)}) collective-permute-start(bf16[128,256]{1,0:T(8,128)(2,1)S(1)} %add_convert_fusion.1), channel_id=1, source_target_pairs={{0,17},{1,16},{2,19},{3,18},{4,21},{5,20},{6,23},{7,22},{8,14},{9,... | collective-permute-start | bytes 196616 | tf_op jit(solution)/shard_map/ppermute | solution.py:29
  31.2 1.2 %collective-permute-start.11 = (bf16[128,256]{1,0:T(8,128)(2,1)S(1)}, bf16[128,256]{1,0:T(8,128)(2,1)S(1)}, u32[]{:S(2)}, u32[]{:S(2)}) collective-permute-start(bf16[128,256]{1,0:T(8,128)(2,1)S(1)} %add_convert_fusion.1), channel_id=1, source_target_pairs={{0,1},{1,0},{2,3},{3,2},{4,5},{5,4},{6,7},{7,6},{8,10},{9,11},{10,... | collective-permute-start | bytes 196616 | tf_op jit(solution)/shard_map/ppermute | solution.py:29
  32.4 1.5 %collective-permute-start.9 = (bf16[128,256]{1,0:T(8,128)(2,1)S(1)}, bf16[128,256]{1,0:T(8,128)(2,1)S(1)}, u32[]{:S(2)}, u32[]{:S(2)}) collective-permute-start(bf16[128,256]{1,0:T(8,128)(2,1)S(1)} %add_convert_fusion.1), channel_id=1, source_target_pairs={{0,16},{1,17},{2,18},{3,19},{4,20},{5,21},{6,22},{7,23},{8,12},{9,... | collective-permute-start | bytes 196616 | tf_op jit(solution)/shard_map/ppermute | solution.py:29
  33.9 0.0 collective-permute-done.12.third
  33.9 0.0 copy-done.4
  33.9 0.0 copy-done.7
  33.9 1.7 %shard_map.125 = bf16[512,256]{1,0:T(8,128)(2,1)} custom-call(s32[8]{0:T(128)S(1)} %bitcast.34, bf16[256,512]{1,0:T(8,128)(2,1)S(1)} %get-tuple-element.49.first, bf16[2,256,512]{2,1,0:T(8,128)(2,1)S(1)} %collective-permute-done.5.others, bf16[256,512]{1,0:T(8,128)(2,1)S(1)} %collective-permute-done.12.third, bf16[8,64,256]{2,1,0:T(8,128)(2,1)S(1)} %all-to-all-done.halo, ...), custom_call_target="tpu_custom_call" | custom-call | flops 1 | bytes 1 | tf_op jit(solution)/shard_map/pallas_call | solution.py:268
  35.6 0.0 collective-permute-done.10
  35.6 0.0 collective-permute-done.11
  35.6 1.0 %collective-permute-done.9 = bf16[128,256]{1,0:T(8,128)(2,1)S(1)} collective-permute-done((bf16[128,256]{1,0:T(8,128)(2,1)S(1)}, bf16[128,256]{1,0:T(8,128)(2,1)S(1)}, u32[]{:S(2)}, u32[]{:S(2)}) %collective-permute-start.9) | collective-permute-done | bytes 65568 | tf_op jit(solution)/shard_map/ppermute | solution.py:29
  36.7 0.1 collective-permute-start.13
  36.8 1.2 %collective-permute-done.13 = bf16[128,256]{1,0:T(8,128)(2,1)S(1)} collective-permute-done((bf16[128,256]{1,0:T(8,128)(2,1)S(1)}, bf16[128,256]{1,0:T(8,128)(2,1)S(1)}, u32[]{:S(2)}, u32[]{:S(2)}) %collective-permute-start.13) | collective-permute-done | bytes 65568 | tf_op jit(solution)/shard_map/ppermute | solution.py:18
  38.0 0.7 %convert_multiply_fusion = f32[256,256]{1,0:T(8,128)} fusion(bf16[128,256]{1,0:T(8,128)(2,1)S(1)} %get-tuple-element.56, bf16[128,256]{1,0:T(8,128)(2,1)S(1)} %get-tuple-element.55), kind=kLoop, calls=%fused_computation.4 | loop fusion | flops 327680 | bytes 393216 | tf_op jit(solution)/shard_map/mul | solution.py:288
  (6 shorter events, 0.1 us)
Async XLA Ops:
  0.6 12.0 %collective-permute-start = (bf16[512,256]{1,0:T(8,128)(2,1)}, bf16[512,256]{1,0:T(8,128)(2,1)}, u32[]{:S(2)}, u32[]{:S(2)}) collective-permute-start(bf16[512,256]{1,0:T(8,128)(2,1)} %bitcast.23), channel_id=1, source_target_pairs={{0,16},{8,24},{16,0},{24,8},{1,17},{9,25},{17,1},{25,9},{2,18},{10... | collective-permute-start | bytes 786440 | tf_op jit(solution)/shard_map/ppermute | solution.py:18
  5.9 6.0 %copy-start.8 = (s32[1,1,4,6]{3,2,1,0:T(4,128)S(1)}, s32[1,1,4,6]{3,2,1,0:T(4,128)}, u32[]{:S(2)}) copy-start(s32[1,1,4,6]{3,2,1,0:T(4,128)} %param.13) | copy-start | bytes 292
  5.9 6.7 %copy-start.1 = (bf16[1,512,256]{2,1,0:T(8,128)(2,1)S(1)}, bf16[1,512,256]{2,1,0:T(8,128)(2,1)}, u32[]{:S(2)}) copy-start(bf16[1,512,256]{2,1,0:T(8,128)(2,1)} %param.10) | copy-start | bytes 786436
  5.9 14.6 %all-to-all-start = ((bf16[8,64,256]{2,1,0:T(8,128)(2,1)}), bf16[8,64,256]{2,1,0:T(8,128)(2,1)S(1)}, u32[]{:S(2)}, u32[]{:S(2)}) async-start(bf16[8,64,256]{2,1,0:T(8,128)(2,1)} %shard_map.121.outgoing), calls=%async_computation | async-start | bytes 524288 | tf_op jit(solution)/shard_map/all_to_all | solution.py:211
  11.9 0.7 %copy-start.9 = (s32[1,1,4]{2,1,0:T(1,128)S(1)}, s32[1,1,4]{2,1,0:T(1,128)}, u32[]{:S(2)}) copy-start(s32[1,1,4]{2,1,0:T(1,128)} %param.14) | copy-start | bytes 52
  12.6 2.2 %copy-start = (bf16[1,512,256]{2,1,0:T(8,128)(2,1)S(1)}, bf16[1,512,256]{2,1,0:T(8,128)(2,1)}, u32[]{:S(2)}) copy-start(bf16[1,512,256]{2,1,0:T(8,128)(2,1)} %param.19) | copy-start | bytes 786436
  12.7 1.8 %collective-permute-start.1 = (bf16[512,256]{1,0:T(8,128)(2,1)S(1)}, bf16[512,256]{1,0:T(8,128)(2,1)S(1)}, u32[]{:S(2)}, u32[]{:S(2)}) collective-permute-start(bf16[512,256]{1,0:T(8,128)(2,1)S(1)} %bitcast.25), channel_id=1, source_target_pairs={{0,8},{8,0},{16,24},{24,16},{1,9},{9,1},{17,25},{25,17},{2,10},{10... | collective-permute-start | bytes 786440 | tf_op jit(solution)/shard_map/ppermute | solution.py:18
  12.7 2.1 %collective-permute-start.2 = (bf16[512,256]{1,0:T(8,128)(2,1)}, bf16[512,256]{1,0:T(8,128)(2,1)S(1)}, u32[]{:S(2)}, u32[]{:S(2)}) collective-permute-start(bf16[512,256]{1,0:T(8,128)(2,1)} %collective-permute-done.refs_2_), channel_id=1, source_target_pairs={{0,8},{8,0},{16,24},{24,16},{1,9},{9,1},{17,25},{25,17},{2,10},{10... | collective-permute-start | bytes 786440 | tf_op jit(solution)/shard_map/ppermute | solution.py:18
  14.8 5.7 %copy-start.2 = (bf16[8,64,256]{2,1,0:T(8,128)(2,1)S(1)}, bf16[8,64,256]{2,1,0:T(8,128)(2,1)}, u32[]{:S(2)}) copy-start(bf16[8,64,256]{2,1,0:T(8,128)(2,1)} %shard_map.121.outgoing) | copy-start | bytes 786436
  17.8 3.6 %collective-permute-start.5 = (bf16[2,256,512]{2,1,0:T(8,128)(2,1)S(1)}, bf16[2,256,512]{2,1,0:T(8,128)(2,1)S(1)}, u32[]{:S(2)}, u32[]{:S(2)}) collective-permute-start(bf16[2,256,512]{2,1,0:T(8,128)(2,1)S(1)} %get-tuple-element.40), channel_id=1, source_target_pairs={{0,8},{8,0},{16,24},{24,16},{1,9},{9,1},{17,25},{25,17},{2,10},{10... | collective-permute-start | bytes 1572872 | tf_op jit(solution)/shard_map/ppermute | solution.py:18
  20.8 1.3 %collective-permute-start.4 = (bf16[128,256]{1,0:T(8,128)(2,1)S(1)}, bf16[128,256]{1,0:T(8,128)(2,1)S(1)}, u32[]{:S(2)}, u32[]{:S(2)}) collective-permute-start(bf16[128,256]{1,0:T(8,128)(2,1)S(1)} %get-tuple-element.38), channel_id=1, source_target_pairs={{0,8},{8,0},{16,24},{24,16},{1,9},{9,1},{17,25},{25,17},{2,10},{10... | collective-permute-start | bytes 196616 | tf_op jit(solution)/shard_map/ppermute | solution.py:18
  20.9 1.4 %collective-permute-start.3 = (bf16[128,256]{1,0:T(8,128)(2,1)S(1)}, bf16[128,256]{1,0:T(8,128)(2,1)S(1)}, u32[]{:S(2)}, u32[]{:S(2)}) collective-permute-start(bf16[128,256]{1,0:T(8,128)(2,1)S(1)} %get-tuple-element.35), channel_id=1, source_target_pairs={{0,8},{8,0},{16,24},{24,16},{1,9},{9,1},{17,25},{25,17},{2,10},{10... | collective-permute-start | bytes 196616 | tf_op jit(solution)/shard_map/ppermute | solution.py:18
  22.3 4.1 %copy-start.3 = (bf16[256,256]{1,0:T(8,128)(2,1)S(1)}, bf16[256,256]{1,0:T(8,128)(2,1)}, u32[]{:S(2)}) copy-start(bf16[256,256]{1,0:T(8,128)(2,1)} %weight.3) | copy-start | bytes 393220
  22.3 4.1 %copy-start.5 = (s32[1,1,8,32]{3,2,1,0:T(8,128)S(1)}, s32[1,1,8,32]{3,2,1,0:T(8,128)}, u32[]{:S(2)}) copy-start(s32[1,1,8,32]{3,2,1,0:T(8,128)} %param.17) | copy-start | bytes 3076
  22.3 4.1 %copy-start.6 = (f32[1,1,8,32]{3,2,1,0:T(8,128)S(1)}, f32[1,1,8,32]{3,2,1,0:T(8,128)}, u32[]{:S(2)}) copy-start(f32[1,1,8,32]{3,2,1,0:T(8,128)} %param.18) | copy-start | bytes 3076
  22.3 5.9 %collective-permute-start.6 = (bf16[128,256]{1,0:T(8,128)(2,1)S(1)}, bf16[128,256]{1,0:T(8,128)(2,1)S(1)}, u32[]{:S(2)}, u32[]{:S(2)}) collective-permute-start(bf16[128,256]{1,0:T(8,128)(2,1)S(1)} %add_convert_fusion.2), channel_id=1, source_target_pairs={{0,4},{1,5},{2,6},{3,7},{4,0},{5,1},{6,2},{7,3},{8,24},{9,25},{10,... | collective-permute-start | bytes 196616 | tf_op jit(solution)/shard_map/ppermute | solution.py:29
  23.4 6.2 %collective-permute-start.7 = (bf16[128,256]{1,0:T(8,128)(2,1)S(1)}, bf16[128,256]{1,0:T(8,128)(2,1)S(1)}, u32[]{:S(2)}, u32[]{:S(2)}) collective-permute-start(bf16[128,256]{1,0:T(8,128)(2,1)S(1)} %add_convert_fusion.2), channel_id=1, source_target_pairs={{0,6},{1,7},{2,4},{3,5},{4,2},{5,3},{6,0},{7,1},{8,25},{9,24},{10,... | collective-permute-start | bytes 196616 | tf_op jit(solution)/shard_map/ppermute | solution.py:29
  25.8 4.5 %collective-permute-start.8 = (bf16[128,256]{1,0:T(8,128)(2,1)S(1)}, bf16[128,256]{1,0:T(8,128)(2,1)S(1)}, u32[]{:S(2)}, u32[]{:S(2)}) collective-permute-start(bf16[128,256]{1,0:T(8,128)(2,1)S(1)} %add_convert_fusion.2), channel_id=1, source_target_pairs={{0,2},{1,3},{2,0},{3,1},{4,6},{5,7},{6,4},{7,5},{8,9},{9,8},{10,11... | collective-permute-start | bytes 196616 | tf_op jit(solution)/shard_map/ppermute | solution.py:29
  25.9 8.1 %collective-permute-start.12 = (bf16[256,512]{1,0:T(8,128)(2,1)S(1)}, bf16[256,512]{1,0:T(8,128)(2,1)S(1)}, u32[]{:S(2)}, u32[]{:S(2)}) collective-permute-start(bf16[256,512]{1,0:T(8,128)(2,1)S(1)} %fusion), channel_id=1, source_target_pairs={{0,16},{8,24},{16,0},{24,8},{1,17},{9,25},{17,1},{25,9},{2,18},{10... | collective-permute-start | bytes 786440 | tf_op jit(solution)/shard_map/ppermute | solution.py:18
  30.3 3.6 %copy-start.4 = (s32[1,1,8,32]{3,2,1,0:T(8,128)S(1)}, s32[1,1,8,32]{3,2,1,0:T(8,128)}, u32[]{:S(2)}) copy-start(s32[1,1,8,32]{3,2,1,0:T(8,128)} %param.15) | copy-start | bytes 3076
  30.3 3.6 %copy-start.7 = (s32[1,1,8]{2,1,0:T(1,128)S(1)}, s32[1,1,8]{2,1,0:T(1,128)}, u32[]{:S(2)}) copy-start(s32[1,1,8]{2,1,0:T(1,128)} %param.16) | copy-start | bytes 100
  30.4 5.3 %collective-permute-start.10 = (bf16[128,256]{1,0:T(8,128)(2,1)S(1)}, bf16[128,256]{1,0:T(8,128)(2,1)S(1)}, u32[]{:S(2)}, u32[]{:S(2)}) collective-permute-start(bf16[128,256]{1,0:T(8,128)(2,1)S(1)} %add_convert_fusion.1), channel_id=1, source_target_pairs={{0,17},{1,16},{2,19},{3,18},{4,21},{5,20},{6,23},{7,22},{8,14},{9,... | collective-permute-start | bytes 196616 | tf_op jit(solution)/shard_map/ppermute | solution.py:29
  31.2 4.4 %collective-permute-start.11 = (bf16[128,256]{1,0:T(8,128)(2,1)S(1)}, bf16[128,256]{1,0:T(8,128)(2,1)S(1)}, u32[]{:S(2)}, u32[]{:S(2)}) collective-permute-start(bf16[128,256]{1,0:T(8,128)(2,1)S(1)} %add_convert_fusion.1), channel_id=1, source_target_pairs={{0,1},{1,0},{2,3},{3,2},{4,5},{5,4},{6,7},{7,6},{8,10},{9,11},{10,... | collective-permute-start | bytes 196616 | tf_op jit(solution)/shard_map/ppermute | solution.py:29
  32.4 4.3 %collective-permute-start.9 = (bf16[128,256]{1,0:T(8,128)(2,1)S(1)}, bf16[128,256]{1,0:T(8,128)(2,1)S(1)}, u32[]{:S(2)}, u32[]{:S(2)}) collective-permute-start(bf16[128,256]{1,0:T(8,128)(2,1)S(1)} %add_convert_fusion.1), channel_id=1, source_target_pairs={{0,16},{1,17},{2,18},{3,19},{4,20},{5,21},{6,22},{7,23},{8,12},{9,... | collective-permute-start | bytes 196616 | tf_op jit(solution)/shard_map/ppermute | solution.py:29
  36.7 1.3 %collective-permute-start.13 = (bf16[128,256]{1,0:T(8,128)(2,1)S(1)}, bf16[128,256]{1,0:T(8,128)(2,1)S(1)}, u32[]{:S(2)}, u32[]{:S(2)}) collective-permute-start(bf16[128,256]{1,0:T(8,128)(2,1)S(1)} %add_convert_fusion), channel_id=1, source_target_pairs={{0,8},{8,0},{16,24},{24,16},{1,9},{9,1},{17,25},{25,17},{2,10},{10... | collective-permute-start | bytes 196616 | tf_op jit(solution)/shard_map/ppermute | solution.py:18

commit v8 on v7

--- a/solution.py
+++ b/solution.py
@@ -88,7 +88,7 @@
 
 def adjacency_kernel(groups, blk, spots, tiles, grad, *refs):
     panels, refs = refs[:groups], refs[groups:]
-    (local, kept, sent, send, *keep), (dense, term) = refs[:-2], refs[-2:]
+    (local, term, send, *keep), dense = refs[:-1], refs[-1]
     unused, slots, tile, unused = tiles.shape
     rows, width = grad.shape
     dense[...] = jnp.zeros_like(dense)
@@ -111,7 +111,6 @@
     rounded = value.astype(BF16)
     local[...] = rounded
     term[...] = matmul(rounded, grad[...], 0, 0)
-    split_halves(blk, term, kept, sent)
 
 
 def weights_of(rows, owner, edge):
@@ -124,11 +123,11 @@
     return matmul(weights_of(rows, owner, edge), received, 1, 0)
 
 
-def halo_term_kernel(blk, halo, outgoing, kept, sent, term):
+def halo_term_kernel(blk, near, halo, outgoing, kept, sent, term):
     peers, both, width = halo.shape
     received = halo[:, : both // 2, :].reshape(-1, width)
     weighted = outgoing[:, both // 2 :, :].reshape(-1, width)
-    term[...] = matmul(received, weighted, 0, 0)
+    term[...] = near[...] + matmul(received, weighted, 0, 0)
     split_halves(blk, term, kept, sent)
 
 
@@ -223,25 +222,24 @@
     live = jnp.arange(tiles.shape[3])[None, :] < tile_count[0, 0][:, None]
     live_tiles = jnp.where(live[..., None, None], tile_set, jnp.zeros((), BF16))
     spots = jnp.stack([place // per, place % per]) * tile
-    local, kept, sent, send, *keep = call(
+    local, near_term, send, *keep = call(
         functools.partial(adjacency_kernel, groups),
-        [((rows, width), BF16), half_term, half_term, ((half, width, rows), BF16)]
+        [((rows, width), BF16), ((width, width), F32), ((half, width, rows), BF16)]
         + [((width, rows), BF16)] * half,
         [SMEM] * 2 + [VMEM] * (2 + groups),
         40 * MIB,
-        [pltpu.VMEM((rows, groups * rows), BF16), pltpu.VMEM((width, width), F32)],
+        [pltpu.VMEM((rows, groups * rows), BF16)],
     )(blk, spots, live_tiles, grad, *[panels[j] for j in range(groups)])
     got = swap(send, "blk", 1)
 
-    near_term = (kept, swap(sent, "blk", 1))
     kept, sent = call(
         halo_term_kernel,
         [half_term, half_term],
-        [SMEM] + [VMEM] * 2,
+        [SMEM] + [VMEM] * 3,
         16 * MIB,
         [pltpu.VMEM((width, width), F32)],
         flops=2 * 10**10,
-    )(blk, halo, outgoing)
+    )(blk, near_term, halo, outgoing)
     other = swap(sent, "blk", 1)
     inner = bits_of(groups)[1:]
     for bit in inner:
@@ -253,7 +251,7 @@
         else:
             keep = [add(keep[j], got[j]) for j in range(0, len(keep), 2)]
             got = swap(jnp.stack(later), "blk", bit)
-    term = add(*near_term, kept, other)
+    term = add(kept, other)
     bits = [("dom", bit) for bit in bits_of(peers)]
     bits = bits[1:] + bits[:1] + [("blk", bit) for bit in inner]
     fours = [bits[i : i + 2] for i in range(0, len(bits), 2)]
@@ -269,13 +267,14 @@
                 backward_kernel, [((rows, width), BF16)], [SMEM] + [VMEM] * 6, 16 * MIB
             )(send_live, keep[0], got, third, halo, sends, weight)
         mate = fours[i ^ 1] if i ^ 1 < len(fours) and len(fours[i ^ 1]) == len(four) else four
-        ways = [slice(1, 2), slice(0, 2), slice(0, 1)] if len(four) == 2 else [slice(0, 1)]
+        ways = [slice(0, 1), slice(1, 2), slice(0, 2)] if last else [slice(1, 2), slice(0, 2), slice(0, 1)]
+        ways = ways if len(four) == 2 else [slice(0, 1)]
         others = [swap_bits(term, four[way], mate[way]) for way in ways]
         if first:
             others, layer_out = lax.optimization_barrier((others, layer_out))
         if last:
             others, feature_grad = lax.optimization_barrier((others, feature_grad))
-        others = others[-1:] + others[:-1]
+        others = [others[ways.index(way)] for way in sorted(ways, key=str)]
         wide = [value.astype(F32) for value in (term, *others)]
         total = wide[0] + wide[1]
         if len(four) == 2:

time: 39.1 us -> 38.9 us (level)
  starting transfers between devices: 18 us -> 17.5 us
    ppermute x8 -> x7, starting transfers between devices: 4.94 us -> 4.45 us  [swap(): lax.ppermute(value, axis, [(i, i ^ bit) for i in range(lax.axis_size(axis...]
    ppermute x8 -> x7, waiting for transfers between devices: 2.41 us -> 2.73 us  [swap(): lax.ppermute(value, axis, [(i, i ^ bit) for i in range(lax.axis_size(axis...]
  transfers between devices with their start and end apart: 15 -> 14, of which waited for: 9 -> 8; matrix products, arithmetic and copies ran while one was open for 4% -> 4% of each run, Pallas kernels for 21% -> 21%
where the time goes in v8:
time: 38.9 us; the launch traced here: 38.6 us
  starting transfers between devices  17.5 us (45%)
  waiting for transfers between devices  9.07 us (23%)
  Pallas kernels  8.27 us (21%)
  other arithmetic  2.24 us (6%)
  between operations  0.81 us (2%)
  local copies, waits for them, and re-layouts  0.69 us (2%)
    ppermute x6, starting transfers between devices, swap_bits(): return lax.ppermute(value, ('blk', 'dom'), pairs)  7.11 us
    all_to_all x1, starting transfers between devices, on_device(): lax.all_to_all(outgoing, 'dom', split_axis=0, concat_axis=0, tiled=True)  5.95 us
    ppermute x7, starting transfers between devices, swap(): lax.ppermute(value, axis, [(i, i ^ bit) for i in range(lax.axis_size(axis...  4.45 us
    ppermute x6, waiting for transfers between devices, swap_bits(): return lax.ppermute(value, ('blk', 'dom'), pairs)  3.8 us
    pallas_call x1, Pallas kernels, on_device(): call(functools.partial(adjacency_kernel, groups), [((rows, width), BF16),...  2.9 us
    ppermute x7, waiting for transfers between devices, swap(): lax.ppermute(value, axis, [(i, i ^ bit) for i in range(lax.axis_size(axis...  2.73 us
    all_to_all x1, waiting for transfers between devices, on_device(): lax.all_to_all(outgoing, 'dom', split_axis=0, concat_axis=0, tiled=True)  2.55 us
    pallas_call x1, Pallas kernels, on_device(): call(halo_kernel, [((peers, 2 * slots, width), BF16)], [HBM] * 6, 64 * MI...  2.23 us
  transfers between devices with their start and end apart: 14, of which 8 were waited for; matrix products, arithmetic and copies ran while one was open for 4% of the time, Pallas kernels for 21%

profile of v8, /device:TPU:0, one launch (start us, length us, event | category | flops | bytes accessed | tf_op | source)
XLA Modules:
  0.0 38.6 jit_solution(8452881575688637766)
XLA Ops:
  0.6 3.0 %collective-permute-start = (bf16[512,256]{1,0:T(8,128)(2,1)}, bf16[512,256]{1,0:T(8,128)(2,1)}, u32[]{:S(2)}, u32[]{:S(2)}) collective-permute-start(bf16[512,256]{1,0:T(8,128)(2,1)} %bitcast.23), channel_id=1, source_target_pairs={{0,16},{8,24},{16,0},{24,8},{1,17},{9,25},{17,1},{25,9},{2,18},{10... | collective-permute-start | bytes 786440 | tf_op jit(solution)/shard_map/ppermute | solution.py:18
  3.7 2.2 %shard_map.121.outgoing = bf16[8,64,256]{2,1,0:T(8,128)(2,1)} custom-call(bf16[512,256]{1,0:T(8,128)(2,1)} %bitcast.24, bf16[512,256]{1,0:T(8,128)(2,1)} %bitcast.21, s32[8,32]{1,0:T(8,128)} %bitcast.27, s32[8]{0:T(128)} %bitcast.33, s32[8,32]{1,0:T(8,128)} %bitcast.29, f32[8,32]{1,0:T(8,128)} %bitcast.31), custom_call_target="tpu_custom_call" | custom-call | flops 1 | bytes 1 | tf_op jit(solution)/shard_map/pallas_call | solution.py:192
  5.9 0.0 copy-start.8
  5.9 0.0 copy-start.1
  5.9 5.9 %all-to-all-start = ((bf16[8,64,256]{2,1,0:T(8,128)(2,1)}), bf16[8,64,256]{2,1,0:T(8,128)(2,1)S(1)}, u32[]{:S(2)}, u32[]{:S(2)}) async-start(bf16[8,64,256]{2,1,0:T(8,128)(2,1)} %shard_map.121.outgoing), calls=%async_computation | async-start | bytes 524288 | tf_op jit(solution)/shard_map/all_to_all | solution.py:210
  11.9 0.0 copy-done.8
  11.9 0.0 copy-start.9
  11.9 0.6 %copy-done.9 = s32[1,1,4]{2,1,0:T(1,128)S(1)} copy-done((s32[1,1,4]{2,1,0:T(1,128)S(1)}, s32[1,1,4]{2,1,0:T(1,128)}, u32[]{:S(2)}) %copy-start.9) | copy-done | bytes 40
  12.6 0.1 iota_compare_fusion
  12.6 0.0 copy-start
  12.6 0.0 collective-permute-done.refs_2_
  12.6 0.0 copy-done.1
  12.7 0.1 collective-permute-start.1
  12.7 0.5 %collective-permute-start.2 = (bf16[512,256]{1,0:T(8,128)(2,1)}, bf16[512,256]{1,0:T(8,128)(2,1)S(1)}, u32[]{:S(2)}, u32[]{:S(2)}) collective-permute-start(bf16[512,256]{1,0:T(8,128)(2,1)} %collective-permute-done.refs_2_), channel_id=1, source_target_pairs={{0,8},{8,0},{16,24},{24,16},{1,9},{9,1},{17,25},{25,17},{2,10},{10... | collective-permute-start | bytes 786440 | tf_op jit(solution)/shard_map/ppermute | solution.py:18
  13.2 1.3 %broadcast_select_fusion.tiles = bf16[4,6,128,128]{3,2,1,0:T(8,128)(2,1)S(1)} fusion(bf16[4,6,128,128]{3,2,1,0:T(8,128)(2,1)} %bitcast.35, pred[4,6]{1,0:T(4,128)(4,1)S(1)} %iota_compare_fusion), kind=kLoop, calls=%fused_computation | loop fusion | flops 393216 | bytes 1572888 | tf_op jit(solution)/shard_map/jit(_where)/select_n | solution.py:223
  14.5 0.0 collective-permute-done.1.refs_1_
  14.5 0.3 collective-permute-done.2.refs_3_
  14.8 0.0 copy-done
  14.8 0.0 copy-start.2
  14.8 2.9 %shard_map.122 = (bf16[512,256]{1,0:T(8,128)(2,1)S(1)}, f32[256,256]{1,0:T(8,128)S(1)}, bf16[2,256,512]{2,1,0:T(8,128)(2,1)S(1)}, bf16[256,512]{1,0:T(8,128)(2,1)S(1)}, bf16[256,512]{1,0:T(8,128)(2,1)S(1)}) custom-call(s32[1]{0:T(128)} %bitcast.blk, s32[2,4,6]{2,1,0:T(4,128)S(1)} %add_multiply_fusion.spots, ...), custom_call_target="tpu_custom_call" | custom-call | flops 1 | bytes 1 | tf_op jit(solution)/shard_map/pallas_call | solution.py:225
  17.8 0.2 collective-permute-start.4
  18.0 2.5 %all-to-all-done.halo = bf16[8,64,256]{2,1,0:T(8,128)(2,1)S(1)} async-done(((bf16[8,64,256]{2,1,0:T(8,128)(2,1)}), bf16[8,64,256]{2,1,0:T(8,128)(2,1)S(1)}, u32[]{:S(2)}, u32[]{:S(2)}) %all-to-all-start) | async-done | bytes 262176 | tf_op jit(solution)/shard_map/all_to_all | solution.py:210
  20.5 0.0 copy-done.2
  20.5 0.3 shard_map.123
  20.8 0.1 collective-permute-start.3
  20.9 0.0 collective-permute-done.4.others
  20.9 0.1 fusion
  20.9 0.0 copy-start.3
  21.0 1.1 %collective-permute-done.3 = bf16[128,256]{1,0:T(8,128)(2,1)S(1)} collective-permute-done((bf16[128,256]{1,0:T(8,128)(2,1)S(1)}, bf16[128,256]{1,0:T(8,128)(2,1)S(1)}, u32[]{:S(2)}, u32[]{:S(2)}) %collective-permute-start.3) | collective-permute-done | bytes 65568 | tf_op jit(solution)/shard_map/ppermute | solution.py:18
  22.1 0.0 copy-start.5
  22.1 0.0 copy-start.6
  22.1 1.1 %collective-permute-start.5 = (bf16[128,256]{1,0:T(8,128)(2,1)S(1)}, bf16[128,256]{1,0:T(8,128)(2,1)S(1)}, u32[]{:S(2)}, u32[]{:S(2)}) collective-permute-start(bf16[128,256]{1,0:T(8,128)(2,1)S(1)} %add_convert_fusion.2), channel_id=1, source_target_pairs={{0,4},{1,5},{2,6},{3,7},{4,0},{5,1},{6,2},{7,3},{8,24},{9,25},{10,... | collective-permute-start | bytes 196616 | tf_op jit(solution)/shard_map/ppermute | solution.py:29
  23.3 2.4 %collective-permute-start.6 = (bf16[128,256]{1,0:T(8,128)(2,1)S(1)}, bf16[128,256]{1,0:T(8,128)(2,1)S(1)}, u32[]{:S(2)}, u32[]{:S(2)}) collective-permute-start(bf16[128,256]{1,0:T(8,128)(2,1)S(1)} %add_convert_fusion.2), channel_id=1, source_target_pairs={{0,6},{1,7},{2,4},{3,5},{4,2},{5,3},{6,0},{7,1},{8,25},{9,24},{10,... | collective-permute-start | bytes 196616 | tf_op jit(solution)/shard_map/ppermute | solution.py:29
  25.7 0.0 collective-permute-start.7
  25.7 0.5 %collective-permute-start.11 = (bf16[256,512]{1,0:T(8,128)(2,1)S(1)}, bf16[256,512]{1,0:T(8,128)(2,1)S(1)}, u32[]{:S(2)}, u32[]{:S(2)}) collective-permute-start(bf16[256,512]{1,0:T(8,128)(2,1)S(1)} %fusion), channel_id=1, source_target_pairs={{0,16},{8,24},{16,0},{24,8},{1,17},{9,25},{17,1},{25,9},{2,18},{10... | collective-permute-start | bytes 786440 | tf_op jit(solution)/shard_map/ppermute | solution.py:18
  26.2 0.0 copy-done.3
  26.2 0.0 copy-done.5
  26.2 0.0 copy-done.6
  26.2 1.2 %shard_map.124 = bf16[512,256]{1,0:T(8,128)(2,1)} custom-call(bf16[512,256]{1,0:T(8,128)(2,1)S(1)} %get-tuple-element.42.local, bf16[8,64,256]{2,1,0:T(8,128)(2,1)S(1)} %all-to-all-done.halo, s32[8,32]{1,0:T(8,128)S(1)} %bitcast.30, f32[8,32]{1,0:T(8,128)S(1)} %bitcast.32, bf16[256,256]{1,0:T(8,128)(2,1)S(1)} %copy-done.3), custom_call_target="tpu_custom_call" | custom-call | flops 20000000000 | bytes 1 | tf_op jit(solution)/shard_map/pallas_call | solution.py:262
  27.4 0.7 %collective-permute-done.5 = bf16[128,256]{1,0:T(8,128)(2,1)S(1)} collective-permute-done((bf16[128,256]{1,0:T(8,128)(2,1)S(1)}, bf16[128,256]{1,0:T(8,128)(2,1)S(1)}, u32[]{:S(2)}, u32[]{:S(2)}) %collective-permute-start.5) | collective-permute-done | bytes 65568 | tf_op jit(solution)/shard_map/ppermute | solution.py:29
  28.1 1.4 %collective-permute-done.6 = bf16[128,256]{1,0:T(8,128)(2,1)S(1)} collective-permute-done((bf16[128,256]{1,0:T(8,128)(2,1)S(1)}, bf16[128,256]{1,0:T(8,128)(2,1)S(1)}, u32[]{:S(2)}, u32[]{:S(2)}) %collective-permute-start.6) | collective-permute-done | bytes 65568 | tf_op jit(solution)/shard_map/ppermute | solution.py:29
  29.4 0.7 %collective-permute-done.7 = bf16[128,256]{1,0:T(8,128)(2,1)S(1)} collective-permute-done((bf16[128,256]{1,0:T(8,128)(2,1)S(1)}, bf16[128,256]{1,0:T(8,128)(2,1)S(1)}, u32[]{:S(2)}, u32[]{:S(2)}) %collective-permute-start.7) | collective-permute-done | bytes 65568 | tf_op jit(solution)/shard_map/ppermute | solution.py:29
  30.1 0.0 copy-start.4
  30.2 0.0 copy-start.7
  30.2 0.9 %collective-permute-start.10 = (bf16[128,256]{1,0:T(8,128)(2,1)S(1)}, bf16[128,256]{1,0:T(8,128)(2,1)S(1)}, u32[]{:S(2)}, u32[]{:S(2)}) collective-permute-start(bf16[128,256]{1,0:T(8,128)(2,1)S(1)} %add_convert_fusion.1), channel_id=1, source_target_pairs={{0,17},{1,16},{2,19},{3,18},{4,21},{5,20},{6,23},{7,22},{8,14},{9,... | collective-permute-start | bytes 196616 | tf_op jit(solution)/shard_map/ppermute | solution.py:29
  31.1 1.2 %collective-permute-start.8 = (bf16[128,256]{1,0:T(8,128)(2,1)S(1)}, bf16[128,256]{1,0:T(8,128)(2,1)S(1)}, u32[]{:S(2)}, u32[]{:S(2)}) collective-permute-start(bf16[128,256]{1,0:T(8,128)(2,1)S(1)} %add_convert_fusion.1), channel_id=1, source_target_pairs={{0,1},{1,0},{2,3},{3,2},{4,5},{5,4},{6,7},{7,6},{8,10},{9,11},{10,... | collective-permute-start | bytes 196616 | tf_op jit(solution)/shard_map/ppermute | solution.py:29
  32.2 1.5 %collective-permute-start.9 = (bf16[128,256]{1,0:T(8,128)(2,1)S(1)}, bf16[128,256]{1,0:T(8,128)(2,1)S(1)}, u32[]{:S(2)}, u32[]{:S(2)}) collective-permute-start(bf16[128,256]{1,0:T(8,128)(2,1)S(1)} %add_convert_fusion.1), channel_id=1, source_target_pairs={{0,16},{1,17},{2,18},{3,19},{4,20},{5,21},{6,22},{7,23},{8,12},{9,... | collective-permute-start | bytes 196616 | tf_op jit(solution)/shard_map/ppermute | solution.py:29
  33.7 0.0 collective-permute-done.11.third
  33.7 0.0 copy-done.4
  33.7 0.0 copy-done.7
  33.7 1.7 %shard_map.125 = bf16[512,256]{1,0:T(8,128)(2,1)} custom-call(s32[8]{0:T(128)S(1)} %bitcast.34, bf16[256,512]{1,0:T(8,128)(2,1)S(1)} %get-tuple-element.47.first, bf16[2,256,512]{2,1,0:T(8,128)(2,1)S(1)} %collective-permute-done.4.others, bf16[256,512]{1,0:T(8,128)(2,1)S(1)} %collective-permute-done.11.third, bf16[8,64,256]{2,1,0:T(8,128)(2,1)S(1)} %all-to-all-done.halo, ...), custom_call_target="tpu_custom_call" | custom-call | flops 1 | bytes 1 | tf_op jit(solution)/shard_map/pallas_call | solution.py:266
  35.5 0.0 collective-permute-done.10
  35.5 0.0 collective-permute-done.8
  35.5 1.0 %collective-permute-done.9 = bf16[128,256]{1,0:T(8,128)(2,1)S(1)} collective-permute-done((bf16[128,256]{1,0:T(8,128)(2,1)S(1)}, bf16[128,256]{1,0:T(8,128)(2,1)S(1)}, u32[]{:S(2)}, u32[]{:S(2)}) %collective-permute-start.9) | collective-permute-done | bytes 65568 | tf_op jit(solution)/shard_map/ppermute | solution.py:29
  36.5 0.1 collective-permute-start.12
  36.6 1.2 %collective-permute-done.12 = bf16[128,256]{1,0:T(8,128)(2,1)S(1)} collective-permute-done((bf16[128,256]{1,0:T(8,128)(2,1)S(1)}, bf16[128,256]{1,0:T(8,128)(2,1)S(1)}, u32[]{:S(2)}, u32[]{:S(2)}) %collective-permute-start.12) | collective-permute-done | bytes 65568 | tf_op jit(solution)/shard_map/ppermute | solution.py:18
  37.9 0.7 %convert_multiply_fusion = f32[256,256]{1,0:T(8,128)} fusion(bf16[128,256]{1,0:T(8,128)(2,1)S(1)} %get-tuple-element.54, bf16[128,256]{1,0:T(8,128)(2,1)S(1)} %get-tuple-element.53), kind=kLoop, calls=%fused_computation.4 | loop fusion | flops 327680 | bytes 393216 | tf_op jit(solution)/shard_map/mul | solution.py:287
  (6 shorter events, 0.1 us)
Async XLA Ops:
  0.6 12.0 %collective-permute-start = (bf16[512,256]{1,0:T(8,128)(2,1)}, bf16[512,256]{1,0:T(8,128)(2,1)}, u32[]{:S(2)}, u32[]{:S(2)}) collective-permute-start(bf16[512,256]{1,0:T(8,128)(2,1)} %bitcast.23), channel_id=1, source_target_pairs={{0,16},{8,24},{16,0},{24,8},{1,17},{9,25},{17,1},{25,9},{2,18},{10... | collective-permute-start | bytes 786440 | tf_op jit(solution)/shard_map/ppermute | solution.py:18
  5.9 6.0 %copy-start.8 = (s32[1,1,4,6]{3,2,1,0:T(4,128)S(1)}, s32[1,1,4,6]{3,2,1,0:T(4,128)}, u32[]{:S(2)}) copy-start(s32[1,1,4,6]{3,2,1,0:T(4,128)} %param.13) | copy-start | bytes 292
  5.9 6.7 %copy-start.1 = (bf16[1,512,256]{2,1,0:T(8,128)(2,1)S(1)}, bf16[1,512,256]{2,1,0:T(8,128)(2,1)}, u32[]{:S(2)}) copy-start(bf16[1,512,256]{2,1,0:T(8,128)(2,1)} %param.10) | copy-start | bytes 786436
  5.9 14.6 %all-to-all-start = ((bf16[8,64,256]{2,1,0:T(8,128)(2,1)}), bf16[8,64,256]{2,1,0:T(8,128)(2,1)S(1)}, u32[]{:S(2)}, u32[]{:S(2)}) async-start(bf16[8,64,256]{2,1,0:T(8,128)(2,1)} %shard_map.121.outgoing), calls=%async_computation | async-start | bytes 524288 | tf_op jit(solution)/shard_map/all_to_all | solution.py:210
  11.9 0.7 %copy-start.9 = (s32[1,1,4]{2,1,0:T(1,128)S(1)}, s32[1,1,4]{2,1,0:T(1,128)}, u32[]{:S(2)}) copy-start(s32[1,1,4]{2,1,0:T(1,128)} %param.14) | copy-start | bytes 52
  12.6 2.2 %copy-start = (bf16[1,512,256]{2,1,0:T(8,128)(2,1)S(1)}, bf16[1,512,256]{2,1,0:T(8,128)(2,1)}, u32[]{:S(2)}) copy-start(bf16[1,512,256]{2,1,0:T(8,128)(2,1)} %param.19) | copy-start | bytes 786436
  12.7 1.8 %collective-permute-start.1 = (bf16[512,256]{1,0:T(8,128)(2,1)S(1)}, bf16[512,256]{1,0:T(8,128)(2,1)S(1)}, u32[]{:S(2)}, u32[]{:S(2)}) collective-permute-start(bf16[512,256]{1,0:T(8,128)(2,1)S(1)} %bitcast.25), channel_id=1, source_target_pairs={{0,8},{8,0},{16,24},{24,16},{1,9},{9,1},{17,25},{25,17},{2,10},{10... | collective-permute-start | bytes 786440 | tf_op jit(solution)/shard_map/ppermute | solution.py:18
  12.7 2.1 %collective-permute-start.2 = (bf16[512,256]{1,0:T(8,128)(2,1)}, bf16[512,256]{1,0:T(8,128)(2,1)S(1)}, u32[]{:S(2)}, u32[]{:S(2)}) collective-permute-start(bf16[512,256]{1,0:T(8,128)(2,1)} %collective-permute-done.refs_2_), channel_id=1, source_target_pairs={{0,8},{8,0},{16,24},{24,16},{1,9},{9,1},{17,25},{25,17},{2,10},{10... | collective-permute-start | bytes 786440 | tf_op jit(solution)/shard_map/ppermute | solution.py:18
  14.8 5.7 %copy-start.2 = (bf16[8,64,256]{2,1,0:T(8,128)(2,1)S(1)}, bf16[8,64,256]{2,1,0:T(8,128)(2,1)}, u32[]{:S(2)}) copy-start(bf16[8,64,256]{2,1,0:T(8,128)(2,1)} %shard_map.121.outgoing) | copy-start | bytes 786436
  17.8 3.1 %collective-permute-start.4 = (bf16[2,256,512]{2,1,0:T(8,128)(2,1)S(1)}, bf16[2,256,512]{2,1,0:T(8,128)(2,1)S(1)}, u32[]{:S(2)}, u32[]{:S(2)}) collective-permute-start(bf16[2,256,512]{2,1,0:T(8,128)(2,1)S(1)} %get-tuple-element.38), channel_id=1, source_target_pairs={{0,8},{8,0},{16,24},{24,16},{1,9},{9,1},{17,25},{25,17},{2,10},{10... | collective-permute-start | bytes 1572872 | tf_op jit(solution)/shard_map/ppermute | solution.py:18
  20.8 1.3 %collective-permute-start.3 = (bf16[128,256]{1,0:T(8,128)(2,1)S(1)}, bf16[128,256]{1,0:T(8,128)(2,1)S(1)}, u32[]{:S(2)}, u32[]{:S(2)}) collective-permute-start(bf16[128,256]{1,0:T(8,128)(2,1)S(1)} %get-tuple-element.36), channel_id=1, source_target_pairs={{0,8},{8,0},{16,24},{24,16},{1,9},{9,1},{17,25},{25,17},{2,10},{10... | collective-permute-start | bytes 196616 | tf_op jit(solution)/shard_map/ppermute | solution.py:18
  20.9 5.2 %copy-start.3 = (bf16[256,256]{1,0:T(8,128)(2,1)S(1)}, bf16[256,256]{1,0:T(8,128)(2,1)}, u32[]{:S(2)}) copy-start(bf16[256,256]{1,0:T(8,128)(2,1)} %weight.3) | copy-start | bytes 393220
  22.1 4.1 %copy-start.5 = (s32[1,1,8,32]{3,2,1,0:T(8,128)S(1)}, s32[1,1,8,32]{3,2,1,0:T(8,128)}, u32[]{:S(2)}) copy-start(s32[1,1,8,32]{3,2,1,0:T(8,128)} %param.17) | copy-start | bytes 3076
  22.1 4.1 %copy-start.6 = (f32[1,1,8,32]{3,2,1,0:T(8,128)S(1)}, f32[1,1,8,32]{3,2,1,0:T(8,128)}, u32[]{:S(2)}) copy-start(f32[1,1,8,32]{3,2,1,0:T(8,128)} %param.18) | copy-start | bytes 3076
  22.1 5.9 %collective-permute-start.5 = (bf16[128,256]{1,0:T(8,128)(2,1)S(1)}, bf16[128,256]{1,0:T(8,128)(2,1)S(1)}, u32[]{:S(2)}, u32[]{:S(2)}) collective-permute-start(bf16[128,256]{1,0:T(8,128)(2,1)S(1)} %add_convert_fusion.2), channel_id=1, source_target_pairs={{0,4},{1,5},{2,6},{3,7},{4,0},{5,1},{6,2},{7,3},{8,24},{9,25},{10,... | collective-permute-start | bytes 196616 | tf_op jit(solution)/shard_map/ppermute | solution.py:29
  23.3 6.2 %collective-permute-start.6 = (bf16[128,256]{1,0:T(8,128)(2,1)S(1)}, bf16[128,256]{1,0:T(8,128)(2,1)S(1)}, u32[]{:S(2)}, u32[]{:S(2)}) collective-permute-start(bf16[128,256]{1,0:T(8,128)(2,1)S(1)} %add_convert_fusion.2), channel_id=1, source_target_pairs={{0,6},{1,7},{2,4},{3,5},{4,2},{5,3},{6,0},{7,1},{8,25},{9,24},{10,... | collective-permute-start | bytes 196616 | tf_op jit(solution)/shard_map/ppermute | solution.py:29
  25.7 4.5 %collective-permute-start.7 = (bf16[128,256]{1,0:T(8,128)(2,1)S(1)}, bf16[128,256]{1,0:T(8,128)(2,1)S(1)}, u32[]{:S(2)}, u32[]{:S(2)}) collective-permute-start(bf16[128,256]{1,0:T(8,128)(2,1)S(1)} %add_convert_fusion.2), channel_id=1, source_target_pairs={{0,2},{1,3},{2,0},{3,1},{4,6},{5,7},{6,4},{7,5},{8,9},{9,8},{10,11... | collective-permute-start | bytes 196616 | tf_op jit(solution)/shard_map/ppermute | solution.py:29
  25.7 8.1 %collective-permute-start.11 = (bf16[256,512]{1,0:T(8,128)(2,1)S(1)}, bf16[256,512]{1,0:T(8,128)(2,1)S(1)}, u32[]{:S(2)}, u32[]{:S(2)}) collective-permute-start(bf16[256,512]{1,0:T(8,128)(2,1)S(1)} %fusion), channel_id=1, source_target_pairs={{0,16},{8,24},{16,0},{24,8},{1,17},{9,25},{17,1},{25,9},{2,18},{10... | collective-permute-start | bytes 786440 | tf_op jit(solution)/shard_map/ppermute | solution.py:18
  30.1 3.6 %copy-start.4 = (s32[1,1,8,32]{3,2,1,0:T(8,128)S(1)}, s32[1,1,8,32]{3,2,1,0:T(8,128)}, u32[]{:S(2)}) copy-start(s32[1,1,8,32]{3,2,1,0:T(8,128)} %param.15) | copy-start | bytes 3076
  30.2 3.6 %copy-start.7 = (s32[1,1,8]{2,1,0:T(1,128)S(1)}, s32[1,1,8]{2,1,0:T(1,128)}, u32[]{:S(2)}) copy-start(s32[1,1,8]{2,1,0:T(1,128)} %param.16) | copy-start | bytes 100
  30.2 5.3 %collective-permute-start.10 = (bf16[128,256]{1,0:T(8,128)(2,1)S(1)}, bf16[128,256]{1,0:T(8,128)(2,1)S(1)}, u32[]{:S(2)}, u32[]{:S(2)}) collective-permute-start(bf16[128,256]{1,0:T(8,128)(2,1)S(1)} %add_convert_fusion.1), channel_id=1, source_target_pairs={{0,17},{1,16},{2,19},{3,18},{4,21},{5,20},{6,23},{7,22},{8,14},{9,... | collective-permute-start | bytes 196616 | tf_op jit(solution)/shard_map/ppermute | solution.py:29
  31.1 4.4 %collective-permute-start.8 = (bf16[128,256]{1,0:T(8,128)(2,1)S(1)}, bf16[128,256]{1,0:T(8,128)(2,1)S(1)}, u32[]{:S(2)}, u32[]{:S(2)}) collective-permute-start(bf16[128,256]{1,0:T(8,128)(2,1)S(1)} %add_convert_fusion.1), channel_id=1, source_target_pairs={{0,1},{1,0},{2,3},{3,2},{4,5},{5,4},{6,7},{7,6},{8,10},{9,11},{10,... | collective-permute-start | bytes 196616 | tf_op jit(solution)/shard_map/ppermute | solution.py:29
  32.2 4.3 %collective-permute-start.9 = (bf16[128,256]{1,0:T(8,128)(2,1)S(1)}, bf16[128,256]{1,0:T(8,128)(2,1)S(1)}, u32[]{:S(2)}, u32[]{:S(2)}) collective-permute-start(bf16[128,256]{1,0:T(8,128)(2,1)S(1)} %add_convert_fusion.1), channel_id=1, source_target_pairs={{0,16},{1,17},{2,18},{3,19},{4,20},{5,21},{6,22},{7,23},{8,12},{9,... | collective-permute-start | bytes 196616 | tf_op jit(solution)/shard_map/ppermute | solution.py:29
  36.5 1.3 %collective-permute-start.12 = (bf16[128,256]{1,0:T(8,128)(2,1)S(1)}, bf16[128,256]{1,0:T(8,128)(2,1)S(1)}, u32[]{:S(2)}, u32[]{:S(2)}) collective-permute-start(bf16[128,256]{1,0:T(8,128)(2,1)S(1)} %add_convert_fusion), channel_id=1, source_target_pairs={{0,8},{8,0},{16,24},{24,16},{1,9},{9,1},{17,25},{25,17},{2,10},{10... | collective-permute-start | bytes 196616 | tf_op jit(solution)/shard_map/ppermute | solution.py:18

commit v9 on v8

--- a/solution.py
+++ b/solution.py
@@ -267,7 +267,7 @@
                 backward_kernel, [((rows, width), BF16)], [SMEM] + [VMEM] * 6, 16 * MIB
             )(send_live, keep[0], got, third, halo, sends, weight)
         mate = fours[i ^ 1] if i ^ 1 < len(fours) and len(fours[i ^ 1]) == len(four) else four
-        ways = [slice(0, 1), slice(1, 2), slice(0, 2)] if last else [slice(1, 2), slice(0, 2), slice(0, 1)]
+        ways = [slice(0, 1), slice(1, 2), slice(0, 2)] if last else [slice(0, 2), slice(0, 1), slice(1, 2)]
         ways = ways if len(four) == 2 else [slice(0, 1)]
         others = [swap_bits(term, four[way], mate[way]) for way in ways]
         if first:

time: 38.9 us -> 38.2 us (0.982)
  waiting for transfers between devices: 9.07 us -> 7.48 us
  starting transfers between devices: 17.5 us -> 18.4 us
    ppermute x6, waiting for transfers between devices: 3.8 us -> 2.03 us  [swap_bits(): return lax.ppermute(value, ('blk', 'dom'), pairs)]
    ppermute x6, starting transfers between devices: 7.11 us -> 8.01 us  [swap_bits(): return lax.ppermute(value, ('blk', 'dom'), pairs)]
  transfers between devices with their start and end apart: 14 -> 14, of which waited for: 8 -> 9; matrix products, arithmetic and copies ran while one was open for 4% -> 4% of each run, Pallas kernels for 21% -> 22%
where the time goes in v9:
time: 38.2 us; the launch traced here: 37.9 us
  starting transfers between devices  18.4 us (48%)
  Pallas kernels  8.27 us (22%)
  waiting for transfers between devices  7.48 us (20%)
  other arithmetic  2.24 us (6%)
  between operations  0.81 us (2%)
  local copies, waits for them, and re-layouts  0.69 us (2%)
    ppermute x6, starting transfers between devices, swap_bits(): return lax.ppermute(value, ('blk', 'dom'), pairs)  8.01 us
    all_to_all x1, starting transfers between devices, on_device(): lax.all_to_all(outgoing, 'dom', split_axis=0, concat_axis=0, tiled=True)  5.95 us
    ppermute x7, starting transfers between devices, swap(): lax.ppermute(value, axis, [(i, i ^ bit) for i in range(lax.axis_size(axis...  4.44 us
    pallas_call x1, Pallas kernels, on_device(): call(functools.partial(adjacency_kernel, groups), [((rows, width), BF16),...  2.91 us
    ppermute x7, waiting for transfers between devices, swap(): lax.ppermute(value, axis, [(i, i ^ bit) for i in range(lax.axis_size(axis...  2.9 us
    all_to_all x1, waiting for transfers between devices, on_device(): lax.all_to_all(outgoing, 'dom', split_axis=0, concat_axis=0, tiled=True)  2.55 us
    pallas_call x1, Pallas kernels, on_device(): call(halo_kernel, [((peers, 2 * slots, width), BF16)], [HBM] * 6, 64 * MI...  2.23 us
    ppermute x6, waiting for transfers between devices, swap_bits(): return lax.ppermute(value, ('blk', 'dom'), pairs)  2.03 us
  transfers between devices with their start and end apart: 14, of which 9 were waited for; matrix products, arithmetic and copies ran while one was open for 4% of the time, Pallas kernels for 22%

profile of v9, /device:TPU:0, one launch (start us, length us, event | category | flops | bytes accessed | tf_op | source)
XLA Modules:
  0.0 37.9 jit_solution(15430597299715180634)
XLA Ops:
  0.6 3.0 %collective-permute-start = (bf16[512,256]{1,0:T(8,128)(2,1)}, bf16[512,256]{1,0:T(8,128)(2,1)}, u32[]{:S(2)}, u32[]{:S(2)}) collective-permute-start(bf16[512,256]{1,0:T(8,128)(2,1)} %bitcast.23), channel_id=1, source_target_pairs={{0,16},{8,24},{16,0},{24,8},{1,17},{9,25},{17,1},{25,9},{2,18},{10... | collective-permute-start | bytes 786440 | tf_op jit(solution)/shard_map/ppermute | solution.py:18
  3.7 2.2 %shard_map.121.outgoing = bf16[8,64,256]{2,1,0:T(8,128)(2,1)} custom-call(bf16[512,256]{1,0:T(8,128)(2,1)} %bitcast.24, bf16[512,256]{1,0:T(8,128)(2,1)} %bitcast.21, s32[8,32]{1,0:T(8,128)} %bitcast.27, s32[8]{0:T(128)} %bitcast.33, s32[8,32]{1,0:T(8,128)} %bitcast.29, f32[8,32]{1,0:T(8,128)} %bitcast.31), custom_call_target="tpu_custom_call" | custom-call | flops 1 | bytes 1 | tf_op jit(solution)/shard_map/pallas_call | solution.py:192
  5.9 0.0 copy-start.8
  5.9 0.0 copy-start.1
  5.9 5.9 %all-to-all-start = ((bf16[8,64,256]{2,1,0:T(8,128)(2,1)}), bf16[8,64,256]{2,1,0:T(8,128)(2,1)S(1)}, u32[]{:S(2)}, u32[]{:S(2)}) async-start(bf16[8,64,256]{2,1,0:T(8,128)(2,1)} %shard_map.121.outgoing), calls=%async_computation | async-start | bytes 524288 | tf_op jit(solution)/shard_map/all_to_all | solution.py:210
  11.9 0.0 copy-done.8
  11.9 0.0 copy-start.9
  11.9 0.6 %copy-done.9 = s32[1,1,4]{2,1,0:T(1,128)S(1)} copy-done((s32[1,1,4]{2,1,0:T(1,128)S(1)}, s32[1,1,4]{2,1,0:T(1,128)}, u32[]{:S(2)}) %copy-start.9) | copy-done | bytes 40
  12.6 0.1 iota_compare_fusion
  12.6 0.0 copy-start
  12.6 0.0 collective-permute-done.refs_2_
  12.6 0.0 copy-done.1
  12.7 0.1 collective-permute-start.1
  12.7 0.5 %collective-permute-start.2 = (bf16[512,256]{1,0:T(8,128)(2,1)}, bf16[512,256]{1,0:T(8,128)(2,1)S(1)}, u32[]{:S(2)}, u32[]{:S(2)}) collective-permute-start(bf16[512,256]{1,0:T(8,128)(2,1)} %collective-permute-done.refs_2_), channel_id=1, source_target_pairs={{0,8},{8,0},{16,24},{24,16},{1,9},{9,1},{17,25},{25,17},{2,10},{10... | collective-permute-start | bytes 786440 | tf_op jit(solution)/shard_map/ppermute | solution.py:18
  13.2 1.3 %broadcast_select_fusion.tiles = bf16[4,6,128,128]{3,2,1,0:T(8,128)(2,1)S(1)} fusion(bf16[4,6,128,128]{3,2,1,0:T(8,128)(2,1)} %bitcast.35, pred[4,6]{1,0:T(4,128)(4,1)S(1)} %iota_compare_fusion), kind=kLoop, calls=%fused_computation | loop fusion | flops 393216 | bytes 1572888 | tf_op jit(solution)/shard_map/jit(_where)/select_n | solution.py:223
  14.5 0.0 collective-permute-done.1.refs_1_
  14.5 0.3 collective-permute-done.2.refs_3_
  14.8 0.0 copy-done
  14.8 0.0 copy-start.2
  14.8 2.9 %shard_map.122 = (bf16[512,256]{1,0:T(8,128)(2,1)S(1)}, f32[256,256]{1,0:T(8,128)S(1)}, bf16[2,256,512]{2,1,0:T(8,128)(2,1)S(1)}, bf16[256,512]{1,0:T(8,128)(2,1)S(1)}, bf16[256,512]{1,0:T(8,128)(2,1)S(1)}) custom-call(s32[1]{0:T(128)} %bitcast.blk, s32[2,4,6]{2,1,0:T(4,128)S(1)} %add_multiply_fusion.spots, ...), custom_call_target="tpu_custom_call" | custom-call | flops 1 | bytes 1 | tf_op jit(solution)/shard_map/pallas_call | solution.py:225
  17.8 0.2 collective-permute-start.4
  18.0 2.5 %all-to-all-done.halo = bf16[8,64,256]{2,1,0:T(8,128)(2,1)S(1)} async-done(((bf16[8,64,256]{2,1,0:T(8,128)(2,1)}), bf16[8,64,256]{2,1,0:T(8,128)(2,1)S(1)}, u32[]{:S(2)}, u32[]{:S(2)}) %all-to-all-start) | async-done | bytes 262176 | tf_op jit(solution)/shard_map/all_to_all | solution.py:210
  20.5 0.0 copy-done.2
  20.5 0.3 shard_map.123
  20.8 0.1 collective-permute-start.3
  20.9 0.0 collective-permute-done.4.others
  20.9 0.1 fusion
  20.9 0.0 copy-start.3
  21.0 1.1 %collective-permute-done.3 = bf16[128,256]{1,0:T(8,128)(2,1)S(1)} collective-permute-done((bf16[128,256]{1,0:T(8,128)(2,1)S(1)}, bf16[128,256]{1,0:T(8,128)(2,1)S(1)}, u32[]{:S(2)}, u32[]{:S(2)}) %collective-permute-start.3) | collective-permute-done | bytes 65568 | tf_op jit(solution)/shard_map/ppermute | solution.py:18
  22.1 0.0 copy-start.5
  22.1 0.0 copy-start.6
  22.1 1.6 %collective-permute-start.5 = (bf16[128,256]{1,0:T(8,128)(2,1)S(1)}, bf16[128,256]{1,0:T(8,128)(2,1)S(1)}, u32[]{:S(2)}, u32[]{:S(2)}) collective-permute-start(bf16[128,256]{1,0:T(8,128)(2,1)S(1)} %add_convert_fusion.2), channel_id=1, source_target_pairs={{0,6},{1,7},{2,4},{3,5},{4,2},{5,3},{6,0},{7,1},{8,25},{9,24},{10,... | collective-permute-start | bytes 196616 | tf_op jit(solution)/shard_map/ppermute | solution.py:29
  23.8 0.1 collective-permute-start.6
  23.8 2.8 %collective-permute-start.7 = (bf16[128,256]{1,0:T(8,128)(2,1)S(1)}, bf16[128,256]{1,0:T(8,128)(2,1)S(1)}, u32[]{:S(2)}, u32[]{:S(2)}) collective-permute-start(bf16[128,256]{1,0:T(8,128)(2,1)S(1)} %add_convert_fusion.2), channel_id=1, source_target_pairs={{0,4},{1,5},{2,6},{3,7},{4,0},{5,1},{6,2},{7,3},{8,24},{9,25},{10,... | collective-permute-start | bytes 196616 | tf_op jit(solution)/shard_map/ppermute | solution.py:29
  26.6 0.5 %collective-permute-start.11 = (bf16[256,512]{1,0:T(8,128)(2,1)S(1)}, bf16[256,512]{1,0:T(8,128)(2,1)S(1)}, u32[]{:S(2)}, u32[]{:S(2)}) collective-permute-start(bf16[256,512]{1,0:T(8,128)(2,1)S(1)} %fusion), channel_id=1, source_target_pairs={{0,16},{8,24},{16,0},{24,8},{1,17},{9,25},{17,1},{25,9},{2,18},{10... | collective-permute-start | bytes 786440 | tf_op jit(solution)/shard_map/ppermute | solution.py:18
  27.1 0.0 copy-done.3
  27.1 0.0 copy-done.5
  27.1 0.0 copy-done.6
  27.1 1.2 %shard_map.124 = bf16[512,256]{1,0:T(8,128)(2,1)} custom-call(bf16[512,256]{1,0:T(8,128)(2,1)S(1)} %get-tuple-element.42.local, bf16[8,64,256]{2,1,0:T(8,128)(2,1)S(1)} %all-to-all-done.halo, s32[8,32]{1,0:T(8,128)S(1)} %bitcast.30, f32[8,32]{1,0:T(8,128)S(1)} %bitcast.32, bf16[256,256]{1,0:T(8,128)(2,1)S(1)} %copy-done.3), custom_call_target="tpu_custom_call" | custom-call | flops 20000000000 | bytes 1 | tf_op jit(solution)/shard_map/pallas_call | solution.py:262
  28.3 0.1 collective-permute-done.5
  28.4 1.1 %collective-permute-done.6 = bf16[128,256]{1,0:T(8,128)(2,1)S(1)} collective-permute-done((bf16[128,256]{1,0:T(8,128)(2,1)S(1)}, bf16[128,256]{1,0:T(8,128)(2,1)S(1)}, u32[]{:S(2)}, u32[]{:S(2)}) %collective-permute-start.6) | collective-permute-done | bytes 65568 | tf_op jit(solution)/shard_map/ppermute | solution.py:29
  29.4 0.0 collective-permute-done.7
  29.4 0.0 copy-start.4
  29.5 0.0 copy-start.7
  29.5 1.5 %collective-permute-start.10 = (bf16[128,256]{1,0:T(8,128)(2,1)S(1)}, bf16[128,256]{1,0:T(8,128)(2,1)S(1)}, u32[]{:S(2)}, u32[]{:S(2)}) collective-permute-start(bf16[128,256]{1,0:T(8,128)(2,1)S(1)} %add_convert_fusion.1), channel_id=1, source_target_pairs={{0,17},{1,16},{2,19},{3,18},{4,21},{5,20},{6,23},{7,22},{8,14},{9,... | collective-permute-start | bytes 196616 | tf_op jit(solution)/shard_map/ppermute | solution.py:29
  31.0 0.6 %collective-permute-start.8 = (bf16[128,256]{1,0:T(8,128)(2,1)S(1)}, bf16[128,256]{1,0:T(8,128)(2,1)S(1)}, u32[]{:S(2)}, u32[]{:S(2)}) collective-permute-start(bf16[128,256]{1,0:T(8,128)(2,1)S(1)} %add_convert_fusion.1), channel_id=1, source_target_pairs={{0,1},{1,0},{2,3},{3,2},{4,5},{5,4},{6,7},{7,6},{8,10},{9,11},{10,... | collective-permute-start | bytes 196616 | tf_op jit(solution)/shard_map/ppermute | solution.py:29
  31.5 1.5 %collective-permute-start.9 = (bf16[128,256]{1,0:T(8,128)(2,1)S(1)}, bf16[128,256]{1,0:T(8,128)(2,1)S(1)}, u32[]{:S(2)}, u32[]{:S(2)}) collective-permute-start(bf16[128,256]{1,0:T(8,128)(2,1)S(1)} %add_convert_fusion.1), channel_id=1, source_target_pairs={{0,16},{1,17},{2,18},{3,19},{4,20},{5,21},{6,22},{7,23},{8,12},{9,... | collective-permute-start | bytes 196616 | tf_op jit(solution)/shard_map/ppermute | solution.py:29
  33.0 0.2 collective-permute-done.11.third
  33.2 0.0 copy-done.4
  33.2 0.0 copy-done.7
  33.2 1.7 %shard_map.125 = bf16[512,256]{1,0:T(8,128)(2,1)} custom-call(s32[8]{0:T(128)S(1)} %bitcast.34, bf16[256,512]{1,0:T(8,128)(2,1)S(1)} %get-tuple-element.47.first, bf16[2,256,512]{2,1,0:T(8,128)(2,1)S(1)} %collective-permute-done.4.others, bf16[256,512]{1,0:T(8,128)(2,1)S(1)} %collective-permute-done.11.third, bf16[8,64,256]{2,1,0:T(8,128)(2,1)S(1)} %all-to-all-done.halo, ...), custom_call_target="tpu_custom_call" | custom-call | flops 1 | bytes 1 | tf_op jit(solution)/shard_map/pallas_call | solution.py:266
  34.9 0.0 collective-permute-done.10
  34.9 0.3 collective-permute-done.8
  35.2 0.6 %collective-permute-done.9 = bf16[128,256]{1,0:T(8,128)(2,1)S(1)} collective-permute-done((bf16[128,256]{1,0:T(8,128)(2,1)S(1)}, bf16[128,256]{1,0:T(8,128)(2,1)S(1)}, u32[]{:S(2)}, u32[]{:S(2)}) %collective-permute-start.9) | collective-permute-done | bytes 65568 | tf_op jit(solution)/shard_map/ppermute | solution.py:29
  35.8 0.1 collective-permute-start.12
  35.9 1.2 %collective-permute-done.12 = bf16[128,256]{1,0:T(8,128)(2,1)S(1)} collective-permute-done((bf16[128,256]{1,0:T(8,128)(2,1)S(1)}, bf16[128,256]{1,0:T(8,128)(2,1)S(1)}, u32[]{:S(2)}, u32[]{:S(2)}) %collective-permute-start.12) | collective-permute-done | bytes 65568 | tf_op jit(solution)/shard_map/ppermute | solution.py:18
  37.2 0.7 %convert_multiply_fusion = f32[256,256]{1,0:T(8,128)} fusion(bf16[128,256]{1,0:T(8,128)(2,1)S(1)} %get-tuple-element.54, bf16[128,256]{1,0:T(8,128)(2,1)S(1)} %get-tuple-element.53), kind=kLoop, calls=%fused_computation.4 | loop fusion | flops 327680 | bytes 393216 | tf_op jit(solution)/shard_map/mul | solution.py:287
  (6 shorter events, 0.1 us)
Async XLA Ops:
  0.6 12.0 %collective-permute-start = (bf16[512,256]{1,0:T(8,128)(2,1)}, bf16[512,256]{1,0:T(8,128)(2,1)}, u32[]{:S(2)}, u32[]{:S(2)}) collective-permute-start(bf16[512,256]{1,0:T(8,128)(2,1)} %bitcast.23), channel_id=1, source_target_pairs={{0,16},{8,24},{16,0},{24,8},{1,17},{9,25},{17,1},{25,9},{2,18},{10... | collective-permute-start | bytes 786440 | tf_op jit(solution)/shard_map/ppermute | solution.py:18
  5.9 6.0 %copy-start.8 = (s32[1,1,4,6]{3,2,1,0:T(4,128)S(1)}, s32[1,1,4,6]{3,2,1,0:T(4,128)}, u32[]{:S(2)}) copy-start(s32[1,1,4,6]{3,2,1,0:T(4,128)} %param.13) | copy-start | bytes 292
  5.9 6.7 %copy-start.1 = (bf16[1,512,256]{2,1,0:T(8,128)(2,1)S(1)}, bf16[1,512,256]{2,1,0:T(8,128)(2,1)}, u32[]{:S(2)}) copy-start(bf16[1,512,256]{2,1,0:T(8,128)(2,1)} %param.10) | copy-start | bytes 786436
  5.9 14.6 %all-to-all-start = ((bf16[8,64,256]{2,1,0:T(8,128)(2,1)}), bf16[8,64,256]{2,1,0:T(8,128)(2,1)S(1)}, u32[]{:S(2)}, u32[]{:S(2)}) async-start(bf16[8,64,256]{2,1,0:T(8,128)(2,1)} %shard_map.121.outgoing), calls=%async_computation | async-start | bytes 524288 | tf_op jit(solution)/shard_map/all_to_all | solution.py:210
  11.9 0.7 %copy-start.9 = (s32[1,1,4]{2,1,0:T(1,128)S(1)}, s32[1,1,4]{2,1,0:T(1,128)}, u32[]{:S(2)}) copy-start(s32[1,1,4]{2,1,0:T(1,128)} %param.14) | copy-start | bytes 52
  12.6 2.2 %copy-start = (bf16[1,512,256]{2,1,0:T(8,128)(2,1)S(1)}, bf16[1,512,256]{2,1,0:T(8,128)(2,1)}, u32[]{:S(2)}) copy-start(bf16[1,512,256]{2,1,0:T(8,128)(2,1)} %param.19) | copy-start | bytes 786436
  12.7 1.8 %collective-permute-start.1 = (bf16[512,256]{1,0:T(8,128)(2,1)S(1)}, bf16[512,256]{1,0:T(8,128)(2,1)S(1)}, u32[]{:S(2)}, u32[]{:S(2)}) collective-permute-start(bf16[512,256]{1,0:T(8,128)(2,1)S(1)} %bitcast.25), channel_id=1, source_target_pairs={{0,8},{8,0},{16,24},{24,16},{1,9},{9,1},{17,25},{25,17},{2,10},{10... | collective-permute-start | bytes 786440 | tf_op jit(solution)/shard_map/ppermute | solution.py:18
  12.7 2.1 %collective-permute-start.2 = (bf16[512,256]{1,0:T(8,128)(2,1)}, bf16[512,256]{1,0:T(8,128)(2,1)S(1)}, u32[]{:S(2)}, u32[]{:S(2)}) collective-permute-start(bf16[512,256]{1,0:T(8,128)(2,1)} %collective-permute-done.refs_2_), channel_id=1, source_target_pairs={{0,8},{8,0},{16,24},{24,16},{1,9},{9,1},{17,25},{25,17},{2,10},{10... | collective-permute-start | bytes 786440 | tf_op jit(solution)/shard_map/ppermute | solution.py:18
  14.8 5.7 %copy-start.2 = (bf16[8,64,256]{2,1,0:T(8,128)(2,1)S(1)}, bf16[8,64,256]{2,1,0:T(8,128)(2,1)}, u32[]{:S(2)}) copy-start(bf16[8,64,256]{2,1,0:T(8,128)(2,1)} %shard_map.121.outgoing) | copy-start | bytes 786436
  17.8 3.1 %collective-permute-start.4 = (bf16[2,256,512]{2,1,0:T(8,128)(2,1)S(1)}, bf16[2,256,512]{2,1,0:T(8,128)(2,1)S(1)}, u32[]{:S(2)}, u32[]{:S(2)}) collective-permute-start(bf16[2,256,512]{2,1,0:T(8,128)(2,1)S(1)} %get-tuple-element.38), channel_id=1, source_target_pairs={{0,8},{8,0},{16,24},{24,16},{1,9},{9,1},{17,25},{25,17},{2,10},{10... | collective-permute-start | bytes 1572872 | tf_op jit(solution)/shard_map/ppermute | solution.py:18
  20.8 1.3 %collective-permute-start.3 = (bf16[128,256]{1,0:T(8,128)(2,1)S(1)}, bf16[128,256]{1,0:T(8,128)(2,1)S(1)}, u32[]{:S(2)}, u32[]{:S(2)}) collective-permute-start(bf16[128,256]{1,0:T(8,128)(2,1)S(1)} %get-tuple-element.36), channel_id=1, source_target_pairs={{0,8},{8,0},{16,24},{24,16},{1,9},{9,1},{17,25},{25,17},{2,10},{10... | collective-permute-start | bytes 196616 | tf_op jit(solution)/shard_map/ppermute | solution.py:18
  20.9 6.1 %copy-start.3 = (bf16[256,256]{1,0:T(8,128)(2,1)S(1)}, bf16[256,256]{1,0:T(8,128)(2,1)}, u32[]{:S(2)}) copy-start(bf16[256,256]{1,0:T(8,128)(2,1)} %weight.3) | copy-start | bytes 393220
  22.1 5.0 %copy-start.5 = (s32[1,1,8,32]{3,2,1,0:T(8,128)S(1)}, s32[1,1,8,32]{3,2,1,0:T(8,128)}, u32[]{:S(2)}) copy-start(s32[1,1,8,32]{3,2,1,0:T(8,128)} %param.17) | copy-start | bytes 3076
  22.1 5.0 %copy-start.6 = (f32[1,1,8,32]{3,2,1,0:T(8,128)S(1)}, f32[1,1,8,32]{3,2,1,0:T(8,128)}, u32[]{:S(2)}) copy-start(f32[1,1,8,32]{3,2,1,0:T(8,128)} %param.18) | copy-start | bytes 3076
  22.1 6.2 %collective-permute-start.5 = (bf16[128,256]{1,0:T(8,128)(2,1)S(1)}, bf16[128,256]{1,0:T(8,128)(2,1)S(1)}, u32[]{:S(2)}, u32[]{:S(2)}) collective-permute-start(bf16[128,256]{1,0:T(8,128)(2,1)S(1)} %add_convert_fusion.2), channel_id=1, source_target_pairs={{0,6},{1,7},{2,4},{3,5},{4,2},{5,3},{6,0},{7,1},{8,25},{9,24},{10,... | collective-permute-start | bytes 196616 | tf_op jit(solution)/shard_map/ppermute | solution.py:29
  23.8 5.7 %collective-permute-start.6 = (bf16[128,256]{1,0:T(8,128)(2,1)S(1)}, bf16[128,256]{1,0:T(8,128)(2,1)S(1)}, u32[]{:S(2)}, u32[]{:S(2)}) collective-permute-start(bf16[128,256]{1,0:T(8,128)(2,1)S(1)} %add_convert_fusion.2), channel_id=1, source_target_pairs={{0,2},{1,3},{2,0},{3,1},{4,6},{5,7},{6,4},{7,5},{8,9},{9,8},{10,11... | collective-permute-start | bytes 196616 | tf_op jit(solution)/shard_map/ppermute | solution.py:29
  23.8 5.6 %collective-permute-start.7 = (bf16[128,256]{1,0:T(8,128)(2,1)S(1)}, bf16[128,256]{1,0:T(8,128)(2,1)S(1)}, u32[]{:S(2)}, u32[]{:S(2)}) collective-permute-start(bf16[128,256]{1,0:T(8,128)(2,1)S(1)} %add_convert_fusion.2), channel_id=1, source_target_pairs={{0,4},{1,5},{2,6},{3,7},{4,0},{5,1},{6,2},{7,3},{8,24},{9,25},{10,... | collective-permute-start | bytes 196616 | tf_op jit(solution)/shard_map/ppermute | solution.py:29
  26.6 6.6 %collective-permute-start.11 = (bf16[256,512]{1,0:T(8,128)(2,1)S(1)}, bf16[256,512]{1,0:T(8,128)(2,1)S(1)}, u32[]{:S(2)}, u32[]{:S(2)}) collective-permute-start(bf16[256,512]{1,0:T(8,128)(2,1)S(1)} %fusion), channel_id=1, source_target_pairs={{0,16},{8,24},{16,0},{24,8},{1,17},{9,25},{17,1},{25,9},{2,18},{10... | collective-permute-start | bytes 786440 | tf_op jit(solution)/shard_map/ppermute | solution.py:18
  29.4 3.8 %copy-start.4 = (s32[1,1,8,32]{3,2,1,0:T(8,128)S(1)}, s32[1,1,8,32]{3,2,1,0:T(8,128)}, u32[]{:S(2)}) copy-start(s32[1,1,8,32]{3,2,1,0:T(8,128)} %param.15) | copy-start | bytes 3076
  29.5 3.8 %copy-start.7 = (s32[1,1,8]{2,1,0:T(1,128)S(1)}, s32[1,1,8]{2,1,0:T(1,128)}, u32[]{:S(2)}) copy-start(s32[1,1,8]{2,1,0:T(1,128)} %param.16) | copy-start | bytes 100
  29.5 5.5 %collective-permute-start.10 = (bf16[128,256]{1,0:T(8,128)(2,1)S(1)}, bf16[128,256]{1,0:T(8,128)(2,1)S(1)}, u32[]{:S(2)}, u32[]{:S(2)}) collective-permute-start(bf16[128,256]{1,0:T(8,128)(2,1)S(1)} %add_convert_fusion.1), channel_id=1, source_target_pairs={{0,17},{1,16},{2,19},{3,18},{4,21},{5,20},{6,23},{7,22},{8,14},{9,... | collective-permute-start | bytes 196616 | tf_op jit(solution)/shard_map/ppermute | solution.py:29
  31.0 4.3 %collective-permute-start.8 = (bf16[128,256]{1,0:T(8,128)(2,1)S(1)}, bf16[128,256]{1,0:T(8,128)(2,1)S(1)}, u32[]{:S(2)}, u32[]{:S(2)}) collective-permute-start(bf16[128,256]{1,0:T(8,128)(2,1)S(1)} %add_convert_fusion.1), channel_id=1, source_target_pairs={{0,1},{1,0},{2,3},{3,2},{4,5},{5,4},{6,7},{7,6},{8,10},{9,11},{10,... | collective-permute-start | bytes 196616 | tf_op jit(solution)/shard_map/ppermute | solution.py:29
  31.5 4.3 %collective-permute-start.9 = (bf16[128,256]{1,0:T(8,128)(2,1)S(1)}, bf16[128,256]{1,0:T(8,128)(2,1)S(1)}, u32[]{:S(2)}, u32[]{:S(2)}) collective-permute-start(bf16[128,256]{1,0:T(8,128)(2,1)S(1)} %add_convert_fusion.1), channel_id=1, source_target_pairs={{0,16},{1,17},{2,18},{3,19},{4,20},{5,21},{6,22},{7,23},{8,12},{9,... | collective-permute-start | bytes 196616 | tf_op jit(solution)/shard_map/ppermute | solution.py:29
  35.8 1.3 %collective-permute-start.12 = (bf16[128,256]{1,0:T(8,128)(2,1)S(1)}, bf16[128,256]{1,0:T(8,128)(2,1)S(1)}, u32[]{:S(2)}, u32[]{:S(2)}) collective-permute-start(bf16[128,256]{1,0:T(8,128)(2,1)S(1)} %add_convert_fusion), channel_id=1, source_target_pairs={{0,8},{8,0},{16,24},{24,16},{1,9},{9,1},{17,25},{25,17},{2,10},{10... | collective-permute-start | bytes 196616 | tf_op jit(solution)/shard_map/ppermute | solution.py:18

commit v10 on v9

--- a/solution.py
+++ b/solution.py
@@ -77,13 +77,6 @@
     out[:, :slots, :] = sent.astype(BF16).reshape(peers, slots, width)
     back = matmul(weights_of(rows, owner, edge), grad[...], 0, 0)
     out[:, slots:, :] = back.astype(BF16).reshape(peers, slots, width)
-
-
-def split_halves(blk, term, kept, sent):
-    half = term.shape[0] // 2
-    core = blk[0] % 2
-    kept[...] = term[pl.ds(pl.multiple_of(core * half, half), half), :].astype(BF16)
-    sent[...] = term[pl.ds(pl.multiple_of((1 - core) * half, half), half), :].astype(BF16)
 
 
 def adjacency_kernel(groups, blk, spots, tiles, grad, *refs):
@@ -123,12 +116,15 @@
     return matmul(weights_of(rows, owner, edge), received, 1, 0)
 
 
-def halo_term_kernel(blk, near, halo, outgoing, kept, sent, term):
+def halo_term_kernel(blk, near, halo, outgoing, kept, sent):
     peers, both, width = halo.shape
     received = halo[:, : both // 2, :].reshape(-1, width)
     weighted = outgoing[:, both // 2 :, :].reshape(-1, width)
-    term[...] = near[...] + matmul(received, weighted, 0, 0)
-    split_halves(blk, term, kept, sent)
+    product = near[...] + matmul(received, weighted, 0, 0)
+    low, high = product[: width // 2].astype(BF16), product[width // 2 :].astype(BF16)
+    first = blk[0] % 2 == 0
+    kept[...] = jnp.where(first, low, high)
+    sent[...] = jnp.where(first, high, low)
 
 
 def output_kernel(local, halo, owner, edge, weight, out):
@@ -237,7 +233,6 @@
         [half_term, half_term],
         [SMEM] + [VMEM] * 3,
         16 * MIB,
-        [pltpu.VMEM((width, width), F32)],
         flops=2 * 10**10,
     )(blk, near_term, halo, outgoing)
     other = swap(sent, "blk", 1)

time: 38.2 us -> 38.2 us (level)
  no operation moved by 1% of the time
where the time goes in v10:
time: 38.2 us; the launch traced here: 37.9 us
  starting transfers between devices  18.4 us (48%)
  Pallas kernels  8.22 us (22%)
  waiting for transfers between devices  7.52 us (20%)
  other arithmetic  2.24 us (6%)
  between operations  0.81 us (2%)
  local copies, waits for them, and re-layouts  0.69 us (2%)
    ppermute x6, starting transfers between devices, swap_bits(): return lax.ppermute(value, ('blk', 'dom'), pairs)  8.01 us
    all_to_all x1, starting transfers between devices, on_device(): lax.all_to_all(outgoing, 'dom', split_axis=0, concat_axis=0, tiled=True)  5.95 us
    ppermute x7, starting transfers between devices, swap(): lax.ppermute(value, axis, [(i, i ^ bit) for i in range(lax.axis_size(axis...  4.45 us
    pallas_call x1, Pallas kernels, on_device(): call(functools.partial(adjacency_kernel, groups), [((rows, width), BF16),...  2.9 us
    ppermute x7, waiting for transfers between devices, swap(): lax.ppermute(value, axis, [(i, i ^ bit) for i in range(lax.axis_size(axis...  2.86 us
    all_to_all x1, waiting for transfers between devices, on_device(): lax.all_to_all(outgoing, 'dom', split_axis=0, concat_axis=0, tiled=True)  2.55 us
    pallas_call x1, Pallas kernels, on_device(): call(halo_kernel, [((peers, 2 * slots, width), BF16)], [HBM] * 6, 64 * MI...  2.23 us
    ppermute x6, waiting for transfers between devices, swap_bits(): return lax.ppermute(value, ('blk', 'dom'), pairs)  2.12 us
  transfers between devices with their start and end apart: 14, of which 9 were waited for; matrix products, arithmetic and copies ran while one was open for 4% of the time, Pallas kernels for 22%

profile of v10, /device:TPU:0, one launch (start us, length us, event | category | flops | bytes accessed | tf_op | source)
XLA Modules:
  0.0 37.9 jit_solution(1587819218156288111)
XLA Ops:
  0.6 3.0 %collective-permute-start = (bf16[512,256]{1,0:T(8,128)(2,1)}, bf16[512,256]{1,0:T(8,128)(2,1)}, u32[]{:S(2)}, u32[]{:S(2)}) collective-permute-start(bf16[512,256]{1,0:T(8,128)(2,1)} %bitcast.23), channel_id=1, source_target_pairs={{0,16},{8,24},{16,0},{24,8},{1,17},{9,25},{17,1},{25,9},{2,18},{10... | collective-permute-start | bytes 786440 | tf_op jit(solution)/shard_map/ppermute | solution.py:18
  3.7 2.2 %shard_map.121.outgoing = bf16[8,64,256]{2,1,0:T(8,128)(2,1)} custom-call(bf16[512,256]{1,0:T(8,128)(2,1)} %bitcast.24, bf16[512,256]{1,0:T(8,128)(2,1)} %bitcast.21, s32[8,32]{1,0:T(8,128)} %bitcast.27, s32[8]{0:T(128)} %bitcast.33, s32[8,32]{1,0:T(8,128)} %bitcast.29, f32[8,32]{1,0:T(8,128)} %bitcast.31), custom_call_target="tpu_custom_call" | custom-call | flops 1 | bytes 1 | tf_op jit(solution)/shard_map/pallas_call | solution.py:188
  5.9 0.0 copy-start.8
  5.9 0.0 copy-start.1
  5.9 5.9 %all-to-all-start = ((bf16[8,64,256]{2,1,0:T(8,128)(2,1)}), bf16[8,64,256]{2,1,0:T(8,128)(2,1)S(1)}, u32[]{:S(2)}, u32[]{:S(2)}) async-start(bf16[8,64,256]{2,1,0:T(8,128)(2,1)} %shard_map.121.outgoing), calls=%async_computation | async-start | bytes 524288 | tf_op jit(solution)/shard_map/all_to_all | solution.py:206
  11.9 0.0 copy-done.8
  11.9 0.0 copy-start.9
  11.9 0.6 %copy-done.9 = s32[1,1,4]{2,1,0:T(1,128)S(1)} copy-done((s32[1,1,4]{2,1,0:T(1,128)S(1)}, s32[1,1,4]{2,1,0:T(1,128)}, u32[]{:S(2)}) %copy-start.9) | copy-done | bytes 40
  12.6 0.1 iota_compare_fusion
  12.6 0.0 copy-start
  12.6 0.0 collective-permute-done.refs_2_
  12.6 0.0 copy-done.1
  12.7 0.1 collective-permute-start.1
  12.7 0.5 %collective-permute-start.2 = (bf16[512,256]{1,0:T(8,128)(2,1)}, bf16[512,256]{1,0:T(8,128)(2,1)S(1)}, u32[]{:S(2)}, u32[]{:S(2)}) collective-permute-start(bf16[512,256]{1,0:T(8,128)(2,1)} %collective-permute-done.refs_2_), channel_id=1, source_target_pairs={{0,8},{8,0},{16,24},{24,16},{1,9},{9,1},{17,25},{25,17},{2,10},{10... | collective-permute-start | bytes 786440 | tf_op jit(solution)/shard_map/ppermute | solution.py:18
  13.2 1.3 %broadcast_select_fusion.tiles = bf16[4,6,128,128]{3,2,1,0:T(8,128)(2,1)S(1)} fusion(bf16[4,6,128,128]{3,2,1,0:T(8,128)(2,1)} %bitcast.35, pred[4,6]{1,0:T(4,128)(4,1)S(1)} %iota_compare_fusion), kind=kLoop, calls=%fused_computation | loop fusion | flops 393216 | bytes 1572888 | tf_op jit(solution)/shard_map/jit(_where)/select_n | solution.py:219
  14.5 0.0 collective-permute-done.1.refs_1_
  14.5 0.3 collective-permute-done.2.refs_3_
  14.8 0.0 copy-done
  14.8 0.0 copy-start.2
  14.8 2.9 %shard_map.122 = (bf16[512,256]{1,0:T(8,128)(2,1)S(1)}, f32[256,256]{1,0:T(8,128)S(1)}, bf16[2,256,512]{2,1,0:T(8,128)(2,1)S(1)}, bf16[256,512]{1,0:T(8,128)(2,1)S(1)}, bf16[256,512]{1,0:T(8,128)(2,1)S(1)}) custom-call(s32[1]{0:T(128)} %bitcast.blk, s32[2,4,6]{2,1,0:T(4,128)S(1)} %add_multiply_fusion.spots, ...), custom_call_target="tpu_custom_call" | custom-call | flops 1 | bytes 1 | tf_op jit(solution)/shard_map/pallas_call | solution.py:221
  17.8 0.2 collective-permute-start.4
  18.0 2.5 %all-to-all-done.halo = bf16[8,64,256]{2,1,0:T(8,128)(2,1)S(1)} async-done(((bf16[8,64,256]{2,1,0:T(8,128)(2,1)}), bf16[8,64,256]{2,1,0:T(8,128)(2,1)S(1)}, u32[]{:S(2)}, u32[]{:S(2)}) %all-to-all-start) | async-done | bytes 262176 | tf_op jit(solution)/shard_map/all_to_all | solution.py:206
  20.5 0.0 copy-done.2
  20.5 0.2 shard_map.123
  20.7 0.1 collective-permute-start.3
  20.8 0.0 collective-permute-done.4.others
  20.8 0.1 fusion
  20.9 0.0 copy-start.3
  20.9 1.1 %collective-permute-done.3 = bf16[128,256]{1,0:T(8,128)(2,1)S(1)} collective-permute-done((bf16[128,256]{1,0:T(8,128)(2,1)S(1)}, bf16[128,256]{1,0:T(8,128)(2,1)S(1)}, u32[]{:S(2)}, u32[]{:S(2)}) %collective-permute-start.3) | collective-permute-done | bytes 65568 | tf_op jit(solution)/shard_map/ppermute | solution.py:18
  22.1 0.0 copy-start.5
  22.1 0.0 copy-start.6
  22.1 1.7 %collective-permute-start.5 = (bf16[128,256]{1,0:T(8,128)(2,1)S(1)}, bf16[128,256]{1,0:T(8,128)(2,1)S(1)}, u32[]{:S(2)}, u32[]{:S(2)}) collective-permute-start(bf16[128,256]{1,0:T(8,128)(2,1)S(1)} %add_convert_fusion.2), channel_id=1, source_target_pairs={{0,6},{1,7},{2,4},{3,5},{4,2},{5,3},{6,0},{7,1},{8,25},{9,24},{10,... | collective-permute-start | bytes 196616 | tf_op jit(solution)/shard_map/ppermute | solution.py:29
  23.8 0.0 collective-permute-start.6
  23.8 2.8 %collective-permute-start.7 = (bf16[128,256]{1,0:T(8,128)(2,1)S(1)}, bf16[128,256]{1,0:T(8,128)(2,1)S(1)}, u32[]{:S(2)}, u32[]{:S(2)}) collective-permute-start(bf16[128,256]{1,0:T(8,128)(2,1)S(1)} %add_convert_fusion.2), channel_id=1, source_target_pairs={{0,4},{1,5},{2,6},{3,7},{4,0},{5,1},{6,2},{7,3},{8,24},{9,25},{10,... | collective-permute-start | bytes 196616 | tf_op jit(solution)/shard_map/ppermute | solution.py:29
  26.5 0.5 %collective-permute-start.11 = (bf16[256,512]{1,0:T(8,128)(2,1)S(1)}, bf16[256,512]{1,0:T(8,128)(2,1)S(1)}, u32[]{:S(2)}, u32[]{:S(2)}) collective-permute-start(bf16[256,512]{1,0:T(8,128)(2,1)S(1)} %fusion), channel_id=1, source_target_pairs={{0,16},{8,24},{16,0},{24,8},{1,17},{9,25},{17,1},{25,9},{2,18},{10... | collective-permute-start | bytes 786440 | tf_op jit(solution)/shard_map/ppermute | solution.py:18
  27.0 0.0 copy-done.3
  27.1 0.0 copy-done.5
  27.1 0.0 copy-done.6
  27.1 1.2 %shard_map.124 = bf16[512,256]{1,0:T(8,128)(2,1)} custom-call(bf16[512,256]{1,0:T(8,128)(2,1)S(1)} %get-tuple-element.42.local, bf16[8,64,256]{2,1,0:T(8,128)(2,1)S(1)} %all-to-all-done.halo, s32[8,32]{1,0:T(8,128)S(1)} %bitcast.30, f32[8,32]{1,0:T(8,128)S(1)} %bitcast.32, bf16[256,256]{1,0:T(8,128)(2,1)S(1)} %copy-done.3), custom_call_target="tpu_custom_call" | custom-call | flops 20000000000 | bytes 1 | tf_op jit(solution)/shard_map/pallas_call | solution.py:257
  28.2 0.1 collective-permute-done.5
  28.3 1.1 %collective-permute-done.6 = bf16[128,256]{1,0:T(8,128)(2,1)S(1)} collective-permute-done((bf16[128,256]{1,0:T(8,128)(2,1)S(1)}, bf16[128,256]{1,0:T(8,128)(2,1)S(1)}, u32[]{:S(2)}, u32[]{:S(2)}) %collective-permute-start.6) | collective-permute-done | bytes 65568 | tf_op jit(solution)/shard_map/ppermute | solution.py:29
  29.4 0.0 collective-permute-done.7
  29.4 0.0 copy-start.4
  29.5 0.0 copy-start.7
  29.5 1.5 %collective-permute-start.10 = (bf16[128,256]{1,0:T(8,128)(2,1)S(1)}, bf16[128,256]{1,0:T(8,128)(2,1)S(1)}, u32[]{:S(2)}, u32[]{:S(2)}) collective-permute-start(bf16[128,256]{1,0:T(8,128)(2,1)S(1)} %add_convert_fusion.1), channel_id=1, source_target_pairs={{0,17},{1,16},{2,19},{3,18},{4,21},{5,20},{6,23},{7,22},{8,14},{9,... | collective-permute-start | bytes 196616 | tf_op jit(solution)/shard_map/ppermute | solution.py:29
  31.0 0.6 %collective-permute-start.8 = (bf16[128,256]{1,0:T(8,128)(2,1)S(1)}, bf16[128,256]{1,0:T(8,128)(2,1)S(1)}, u32[]{:S(2)}, u32[]{:S(2)}) collective-permute-start(bf16[128,256]{1,0:T(8,128)(2,1)S(1)} %add_convert_fusion.1), channel_id=1, source_target_pairs={{0,1},{1,0},{2,3},{3,2},{4,5},{5,4},{6,7},{7,6},{8,10},{9,11},{10,... | collective-permute-start | bytes 196616 | tf_op jit(solution)/shard_map/ppermute | solution.py:29
  31.5 1.5 %collective-permute-start.9 = (bf16[128,256]{1,0:T(8,128)(2,1)S(1)}, bf16[128,256]{1,0:T(8,128)(2,1)S(1)}, u32[]{:S(2)}, u32[]{:S(2)}) collective-permute-start(bf16[128,256]{1,0:T(8,128)(2,1)S(1)} %add_convert_fusion.1), channel_id=1, source_target_pairs={{0,16},{1,17},{2,18},{3,19},{4,20},{5,21},{6,22},{7,23},{8,12},{9,... | collective-permute-start | bytes 196616 | tf_op jit(solution)/shard_map/ppermute | solution.py:29
  33.0 0.1 collective-permute-done.11.third
  33.2 0.0 copy-done.4
  33.2 0.0 copy-done.7
  33.2 1.7 %shard_map.125 = bf16[512,256]{1,0:T(8,128)(2,1)} custom-call(s32[8]{0:T(128)S(1)} %bitcast.34, bf16[256,512]{1,0:T(8,128)(2,1)S(1)} %get-tuple-element.47.first, bf16[2,256,512]{2,1,0:T(8,128)(2,1)S(1)} %collective-permute-done.4.others, bf16[256,512]{1,0:T(8,128)(2,1)S(1)} %collective-permute-done.11.third, bf16[8,64,256]{2,1,0:T(8,128)(2,1)S(1)} %all-to-all-done.halo, ...), custom_call_target="tpu_custom_call" | custom-call | flops 1 | bytes 1 | tf_op jit(solution)/shard_map/pallas_call | solution.py:261
  34.9 0.0 collective-permute-done.10
  34.9 0.3 collective-permute-done.8
  35.2 0.6 %collective-permute-done.9 = bf16[128,256]{1,0:T(8,128)(2,1)S(1)} collective-permute-done((bf16[128,256]{1,0:T(8,128)(2,1)S(1)}, bf16[128,256]{1,0:T(8,128)(2,1)S(1)}, u32[]{:S(2)}, u32[]{:S(2)}) %collective-permute-start.9) | collective-permute-done | bytes 65568 | tf_op jit(solution)/shard_map/ppermute | solution.py:29
  35.8 0.1 collective-permute-start.12
  35.9 1.2 %collective-permute-done.12 = bf16[128,256]{1,0:T(8,128)(2,1)S(1)} collective-permute-done((bf16[128,256]{1,0:T(8,128)(2,1)S(1)}, bf16[128,256]{1,0:T(8,128)(2,1)S(1)}, u32[]{:S(2)}, u32[]{:S(2)}) %collective-permute-start.12) | collective-permute-done | bytes 65568 | tf_op jit(solution)/shard_map/ppermute | solution.py:18
  37.2 0.7 %convert_multiply_fusion = f32[256,256]{1,0:T(8,128)} fusion(bf16[128,256]{1,0:T(8,128)(2,1)S(1)} %get-tuple-element.54, bf16[128,256]{1,0:T(8,128)(2,1)S(1)} %get-tuple-element.53), kind=kLoop, calls=%fused_computation.4 | loop fusion | flops 327680 | bytes 393216 | tf_op jit(solution)/shard_map/mul | solution.py:282
  (6 shorter events, 0.1 us)
Async XLA Ops:
  0.6 12.0 %collective-permute-start = (bf16[512,256]{1,0:T(8,128)(2,1)}, bf16[512,256]{1,0:T(8,128)(2,1)}, u32[]{:S(2)}, u32[]{:S(2)}) collective-permute-start(bf16[512,256]{1,0:T(8,128)(2,1)} %bitcast.23), channel_id=1, source_target_pairs={{0,16},{8,24},{16,0},{24,8},{1,17},{9,25},{17,1},{25,9},{2,18},{10... | collective-permute-start | bytes 786440 | tf_op jit(solution)/shard_map/ppermute | solution.py:18
  5.9 6.0 %copy-start.8 = (s32[1,1,4,6]{3,2,1,0:T(4,128)S(1)}, s32[1,1,4,6]{3,2,1,0:T(4,128)}, u32[]{:S(2)}) copy-start(s32[1,1,4,6]{3,2,1,0:T(4,128)} %param.13) | copy-start | bytes 292
  5.9 6.7 %copy-start.1 = (bf16[1,512,256]{2,1,0:T(8,128)(2,1)S(1)}, bf16[1,512,256]{2,1,0:T(8,128)(2,1)}, u32[]{:S(2)}) copy-start(bf16[1,512,256]{2,1,0:T(8,128)(2,1)} %param.10) | copy-start | bytes 786436
  5.9 14.6 %all-to-all-start = ((bf16[8,64,256]{2,1,0:T(8,128)(2,1)}), bf16[8,64,256]{2,1,0:T(8,128)(2,1)S(1)}, u32[]{:S(2)}, u32[]{:S(2)}) async-start(bf16[8,64,256]{2,1,0:T(8,128)(2,1)} %shard_map.121.outgoing), calls=%async_computation | async-start | bytes 524288 | tf_op jit(solution)/shard_map/all_to_all | solution.py:206
  11.9 0.7 %copy-start.9 = (s32[1,1,4]{2,1,0:T(1,128)S(1)}, s32[1,1,4]{2,1,0:T(1,128)}, u32[]{:S(2)}) copy-start(s32[1,1,4]{2,1,0:T(1,128)} %param.14) | copy-start | bytes 52
  12.6 2.2 %copy-start = (bf16[1,512,256]{2,1,0:T(8,128)(2,1)S(1)}, bf16[1,512,256]{2,1,0:T(8,128)(2,1)}, u32[]{:S(2)}) copy-start(bf16[1,512,256]{2,1,0:T(8,128)(2,1)} %param.19) | copy-start | bytes 786436
  12.7 1.8 %collective-permute-start.1 = (bf16[512,256]{1,0:T(8,128)(2,1)S(1)}, bf16[512,256]{1,0:T(8,128)(2,1)S(1)}, u32[]{:S(2)}, u32[]{:S(2)}) collective-permute-start(bf16[512,256]{1,0:T(8,128)(2,1)S(1)} %bitcast.25), channel_id=1, source_target_pairs={{0,8},{8,0},{16,24},{24,16},{1,9},{9,1},{17,25},{25,17},{2,10},{10... | collective-permute-start | bytes 786440 | tf_op jit(solution)/shard_map/ppermute | solution.py:18
  12.7 2.1 %collective-permute-start.2 = (bf16[512,256]{1,0:T(8,128)(2,1)}, bf16[512,256]{1,0:T(8,128)(2,1)S(1)}, u32[]{:S(2)}, u32[]{:S(2)}) collective-permute-start(bf16[512,256]{1,0:T(8,128)(2,1)} %collective-permute-done.refs_2_), channel_id=1, source_target_pairs={{0,8},{8,0},{16,24},{24,16},{1,9},{9,1},{17,25},{25,17},{2,10},{10... | collective-permute-start | bytes 786440 | tf_op jit(solution)/shard_map/ppermute | solution.py:18
  14.8 5.7 %copy-start.2 = (bf16[8,64,256]{2,1,0:T(8,128)(2,1)S(1)}, bf16[8,64,256]{2,1,0:T(8,128)(2,1)}, u32[]{:S(2)}) copy-start(bf16[8,64,256]{2,1,0:T(8,128)(2,1)} %shard_map.121.outgoing) | copy-start | bytes 786436
  17.8 3.1 %collective-permute-start.4 = (bf16[2,256,512]{2,1,0:T(8,128)(2,1)S(1)}, bf16[2,256,512]{2,1,0:T(8,128)(2,1)S(1)}, u32[]{:S(2)}, u32[]{:S(2)}) collective-permute-start(bf16[2,256,512]{2,1,0:T(8,128)(2,1)S(1)} %get-tuple-element.38), channel_id=1, source_target_pairs={{0,8},{8,0},{16,24},{24,16},{1,9},{9,1},{17,25},{25,17},{2,10},{10... | collective-permute-start | bytes 1572872 | tf_op jit(solution)/shard_map/ppermute | solution.py:18
  20.7 1.3 %collective-permute-start.3 = (bf16[128,256]{1,0:T(8,128)(2,1)S(1)}, bf16[128,256]{1,0:T(8,128)(2,1)S(1)}, u32[]{:S(2)}, u32[]{:S(2)}) collective-permute-start(bf16[128,256]{1,0:T(8,128)(2,1)S(1)} %get-tuple-element.36), channel_id=1, source_target_pairs={{0,8},{8,0},{16,24},{24,16},{1,9},{9,1},{17,25},{25,17},{2,10},{10... | collective-permute-start | bytes 196616 | tf_op jit(solution)/shard_map/ppermute | solution.py:18
  20.9 6.1 %copy-start.3 = (bf16[256,256]{1,0:T(8,128)(2,1)S(1)}, bf16[256,256]{1,0:T(8,128)(2,1)}, u32[]{:S(2)}) copy-start(bf16[256,256]{1,0:T(8,128)(2,1)} %weight.3) | copy-start | bytes 393220
  22.1 5.0 %copy-start.5 = (s32[1,1,8,32]{3,2,1,0:T(8,128)S(1)}, s32[1,1,8,32]{3,2,1,0:T(8,128)}, u32[]{:S(2)}) copy-start(s32[1,1,8,32]{3,2,1,0:T(8,128)} %param.17) | copy-start | bytes 3076
  22.1 5.0 %copy-start.6 = (f32[1,1,8,32]{3,2,1,0:T(8,128)S(1)}, f32[1,1,8,32]{3,2,1,0:T(8,128)}, u32[]{:S(2)}) copy-start(f32[1,1,8,32]{3,2,1,0:T(8,128)} %param.18) | copy-start | bytes 3076
  22.1 6.2 %collective-permute-start.5 = (bf16[128,256]{1,0:T(8,128)(2,1)S(1)}, bf16[128,256]{1,0:T(8,128)(2,1)S(1)}, u32[]{:S(2)}, u32[]{:S(2)}) collective-permute-start(bf16[128,256]{1,0:T(8,128)(2,1)S(1)} %add_convert_fusion.2), channel_id=1, source_target_pairs={{0,6},{1,7},{2,4},{3,5},{4,2},{5,3},{6,0},{7,1},{8,25},{9,24},{10,... | collective-permute-start | bytes 196616 | tf_op jit(solution)/shard_map/ppermute | solution.py:29
  23.8 5.7 %collective-permute-start.6 = (bf16[128,256]{1,0:T(8,128)(2,1)S(1)}, bf16[128,256]{1,0:T(8,128)(2,1)S(1)}, u32[]{:S(2)}, u32[]{:S(2)}) collective-permute-start(bf16[128,256]{1,0:T(8,128)(2,1)S(1)} %add_convert_fusion.2), channel_id=1, source_target_pairs={{0,2},{1,3},{2,0},{3,1},{4,6},{5,7},{6,4},{7,5},{8,9},{9,8},{10,11... | collective-permute-start | bytes 196616 | tf_op jit(solution)/shard_map/ppermute | solution.py:29
  23.8 5.7 %collective-permute-start.7 = (bf16[128,256]{1,0:T(8,128)(2,1)S(1)}, bf16[128,256]{1,0:T(8,128)(2,1)S(1)}, u32[]{:S(2)}, u32[]{:S(2)}) collective-permute-start(bf16[128,256]{1,0:T(8,128)(2,1)S(1)} %add_convert_fusion.2), channel_id=1, source_target_pairs={{0,4},{1,5},{2,6},{3,7},{4,0},{5,1},{6,2},{7,3},{8,24},{9,25},{10,... | collective-permute-start | bytes 196616 | tf_op jit(solution)/shard_map/ppermute | solution.py:29
  26.5 6.6 %collective-permute-start.11 = (bf16[256,512]{1,0:T(8,128)(2,1)S(1)}, bf16[256,512]{1,0:T(8,128)(2,1)S(1)}, u32[]{:S(2)}, u32[]{:S(2)}) collective-permute-start(bf16[256,512]{1,0:T(8,128)(2,1)S(1)} %fusion), channel_id=1, source_target_pairs={{0,16},{8,24},{16,0},{24,8},{1,17},{9,25},{17,1},{25,9},{2,18},{10... | collective-permute-start | bytes 786440 | tf_op jit(solution)/shard_map/ppermute | solution.py:18
  29.4 3.7 %copy-start.4 = (s32[1,1,8,32]{3,2,1,0:T(8,128)S(1)}, s32[1,1,8,32]{3,2,1,0:T(8,128)}, u32[]{:S(2)}) copy-start(s32[1,1,8,32]{3,2,1,0:T(8,128)} %param.15) | copy-start | bytes 3076
  29.5 3.7 %copy-start.7 = (s32[1,1,8]{2,1,0:T(1,128)S(1)}, s32[1,1,8]{2,1,0:T(1,128)}, u32[]{:S(2)}) copy-start(s32[1,1,8]{2,1,0:T(1,128)} %param.16) | copy-start | bytes 100
  29.5 5.4 %collective-permute-start.10 = (bf16[128,256]{1,0:T(8,128)(2,1)S(1)}, bf16[128,256]{1,0:T(8,128)(2,1)S(1)}, u32[]{:S(2)}, u32[]{:S(2)}) collective-permute-start(bf16[128,256]{1,0:T(8,128)(2,1)S(1)} %add_convert_fusion.1), channel_id=1, source_target_pairs={{0,17},{1,16},{2,19},{3,18},{4,21},{5,20},{6,23},{7,22},{8,14},{9,... | collective-permute-start | bytes 196616 | tf_op jit(solution)/shard_map/ppermute | solution.py:29
  31.0 4.3 %collective-permute-start.8 = (bf16[128,256]{1,0:T(8,128)(2,1)S(1)}, bf16[128,256]{1,0:T(8,128)(2,1)S(1)}, u32[]{:S(2)}, u32[]{:S(2)}) collective-permute-start(bf16[128,256]{1,0:T(8,128)(2,1)S(1)} %add_convert_fusion.1), channel_id=1, source_target_pairs={{0,1},{1,0},{2,3},{3,2},{4,5},{5,4},{6,7},{7,6},{8,10},{9,11},{10,... | collective-permute-start | bytes 196616 | tf_op jit(solution)/shard_map/ppermute | solution.py:29
  31.5 4.3 %collective-permute-start.9 = (bf16[128,256]{1,0:T(8,128)(2,1)S(1)}, bf16[128,256]{1,0:T(8,128)(2,1)S(1)}, u32[]{:S(2)}, u32[]{:S(2)}) collective-permute-start(bf16[128,256]{1,0:T(8,128)(2,1)S(1)} %add_convert_fusion.1), channel_id=1, source_target_pairs={{0,16},{1,17},{2,18},{3,19},{4,20},{5,21},{6,22},{7,23},{8,12},{9,... | collective-permute-start | bytes 196616 | tf_op jit(solution)/shard_map/ppermute | solution.py:29
  35.8 1.3 %collective-permute-start.12 = (bf16[128,256]{1,0:T(8,128)(2,1)S(1)}, bf16[128,256]{1,0:T(8,128)(2,1)S(1)}, u32[]{:S(2)}, u32[]{:S(2)}) collective-permute-start(bf16[128,256]{1,0:T(8,128)(2,1)S(1)} %add_convert_fusion), channel_id=1, source_target_pairs={{0,8},{8,0},{16,24},{24,16},{1,9},{9,1},{17,25},{25,17},{2,10},{10... | collective-permute-start | bytes 196616 | tf_op jit(solution)/shard_map/ppermute | solution.py:18
